TPU v7x, 32 devices: a whole 2x2x4 slice. The times are simulated.
32 devices in a mesh: dp: 16 (over z, y, x), tensor: 2 (over core).
Axes of the slice: x: 2, y: 2, z: 4, core: 2. Of those that a mesh axis runs over, the one named last changes fastest.
Arguments:
- tokens: bfloat16 [32, 192, 2048], P('dp'), may hold values from -6 to 6
- cotangent: bfloat16 [32, 192, 2048], P('dp'), may hold values from -6 to 6
- lengths: int32 [32], replicated, may hold values from 1 to 192, 3840 in all
- permutation: int32 [32], replicated, may hold values from 0 to 31, each once
- w_qkv: float32 [2048, 6144], P('dp', 'tensor'), may hold values from -0.125 to 0.125
- w_dense: float32 [2048, 2048], P('dp', 'tensor'), may hold values from -0.375 to 0.375
- w_fc1: float32 [2048, 8192], P('dp', 'tensor'), may hold values from -0.125 to 0.125
- w_fc2: float32 [2048, 8192], P('dp', 'tensor'), may hold values from -0.0625 to 0.0625
- norm_vectors: float32 [6, 2048], replicated, may hold values from -1 to 4
- split_biases: float32 [2, 7168], P('tensor'), may hold values from -0.8 to 0.8
- row_state: float32 [4, 2048], P(None, 'dp'), may hold values from 384 to 12288
- col_state: float32 [2, 12288], P('tensor'), may hold values from 384 to 12288
- norm_moment: float32 [6, 2048], replicated, may hold values from 768 to 12288
- bias_moment: float32 [2, 7168], P('tensor'), may hold values from 384 to 6144
Outputs:
- mixed: bfloat16 [32, 192, 2048], P('dp')
- grad_tokens: bfloat16 [32, 192, 2048], P('dp')
- grad_qkv: float32 [2048, 6144], P('dp', 'tensor')
- grad_dense: float32 [2048, 2048], P('dp', 'tensor')
- grad_fc1: float32 [2048, 8192], P('dp', 'tensor')
- grad_fc2: float32 [2048, 8192], P('dp', 'tensor')
- new_qkv: float32 [2048, 6144], P('dp', 'tensor')
- new_dense: float32 [2048, 2048], P('dp', 'tensor')
- new_fc1: float32 [2048, 8192], P('dp', 'tensor')
- new_fc2: float32 [2048, 8192], P('dp', 'tensor')
- copy_qkv: bfloat16 [2048, 6144], P('dp', 'tensor')
- copy_dense: bfloat16 [2048, 2048], P('dp', 'tensor')
- copy_fc1: bfloat16 [2048, 8192], P('dp', 'tensor')
- copy_fc2: bfloat16 [2048, 8192], P('dp', 'tensor')
- row_state_new: float32 [4, 2048], P(None, 'dp')
- col_state_new: float32 [2, 12288], P('tensor')
- norm_grad: float32 [6, 2048], replicated
- norm_moment_new: float32 [6, 2048], replicated
- norm_new: float32 [6, 2048], replicated
- bias_grad: float32 [2, 7168], P('tensor')
- bias_moment_new: float32 [2, 7168], P('tensor')
- bias_new: float32 [2, 7168], P('tensor')
Inputs may be any that keep to these rules, and one draw needn't show every extreme that they name: `permutation`: each sequence once.
All inputs are finite; a program needn't handle non-finite values.
Results may differ from a plain program's by a relative error of at most 0.03.
Values may be sent and summed in bfloat16 or wider, within the bound.
A program may use at most 512 MiB of HBM per device.

v0:
```python
from functools import partial
import math

import jax
import jax.numpy as jnp
from jax import lax
from jax.sharding import PartitionSpec as P

D = 2048
FF = 8192
HEADS = 8


eps_norm = 1e-05
eps_second = 1e-30
decay = 0.5
rate_scale = 1.0
rate_norm = 0.5
rate_vector = 0.05
neg_large = -1e30


def layer_norm(values, gain, shift):
    centre = values - jnp.mean(values, -1, keepdims=True)
    spread = jnp.mean(centre * centre, -1, keepdims=True)
    return centre * lax.rsqrt(spread + eps_norm) * gain + shift


def rotary_tables(slot_len, rot_dims):
    half = rot_dims // 2
    freq = 10000.0 ** (-2.0 * jnp.arange(half, dtype=jnp.float32) / rot_dims)
    angle = jnp.arange(slot_len, dtype=jnp.float32)[:, None] * freq[None, :]
    return (jnp.cos(angle), jnp.sin(angle))


def rotate(values, cosine, sine, rot_dims):
    half = rot_dims // 2
    first = values[..., :half]
    second = values[..., half:rot_dims]
    cos_b = cosine[:, None, :]
    sin_b = sine[:, None, :]
    return jnp.concatenate(
        [first * cos_b - second * sin_b, second * cos_b + first * sin_b, values[..., rot_dims:]], -1
    )


def unrotate(grads, cosine, sine, rot_dims):
    half = rot_dims // 2
    first = grads[..., :half]
    second = grads[..., half:rot_dims]
    cos_b = cosine[:, None, :]
    sin_b = sine[:, None, :]
    return jnp.concatenate(
        [first * cos_b + second * sin_b, second * cos_b - first * sin_b, grads[..., rot_dims:]], -1
    )


def contract_last(left, right):
    return lax.dot_general(
        left, right, (((1,), (1,)), ((), ())), preferred_element_type=jnp.float32
    )


def contract_first(left, right):
    return lax.dot_general(
        left, right, (((0,), (0,)), ((), ())), preferred_element_type=jnp.float32
    )


def masked_scores(query, keys, causal, root):
    raw = jnp.einsum("sqhd,skhd->shqk", query, keys, preferred_element_type=jnp.float32) / root
    return jnp.where(causal, raw, neg_large)


def route(stacked, order):
    count, seq_dev, slot_len, width = stacked.shape
    n_data = lax.axis_size("dp")
    piece = slot_len // n_data
    pieces = stacked.reshape(count, seq_dev, n_data, piece, width)
    spread = lax.all_to_all(pieces, "dp", split_axis=2, concat_axis=1, tiled=True)
    ordered = jnp.take(spread, order, axis=1)
    settled = lax.all_to_all(ordered, "dp", split_axis=1, concat_axis=2, tiled=True)
    return settled.reshape(count, seq_dev, slot_len, width)


def per_device(
    tokens,
    cotangent,
    lengths,
    permutation,
    w_qkv,
    w_dense,
    w_fc1,
    w_fc2,
    norm_vectors,
    split_biases,
    row_state,
    col_state,
    norm_moment,
    bias_moment,
):
    n_split = lax.axis_size("tensor")
    data_place = lax.axis_index("dp")
    seq_dev, slot_len, width = tokens.shape
    rows_all = seq_dev * slot_len
    local_heads = HEADS // n_split
    head_dim = D // HEADS
    rot_dims = head_dim // 4
    root = math.sqrt(head_dim)
    qkv_cols = w_qkv.shape[1]
    dense_cols = w_dense.shape[1]
    hidden_cols = w_fc1.shape[1]
    edges = (
        0,
        qkv_cols,
        qkv_cols + dense_cols,
        qkv_cols + dense_cols + hidden_cols,
        qkv_cols + dense_cols + 2 * hidden_cols,
    )
    full_cols = (3.0 * D, 1.0 * D, 1.0 * FF, 1.0 * FF)
    rates = (
        rate_scale / math.sqrt(D),
        rate_scale / math.sqrt(D // 8),
        rate_scale / math.sqrt(D),
        rate_scale / math.sqrt(FF),
    )
    dealt = route(jnp.stack([tokens, cotangent]), permutation)
    inputs = dealt[0].reshape(rows_all, width).astype(jnp.float32)
    mine = lax.dynamic_slice_in_dim(permutation, data_place * seq_dev, seq_dev)
    my_lengths = jnp.take(lengths, mine)
    places = jnp.arange(slot_len, dtype=jnp.int32)
    valid = (places[None, :] < my_lengths[:, None]).astype(jnp.float32).reshape(rows_all, 1)
    back_low = jnp.where(
        valid > 0.5, dealt[1].reshape(rows_all, width), jnp.zeros((rows_all, width), jnp.bfloat16)
    )
    back_rows = back_low.astype(jnp.float32)
    gain_one, shift_one, gain_two, shift_two, bias_dense, bias_out = (
        norm_vectors[index] for index in range(6)
    )
    norm_one_low = layer_norm(inputs, gain_one, shift_one).astype(jnp.bfloat16)
    norm_two_low = layer_norm(inputs, gain_two, shift_two).astype(jnp.bfloat16)
    in_local = jnp.concatenate([w_qkv, w_fc1], 1).astype(jnp.bfloat16)
    out_local = jnp.concatenate([w_dense, w_fc2], 1).astype(jnp.bfloat16)
    part = lax.all_gather(in_local, "dp", axis=0, tiled=True)
    left_one = norm_one_low
    left_two = norm_two_low
    qkv_sum = jnp.dot(left_one, part[:, :qkv_cols], preferred_element_type=jnp.float32)
    pre_sum = jnp.dot(left_two, part[:, qkv_cols:], preferred_element_type=jnp.float32)
    qkv_full = (qkv_sum + split_biases[0, :qkv_cols]).reshape(
        seq_dev, slot_len, local_heads, 3, head_dim
    )
    cosine, sine = rotary_tables(slot_len, rot_dims)
    query = rotate(qkv_full[:, :, :, 0], cosine, sine, rot_dims).astype(jnp.bfloat16)
    keys = rotate(qkv_full[:, :, :, 1], cosine, sine, rot_dims).astype(jnp.bfloat16)
    values = qkv_full[:, :, :, 2].astype(jnp.bfloat16)
    causal = places[:, None] >= places[None, :]
    scores = masked_scores(query, keys, causal, root)
    peak = jnp.max(scores, -1, keepdims=True)
    expo = jnp.exp(scores - peak)
    total = jnp.sum(expo, -1, keepdims=True)
    probs_low = (expo / total).astype(jnp.bfloat16)
    attn_low = (
        jnp.einsum("shqk,skhd->sqhd", probs_low, values, preferred_element_type=jnp.float32)
        .astype(jnp.bfloat16)
        .reshape(rows_all, dense_cols)
    )
    pre_act = pre_sum + split_biases[0, qkv_cols:]
    hidden_low = jax.nn.gelu(pre_act, approximate=False).astype(jnp.bfloat16)
    part = lax.all_gather(out_local, "dp", axis=0, tiled=True)
    partial_sum = contract_last(attn_low, part[:, :dense_cols]) + contract_last(
        hidden_low, part[:, dense_cols:]
    )
    branch = lax.psum(partial_sum.astype(jnp.bfloat16), "tensor").astype(jnp.float32)
    mixed = (
        (valid * (inputs + branch + bias_dense + bias_out))
        .astype(jnp.bfloat16)
        .reshape(seq_dev, slot_len, width)
    )
    part = lax.all_gather(out_local, "dp", axis=0, tiled=True)
    attn_grad = jnp.dot(back_low, part[:, :dense_cols], preferred_element_type=jnp.float32)
    hidden_grad = jnp.dot(back_low, part[:, dense_cols:], preferred_element_type=jnp.float32)
    _, gelu_pull = jax.vjp(partial(jax.nn.gelu, approximate=False), pre_act)
    pre_grad_low = gelu_pull(hidden_grad)[0].astype(jnp.bfloat16)
    attn_grad_low = attn_grad.astype(jnp.bfloat16).reshape(seq_dev, slot_len, local_heads, head_dim)
    probs = jnp.exp(masked_scores(query, keys, causal, root) - peak) / total
    prob_grad = jnp.einsum(
        "sqhd,skhd->shqk", attn_grad_low, values, preferred_element_type=jnp.float32
    )
    row_dot = jnp.sum(probs * prob_grad, -1, keepdims=True)
    score_grad = (probs * (prob_grad - row_dot)).astype(jnp.bfloat16)
    value_grad = jnp.einsum(
        "shqk,sqhd->skhd",
        probs.astype(jnp.bfloat16),
        attn_grad_low,
        preferred_element_type=jnp.float32,
    )
    query_grad = (
        jnp.einsum("shqk,skhd->sqhd", score_grad, keys, preferred_element_type=jnp.float32) / root
    )
    key_grad = (
        jnp.einsum("shqk,sqhd->skhd", score_grad, query, preferred_element_type=jnp.float32) / root
    )
    qkv_grad_low = (
        jnp.stack(
            [
                unrotate(query_grad, cosine, sine, rot_dims),
                unrotate(key_grad, cosine, sine, rot_dims),
                value_grad,
            ],
            3,
        )
        .reshape(rows_all, qkv_cols)
        .astype(jnp.bfloat16)
    )
    part = lax.all_gather(in_local, "dp", axis=0, tiled=True)
    norm_grad_parts = jnp.stack(
        [
            contract_last(qkv_grad_low, part[:, :qkv_cols]),
            contract_last(pre_grad_low, part[:, qkv_cols:]),
        ]
    )
    norm_grads = lax.psum(norm_grad_parts.astype(jnp.bfloat16), "tensor").astype(jnp.float32)
    _, pull_one = jax.vjp(layer_norm, inputs, gain_one, shift_one)
    input_one, gain_one_grad, shift_one_grad = pull_one(norm_grads[0])
    _, pull_two = jax.vjp(layer_norm, inputs, gain_two, shift_two)
    input_two, gain_two_grad, shift_two_grad = pull_two(norm_grads[1])
    input_grad = back_rows + input_one + input_two
    inverse = (
        jnp.zeros_like(permutation)
        .at[permutation]
        .set(jnp.arange(permutation.shape[0], dtype=jnp.int32))
    )
    grad_tokens = route(
        input_grad.astype(jnp.bfloat16).reshape(1, seq_dev, slot_len, width), inverse
    )[0]
    out_bias_grad = jnp.sum(back_rows, 0)
    norm_part = jnp.stack(
        [gain_one_grad, shift_one_grad, gain_two_grad, shift_two_grad, out_bias_grad, out_bias_grad]
    )
    bias_part = jnp.concatenate(
        [jnp.sum(qkv_grad_low, 0, dtype=jnp.float32), jnp.sum(pre_grad_low, 0, dtype=jnp.float32)]
    )[None, :]
    left_one = norm_one_low
    left_two = norm_two_low
    inward = jnp.concatenate(
        [contract_first(left_one, qkv_grad_low), contract_first(left_two, pre_grad_low)], 1
    )
    outward = jnp.concatenate(
        [contract_first(back_low, attn_low), contract_first(back_low, hidden_low)], 1
    )
    grads_local = lax.psum_scatter(
        jnp.concatenate(
            [
                inward[:, :qkv_cols],
                outward[:, :dense_cols],
                inward[:, qkv_cols:],
                outward[:, dense_cols:],
            ],
            1,
        ),
        "dp",
        scatter_dimension=0,
        tiled=True,
    )
    squares = grads_local * grads_local + eps_second
    row_part = jnp.stack(
        [jnp.sum(squares[:, edges[index] : edges[index + 1]], 1) for index in range(4)]
    )
    col_part = jnp.sum(squares, 0)
    counts = jnp.array(full_cols, jnp.float32)[:, None]
    row_total = lax.psum(row_part, "tensor")
    row_new = decay * row_state + (1.0 - decay) * (row_total / counts)
    col_total, row_mass, norm_total, bias_total = lax.psum(
        (col_part, jnp.sum(row_new, 1), norm_part, bias_part), "dp"
    )
    row_mean = row_mass / D
    col_new = decay * col_state + (1.0 - decay) * (col_total[None, :] / D)
    weights = (w_qkv, w_dense, w_fc1, w_fc2)
    grads_list = []
    new_list = []
    for index in range(4):
        grad = grads_local[:, edges[index] : edges[index + 1]]
        second = (
            row_new[index][:, None]
            * col_new[0, edges[index] : edges[index + 1]][None, :]
            / row_mean[index]
        )
        grads_list.append(grad)
        new_list.append(weights[index] - rates[index] * grad * lax.rsqrt(second))
    norm_moment_new = decay * norm_moment + (1.0 - decay) * (norm_total * norm_total + eps_second)
    norm_new = norm_vectors - rate_norm * norm_total * lax.rsqrt(norm_moment_new)
    bias_moment_new = decay * bias_moment + (1.0 - decay) * (bias_total * bias_total + eps_second)
    bias_new = split_biases - rate_vector * bias_total * lax.rsqrt(bias_moment_new)
    return (
        mixed,
        grad_tokens,
        grads_list[0],
        grads_list[1],
        grads_list[2],
        grads_list[3],
        new_list[0],
        new_list[1],
        new_list[2],
        new_list[3],
        new_list[0].astype(jnp.bfloat16),
        new_list[1].astype(jnp.bfloat16),
        new_list[2].astype(jnp.bfloat16),
        new_list[3].astype(jnp.bfloat16),
        row_new,
        col_new,
        norm_total,
        norm_moment_new,
        norm_new,
        bias_total,
        bias_moment_new,
        bias_new,
    )


def solution(mesh):
    in_specs = (
        P("dp", None, None),
        P("dp", None, None),
        P(),
        P(),
        P("dp", "tensor"),
        P("dp", "tensor"),
        P("dp", "tensor"),
        P("dp", "tensor"),
        P(),
        P("tensor", None),
        P(None, "dp"),
        P("tensor", None),
        P(),
        P("tensor", None),
    )
    out_specs = (
        P("dp", None, None),
        P("dp", None, None),
        P("dp", "tensor"),
        P("dp", "tensor"),
        P("dp", "tensor"),
        P("dp", "tensor"),
        P("dp", "tensor"),
        P("dp", "tensor"),
        P("dp", "tensor"),
        P("dp", "tensor"),
        P("dp", "tensor"),
        P("dp", "tensor"),
        P("dp", "tensor"),
        P("dp", "tensor"),
        P(None, "dp"),
        P("tensor", None),
        P(),
        P(),
        P(),
        P("tensor", None),
        P("tensor", None),
        P("tensor", None),
    )
    return jax.shard_map(
        per_device, mesh=mesh, in_specs=in_specs, out_specs=out_specs, check_vma=False
    )
```

profile of v0, /device:TPU:0, one launch (start us, length us, event | category | flops | bytes accessed | tf_op | source)
XLA Modules:
  0.0 3750.2 jit_solution(2155600276462976554)
XLA Ops:
  27.0 8.6 all-to-all-start
  36.2 105.1 %all-to-all-done = bf16[2,2,16,12,2048]{4,1,3,0,2:T(2,128)(2,1)S(1)} async-done(((bf16[2,2,16,12,2048]{4,1,3,0,2:T(2,128)(2,1)}), bf16[2,2,16,12,2048]{4,1,3,0,2:T(2,128)(2,1)S(1)}, u32[]{:S(2)}, u32[]{:S(2)}) %all-to-all-start) | async-done | bytes 3145760 | tf_op jit(solution)/shard_map/all_to_all | solution.py:80
  146.3 9.5 gather_fusion.1
  160.3 38.7 %all-to-all-start.1 = ((bf16[2,32,1,12,2048]{4,0,3,2,1:T(2,128)(2,1)}), bf16[2,32,1,12,2048]{4,0,3,2,1:T(2,128)(2,1)S(1)}, u32[]{:S(2)}, u32[]{:S(2)}) async-start(bf16[2,32,1,12,2048]{4,0,3,2,1:T(2,128)(2,1)} %fusion.49), calls=%async_computation.1 | async-start | bytes 6291456 | tf_op jit(solution)/shard_map/all_to_all | solution.py:82
  203.3 103.9 %all-to-all-done.1 = bf16[2,32,1,12,2048]{4,0,3,2,1:T(2,128)(2,1)S(1)} async-done(((bf16[2,32,1,12,2048]{4,0,3,2,1:T(2,128)(2,1)}), bf16[2,32,1,12,2048]{4,0,3,2,1:T(2,128)(2,1)S(1)}, u32[]{:S(2)}, u32[]{:S(2)}) %all-to-all-start.1) | async-done | bytes 3145760 | tf_op jit(solution)/shard_map/all_to_all | solution.py:82
  329.4 42.1 %all-gather.5.cloned.1.call-done = bf16[2048,5120]{1,0:T(8,128)(2,1)} async-done(((bf16[128,5120]{1,0:T(8,128)(2,1)}), bf16[2048,5120]{1,0:T(8,128)(2,1)}) %all-gather.5.cloned.1.call-update) | async-done | bytes 20971536 | tf_op jit(solution)/shard_map/all_gather | solution.py:169
  379.6 305.6 %all-gather.3.cloned.1.call-done = bf16[2048,7168]{1,0:T(8,128)(2,1)} async-done(((bf16[128,7168]{1,0:T(8,128)(2,1)}), bf16[2048,7168]{1,0:T(8,128)(2,1)}) %all-gather.3.cloned.1.call-update) | async-done | bytes 29360144 | tf_op jit(solution)/shard_map/all_gather | solution.py:144
  685.2 9.8 fusion.25
  695.0 8.9 reshape.527
  709.4 7.8 fusion.105
  744.0 7.1 convert_element_type.172
  751.1 8.8 fusion.61
  759.9 25.1 multiply_convert_fusion
  785.0 14.6 convert_reduce_fusion
  799.6 11.4 fusion.58
  814.1 11.0 fusion.3
  831.0 19.1 fusion.91
  850.1 15.7 fusion.93
  874.9 6.9 squeeze.39
  881.8 8.8 convert_reduce_fusion.2
  903.7 7.5 fusion.113
  911.1 11.8 fusion.112
  922.9 65.1 %pad_maximum_fusion = f32[2048,12288]{1,0:T(8,128)} fusion(f32[2048,4096]{1,0:T(8,128)} %fusion.91, f32[2048,4096]{1,0:T(8,128)} %fusion.93, f32[2048,1024]{1,0:T(8,128)} %fusion.113, f32[2048,3072]{1,0:T(8,128)} %fusion.112), kind=kLoop, calls=%fused_computation.5 | loop fusion | flops 75497472 | bytes 201326592 | tf_op jit(solution)/shard_map/concatenate | solution.py:252
  994.0 6.5 squeeze.35
  1007.5 7.4 fusion.40
  1015.2 7.8 fusion.35
  1031.0 56.7 %all-to-all-done.2 = bf16[1,2,16,12,2048]{4,1,3,0,2:T(2,128)(2,1)S(1)} async-done(((bf16[1,2,16,12,2048]{4,1,3,0,2:T(2,128)(2,1)}), bf16[1,2,16,12,2048]{4,1,3,0,2:T(2,128)(2,1)S(1)}, u32[]{:S(2)}, u32[]{:S(2)}) %all-to-all-start.2) | async-done | bytes 1572896 | tf_op jit(solution)/shard_map/all_to_all | solution.py:80
  1096.1 23.5 all-to-all-start.3
  1125.7 66.1 %all-to-all-done.3 = bf16[1,32,1,12,2048]{4,3,2,0,1:T(8,128)(2,1)S(1)} async-done(((bf16[1,32,1,12,2048]{4,3,2,0,1:T(8,128)(2,1)}), bf16[1,32,1,12,2048]{4,3,2,0,1:T(8,128)(2,1)S(1)}, u32[]{:S(2)}, u32[]{:S(2)}) %all-to-all-start.3) | async-done | bytes 1572896 | tf_op jit(solution)/shard_map/all_to_all | solution.py:82
  1196.6 2408.7 %all-reduce.7.cloned.1.call-done = f32[2048,12288]{1,0:T(8,128)} async-done(((f32[2048,12288]{1,0:T(8,128)}), f32[2048,12288]{1,0:T(8,128)}) %all-reduce.7.cloned.1.call-update) | async-done | bytes 100663312
  3613.6 106.4 %all-reduce.9.cloned.1.call-done = (f32[4]{0:T(128)}, f32[12288]{0:T(1024)}, f32[6,2048]{1,0:T(8,128)}, f32[1,7168]{1,0:T(1,128)}) async-done(((f32[4]{0:T(128)}, f32[12288]{0:T(1024)}, f32[6,2048]{1,0:T(8,128)}, f32[1,7168]{1,0:T(1,128)}), (f32[4]{0:T(128)}, f32[12288]{0:T(1024)}, f32[6,2048]{1,0:T(8,128)}, f32[1,7168]{1,0:T(1,128)})) %all-reduce.9.cloned.1.call-update) | async-done | bytes 127008 | tf_op jit(solution)/shard_map/psum | solution.py:273
  3733.0 9.2 fusion.94
  (291 shorter events, 189.5 us)
Async XLA Ops:
  7.2 192.2 %copy-start = (s32[32]{0:T(128)S(1)}, s32[32]{0:T(128)}, u32[]{:S(2)}) copy-start(s32[32]{0:T(128)} %param.17) | copy-start | bytes 388
  7.2 364.3 %all-gather.5.cloned.1.call-start = ((), (), s32[]{:S(2)}) async-start(), calls=%async_computation.5 | async-start | bytes 22282240 | tf_op jit(solution)/shard_map/all_gather | solution.py:169
  11.3 673.9 %all-gather.3.cloned.1.call-start = ((), (), s32[]{:S(2)}) async-start(), calls=%async_computation.4 | async-start | bytes 31195136 | tf_op jit(solution)/shard_map/all_gather | solution.py:144
  27.0 114.3 %all-to-all-start = ((bf16[2,2,16,12,2048]{4,1,3,0,2:T(2,128)(2,1)}), bf16[2,2,16,12,2048]{4,1,3,0,2:T(2,128)(2,1)S(1)}, u32[]{:S(2)}, u32[]{:S(2)}) async-start(bf16[2,2,16,12,2048]{4,1,3,0,2:T(2,128)(2,1)} %copy.241), calls=%async_computation | async-start | bytes 6291456 | tf_op jit(solution)/shard_map/all_to_all | solution.py:80
  160.3 42.3 %copy-start.38 = (f32[6,2048]{1,0:T(8,128)S(1)}, f32[6,2048]{1,0:T(8,128)}, u32[]{:S(2)}) copy-start(f32[6,2048]{1,0:T(8,128)} %param.23) | copy-start | bytes 147460
  160.3 146.9 %all-to-all-start.1 = ((bf16[2,32,1,12,2048]{4,0,3,2,1:T(2,128)(2,1)}), bf16[2,32,1,12,2048]{4,0,3,2,1:T(2,128)(2,1)S(1)}, u32[]{:S(2)}, u32[]{:S(2)}) async-start(bf16[2,32,1,12,2048]{4,0,3,2,1:T(2,128)(2,1)} %fusion.49), calls=%async_computation.1 | async-start | bytes 6291456 | tf_op jit(solution)/shard_map/all_to_all | solution.py:82
  199.1 666.7 %all-reduce.11.cloned.1.call-start = ((), (), s32[]{:S(2)}) async-start(), calls=%async_computation.8 | async-start | bytes 9437184 | tf_op jit(solution)/shard_map/psum | solution.py:173
  200.9 111.6 %copy-start.59 = (f32[384]{0:T(512)}, f32[384]{0:T(512)S(1)}, u32[]{:S(2)}) copy-start(f32[384]{0:T(512)S(1)} %reshape.535) | copy-start | bytes 4612
  201.6 170.0 %copy-start.62 = (pred[384]{0:T(512)(128)(4,1)}, pred[384]{0:T(512)(128)(4,1)S(1)}, u32[]{:S(2)}) copy-start(pred[384]{0:T(512)(128)(4,1)S(1)} %broadcast_compare_fusion) | copy-start | bytes 1156
  203.3 481.9 %copy-start.42 = (f32[1,2048]{1,0:T(1,128)}, f32[1,2048]{1,0:T(1,128)S(1)}, u32[]{:S(2)}) copy-start(f32[1,2048]{1,0:T(1,128)S(1)} %get-tuple-element.228) | copy-start | bytes 24580
  203.3 481.9 %copy-start.54 = (f32[1,2048]{1,0:T(1,128)}, f32[1,2048]{1,0:T(1,128)S(1)}, u32[]{:S(2)}) copy-start(f32[1,2048]{1,0:T(1,128)S(1)} %get-tuple-element.227) | copy-start | bytes 24580
  329.4 520.7 %copy-start.4 = (f32[384,2048]{1,0:T(8,128)}, f32[384,2048]{1,0:T(8,128)S(1)}, u32[]{:S(2)}) copy-start(f32[384,2048]{1,0:T(8,128)S(1)} %reshape.536) | copy-start | bytes 9437188
  329.4 355.8 %slice-start = ((f32[1,7168]{1,0:T(1,128)}), f32[1,3072]{1,0:T(1,128)S(1)}, s32[]{:S(2)}) async-start(f32[1,7168]{1,0:T(1,128)} %param.24), calls=%async_computation.9 | async-start | bytes 24576 | tf_op jit(solution)/shard_map/slice | solution.py:149
  759.9 25.1 copy-start.12
  759.9 25.1 copy-start.63
  799.6 11.4 copy-start.16
  814.1 11.0 copy-start.19
  830.3 2775.0 %all-reduce.7.cloned.1.call-start = ((), (), s32[]{:S(2)}) async-start(), calls=%async_computation.6 | async-start | bytes 201326592
  831.0 19.1 copy-start.17
  1025.8 61.9 %all-to-all-start.2 = ((bf16[1,2,16,12,2048]{4,1,3,0,2:T(2,128)(2,1)}), bf16[1,2,16,12,2048]{4,1,3,0,2:T(2,128)(2,1)S(1)}, u32[]{:S(2)}, u32[]{:S(2)}) async-start(bf16[1,2,16,12,2048]{4,1,3,0,2:T(2,128)(2,1)} %copy.279), calls=%async_computation.2 | async-start | bytes 3145728 | tf_op jit(solution)/shard_map/all_to_all | solution.py:80
  1096.1 23.8 copy-start.72
  1096.1 25.0 copy-start.51
  1096.1 25.0 copy-start.61
  1096.1 95.7 %all-to-all-start.3 = ((bf16[1,32,1,12,2048]{4,3,2,0,1:T(8,128)(2,1)}), bf16[1,32,1,12,2048]{4,3,2,0,1:T(8,128)(2,1)S(1)}, u32[]{:S(2)}, u32[]{:S(2)}) async-start(bf16[1,32,1,12,2048]{4,3,2,0,1:T(8,128)(2,1)} %fusion.64), calls=%async_computation.3 | async-start | bytes 4194304 | tf_op jit(solution)/shard_map/all_to_all | solution.py:82
  1119.6 2600.4 %all-reduce.9.cloned.1.call-start = ((), (), s32[]{:S(2)}) async-start(), calls=%async_computation.7 | async-start | bytes 287744 | tf_op jit(solution)/shard_map/psum | solution.py:273
  3609.7 111.0 %copy-start.50 = (f32[1,12288]{1,0:T(1,128)S(1)}, f32[1,12288]{1,0:T(1,128)}, u32[]{:S(2)}) copy-start(f32[1,12288]{1,0:T(1,128)} %param.26) | copy-start | bytes 147460
  3609.7 112.3 %copy-start.45 = (f32[1,7168]{1,0:T(1,128)S(1)}, f32[1,7168]{1,0:T(1,128)}, u32[]{:S(2)}) copy-start(f32[1,7168]{1,0:T(1,128)} %param.24) | copy-start | bytes 86020
  3609.8 112.3 %copy-start.56 = (f32[1,7168]{1,0:T(1,128)S(1)}, f32[1,7168]{1,0:T(1,128)}, u32[]{:S(2)}) copy-start(f32[1,7168]{1,0:T(1,128)} %param.28) | copy-start | bytes 86020
  3609.8 113.7 %copy-start.39 = (f32[6,2048]{1,0:T(8,128)S(1)}, f32[6,2048]{1,0:T(8,128)}, u32[]{:S(2)}) copy-start(f32[6,2048]{1,0:T(8,128)} %param.23) | copy-start | bytes 147460
  3609.8 113.7 %copy-start.48 = (f32[6,2048]{1,0:T(8,128)S(1)}, f32[6,2048]{1,0:T(8,128)}, u32[]{:S(2)}) copy-start(f32[6,2048]{1,0:T(8,128)} %param.27) | copy-start | bytes 147460
  3609.8 115.2 %copy-start.15 = (f32[128,3072]{1,0:T(8,128)S(1)}, f32[128,3072]{1,0:T(8,128)}, u32[]{:S(2)}) copy-start(f32[128,3072]{1,0:T(8,128)} %param.19) | copy-start | bytes 4718596
  3613.6 116.4 %copy-start.65 = (f32[4,128]{1,0:T(4,128)}, f32[4,128]{1,0:T(4,128)S(1)}, u32[]{:S(2)}) copy-start(f32[4,128]{1,0:T(4,128)S(1)} %get-tuple-element.269) | copy-start | bytes 6148
  (52 other events, 232.5 us)
Sparse Core Ops, SparseCore 0:
  11.4 360.1 all-gather.4
  374.8 310.2 all-gather.2
  830.4 27.3 all-reduce.10
  988.2 2617.0 all-reduce.6
  3613.7 106.2 all-reduce.8
where the time goes:
time: 3760 us; the launch traced here: 3750 us
  waiting for transfers between devices  3190 us (85%)
  other arithmetic  158 us (4%)
  matrix products  156 us (4%)
  local copies, waits for them, and re-layouts  148 us (4%)
  starting transfers between devices  75.8 us (2%)
    unnamed x6, waiting for transfers between devices  2410 us
    all_gather x1, waiting for transfers between devices, per_device(): part = lax.all_gather(in_local, 'dp', axis=0, tiled=True)  306 us
    all_to_all x2, waiting for transfers between devices, route(): lax.all_to_all(ordered, 'dp', split_axis=1, concat_axis=2, tiled=True)  170 us
    all_to_all x2, waiting for transfers between devices, route(): lax.all_to_all(pieces, 'dp', split_axis=2, concat_axis=1, tiled=True)  162 us
    psum x1, waiting for transfers between devices, per_device(): lax.psum((col_part, jnp.sum(row_new, 1), norm_part, bias_part), 'dp')  106 us
  transfers between devices with their start and end apart: 9, of which 8 were waited for; matrix products, arithmetic and copies ran while one was open for 4% of the time, Pallas kernels for 0%

commit v1 on v0

v1 whole, which is shorter than its diff:
```python
from functools import partial
import math

import jax
import jax.numpy as jnp
from jax import lax
from jax.experimental import pallas as pl
from jax.experimental.pallas import tpu as pltpu
from jax.sharding import PartitionSpec as P

D = 2048
FF = 8192
HEADS = 8
LINE = 4

eps_norm = 1e-05
eps_second = 1e-30
decay = 0.5
rate_scale = 1.0
rate_norm = 0.5
rate_vector = 0.05
neg_large = -1e30

MESH = pl.DeviceIdType.MESH
ANY = pl.BlockSpec(memory_space=pl.ANY)
VMEM = pl.BlockSpec(memory_space=pltpu.VMEM)
SMEM = pl.BlockSpec(memory_space=pltpu.SMEM)


def rotary_tables(slot_len, rot_dims):
    half = rot_dims // 2
    freq = 10000.0 ** (-2.0 * jnp.arange(half, dtype=jnp.float32) / rot_dims)
    angle = jnp.arange(slot_len, dtype=jnp.float32)[:, None] * freq[None, :]
    return (jnp.cos(angle), jnp.sin(angle))


def rotate(values, cosine, sine, rot_dims):
    half = rot_dims // 2
    first = values[..., :half]
    second = values[..., half:rot_dims]
    return jnp.concatenate(
        [first * cosine - second * sine, second * cosine + first * sine, values[..., rot_dims:]], -1
    )


def contract_last(left, right):
    return lax.dot_general(
        left, right, (((1,), (1,)), ((), ())), preferred_element_type=jnp.float32
    )


def contract_first(left, right):
    return lax.dot_general(
        left, right, (((0,), (0,)), ((), ())), preferred_element_type=jnp.float32
    )


class Place:
    def __init__(self, groups):
        self.groups = groups
        data = lax.axis_index("dp")
        self.core = lax.axis_index("tensor")
        self.other = 1 - self.core
        self.line = data // groups
        self.group = data % groups

    def at(self, line, group, core):
        return (line * self.groups + group, core)

    def line_to(self, step):
        return (self.line + step) % LINE

    def line_from(self, step):
        return (self.line + LINE - step) % LINE

    def group_to(self, step):
        g = self.group
        if self.groups == 4:
            if step == 1:
                return g + 1 - 2 * (g % 2)
            if step == 2:
                return (g + 2) % 4
            return 3 - g
        return (g + step) % self.groups

    def group_from(self, step):
        if self.groups == 4:
            return self.group_to(step)
        return (self.group + self.groups - step) % self.groups

    def greet(self):
        barrier = pltpu.get_barrier_semaphore()
        count = 0
        for step in range(1, LINE):
            for core in (self.core, self.other):
                pl.semaphore_signal(
                    barrier, inc=1, device_id=self.at(self.line_to(step), self.group, core), device_id_type=MESH
                )
                count += 1
        for step in range(1, self.groups):
            pl.semaphore_signal(
                barrier, inc=1, device_id=self.at(self.line, self.group_to(step), self.core), device_id_type=MESH
            )
            count += 1
        pl.semaphore_signal(
            barrier, inc=1, device_id=self.at(self.line, self.group, self.other), device_id_type=MESH
        )
        pl.semaphore_wait(barrier, count + 1)


def remote(src, dst, send, recv, device):
    return pltpu.make_async_remote_copy(
        src_ref=src, dst_ref=dst, send_sem=send, recv_sem=recv, device_id=device, device_id_type=MESH
    )


def gather_kernel(groups, cols, *refs):
    count = len(cols)
    w_in = refs[:count]
    acts_in = refs[count : count + 2]
    w_out = refs[count + 2 : 2 * count + 2]
    acts_out = refs[2 * count + 2 : 2 * count + 4]
    (one_s, one_r, two_s, two_r, three_s, three_r, up_s, up_r, down_s, down_r, sib_s, sib_r, here) = refs[
        2 * count + 4 :
    ]
    me = Place(groups)
    c, g, k = me.line, me.group, me.core
    me.greet()
    sibling = me.at(c, g, me.other)
    sends = []
    started = []

    def block(ref, line, width):
        return ref.at[:, pl.ds(pl.multiple_of(line * width, 128), width)]

    def slot(line, group):
        return line * groups + group

    def hop_up(which, hop, start):
        origin = c - (hop - 1)
        copy = remote(
            acts_in[which].at[k] if hop == 1 else acts_out[which].at[origin, k],
            acts_out[which].at[origin, k],
            up_s.at[which, hop - 1],
            up_r.at[which, hop - 1],
            me.at(c + 1, g, k),
        )
        pl.when((c < LINE - 1) & (origin >= 0))(copy.start if start else copy.wait_send)

    def hop_down(which, hop, start):
        origin = c + (hop - 1)
        copy = remote(
            acts_in[which].at[k] if hop == 1 else acts_out[which].at[origin, k],
            acts_out[which].at[origin, k],
            down_s.at[which, hop - 1],
            down_r.at[which, hop - 1],
            me.at(c - 1, g, k),
        )
        pl.when((c > 0) & (origin < LINE))(copy.start if start else copy.wait_send)

    def to_sibling(which, way, hop, start):
        origin = c - hop if way == 0 else c + hop
        copy = remote(
            acts_out[which].at[origin, k],
            acts_out[which].at[origin, k],
            sib_s.at[which, way, hop - 1],
            sib_r.at[which, way, hop - 1],
            sibling,
        )
        ok = (origin >= 0) if way == 0 else (origin < LINE)
        pl.when(ok)(copy.start if start else copy.wait_send)

    def arrive(which, way, hop):
        origin = c - hop if way == 0 else c + hop
        sem = (up_r if way == 0 else down_r).at[which, hop - 1]
        dst = acts_out[which].at[origin, k]
        ok = (origin >= 0) if way == 0 else (origin < LINE)
        pl.when(ok)(remote(dst, dst, sem, sem, sibling).wait_recv)

    def arrive_sibling(which, way, hop):
        origin = c - hop if way == 0 else c + hop
        sem = sib_r.at[which, way, hop - 1]
        dst = acts_out[which].at[origin, me.other]
        ok = (origin >= 0) if way == 0 else (origin < LINE)
        pl.when(ok)(remote(dst, dst, sem, sem, sibling).wait_recv)

    local = []
    for which in range(2):
        local.append(pltpu.make_async_copy(acts_in[which], acts_out[which].at[c], here.at[count + which]))
    for m in range(count):
        local.append(pltpu.make_async_copy(block(w_in[m], c, cols[m]), w_out[m].at[slot(c, g)], here.at[m]))

    def stage_one(m):
        for step in range(1, LINE):
            to = me.line_to(step)
            copy = remote(
                block(w_in[m], to, cols[m]),
                w_out[m].at[slot(c, g)],
                one_s.at[m, step],
                one_r.at[m, step],
                me.at(to, g, k),
            )
            copy.start()
            sends.append(copy)

    def wait_one(m, step):
        dst = w_out[m].at[slot(me.line_from(step), g)]
        remote(dst, dst, one_s.at[m, step], one_r.at[m, step], sibling).wait_recv()

    def stage_two(m, step):
        where = w_out[m].at[slot(me.line_from(step), g)]
        src = block(w_in[m], c, cols[m]) if step == 0 else where
        for peer in range(1, 3 if groups == 4 else groups):
            copy = remote(
                src, where, two_s.at[m, step, peer], two_r.at[m, step, peer], me.at(c, me.group_to(peer), k)
            )
            copy.start()
            sends.append(copy)

    def wait_two(m, step, peer):
        dst = w_out[m].at[slot(me.line_from(step), me.group_from(peer))]
        remote(dst, dst, two_s.at[m, step, peer], two_r.at[m, step, peer], sibling).wait_recv()

    def stage_three(m, step):
        source, target = (1, 2) if step % 2 == 0 else (2, 1)
        where = w_out[m].at[slot(me.line_from(step), me.group_to(source))]
        copy = remote(where, where, three_s.at[m, step], three_r.at[m, step], me.at(c, me.group_to(target), k))
        copy.start()
        sends.append(copy)

    def wait_three(m, step):
        dst = w_out[m].at[slot(me.line_from(step), me.group_to(3))]
        remote(dst, dst, three_s.at[m, step], three_r.at[m, step], sibling).wait_recv()

    def relay(m):
        for step in range(LINE):
            for peer in (1, 2):
                wait_two(m, step, peer)
            stage_three(m, step)

    def pass_on(which, hop):
        for way in range(2):
            arrive(which, way, hop)
            if hop < LINE - 1:
                (hop_up if way == 0 else hop_down)(which, hop + 1, True)
            to_sibling(which, way, hop, True)

    def first_half(m):
        for step in range(1, LINE):
            wait_one(m, step)
            stage_two(m, step)

    order = list(range(count))
    near = groups == 4
    hop_up(0, 1, True)
    hop_down(0, 1, True)
    for m in order[:2]:
        stage_one(m)
        stage_two(m, 0)
    for copy in local:
        copy.start()
    hop_up(1, 1, True)
    hop_down(1, 1, True)
    for m in order[2:]:
        stage_one(m)
        stage_two(m, 0)
    first_half(0)
    pass_on(0, 1)
    first_half(1)
    if near:
        relay(0)
    pass_on(0, 2)
    first_half(2)
    pass_on(1, 1)
    if near:
        relay(1)
    first_half(3)
    pass_on(0, 3)
    pass_on(1, 2)
    if near:
        relay(2)
    pass_on(1, 3)
    if groups == 4:
        relay(order[-1])
        for m in order:
            for step in range(LINE):
                wait_three(m, step)
    else:
        for m in order:
            for step in range(LINE):
                for peer in range(1, groups):
                    wait_two(m, step, peer)
    for which in range(2):
        for hop in range(1, LINE):
            for way in range(2):
                arrive_sibling(which, way, hop)
    for copy in sends:
        copy.wait_send()
    for which in range(2):
        for hop in range(1, LINE):
            hop_up(which, hop, False)
            hop_down(which, hop, False)
            for way in range(2):
                to_sibling(which, way, hop, False)
    for copy in local:
        copy.wait()


def gather_all(groups, weights, tokens, cotangent):
    rows = weights[0].shape[0]
    cols = tuple(w.shape[1] // LINE for w in weights)
    count = len(weights)
    n_data = groups * LINE
    out_shape = [jax.ShapeDtypeStruct((n_data, rows, width), jnp.bfloat16) for width in cols]
    out_shape += [jax.ShapeDtypeStruct((LINE,) + tokens.shape, jnp.bfloat16)] * 2
    dma = pltpu.SemaphoreType.DMA
    peers = 3 if groups == 4 else groups
    return pl.pallas_call(
        partial(gather_kernel, groups, cols),
        out_shape=out_shape,
        in_specs=[ANY] * (count + 2),
        out_specs=[ANY] * (count + 2),
        scratch_shapes=[
            dma((count, LINE)),
            dma((count, LINE)),
            dma((count, LINE, peers)),
            dma((count, LINE, peers)),
            dma((count, LINE)),
            dma((count, LINE)),
            dma((2, LINE)),
            dma((2, LINE)),
            dma((2, LINE)),
            dma((2, LINE)),
            dma((2, 2, LINE)),
            dma((2, 2, LINE)),
            dma((count + 2,)),
        ],
        compiler_params=pltpu.CompilerParams(collective_id=0, has_side_effects=True),
        name="gather_all",
    )(*weights, tokens, cotangent)


def scatter_kernel(groups, cols, seq_dev, slot_len, *refs):
    count = len(cols)
    pick, m_ref, s_ref = refs[:3]
    g_in = refs[3 : 3 + count]
    mixed_ref, ssum_ref = refs[3 + count : 5 + count]
    g_out = refs[5 + count : 5 + 2 * count]
    rest = refs[5 + 2 * count :]
    m_own, m_got, m_line, m_all, m_send, s_own, s_got, s_line = rest[:8]
    g_own = rest[8 : 8 + count]
    g_got = rest[8 + count : 8 + 2 * count]
    (here, msib_s, msib_r, ssib_s, ssib_r, mline_s, mline_r, sline_s, sline_r, fin_s, fin_r, mall_s, mall_r,
     mout_s, mout_r, gp_s, gp_r, gl_s, gl_r) = rest[8 + 2 * count :]
    me = Place(groups)
    c, g, k = me.line, me.group, me.core
    me.greet()
    sibling = me.at(c, g, me.other)
    feat = D // (2 * LINE)
    seqs = LINE * seq_dev
    sends = []

    def go(copy):
        copy.start()
        sends.append(copy)

    def feature(ref, line, core):
        return ref.at[:, :, pl.ds(pl.multiple_of((line * 2 + core) * feat, 128), feat)]

    own_m, own_s = [], []
    for step in range(LINE):
        line = me.line_to(step)
        go(remote(s_ref.at[line, me.other], s_got.at[line], ssib_s.at[step], ssib_r.at[step], sibling))
        copy = pltpu.make_async_copy(s_ref.at[line, k], s_own.at[line], here.at[0, step])
        copy.start()
        own_s.append(copy)
    for step in range(LINE):
        line = me.line_to(step)
        go(remote(feature(m_ref, line, me.other), m_got.at[line], msib_s.at[step], msib_r.at[step], sibling))
        copy = pltpu.make_async_copy(feature(m_ref, line, k), m_own.at[line], here.at[1, step])
        copy.start()
        own_m.append(copy)
    own_g = []
    for m in range(count):
        for peer in range(1, groups):
            to = me.group_to(peer)
            go(remote(g_in[m].at[:, to], g_got[m].at[peer - 1], gp_s.at[m, peer], gp_r.at[m, peer], me.at(c, to, k)))
        copy = pltpu.make_async_copy(g_in[m].at[:, g], g_own[m], here.at[2, m])
        copy.start()
        own_g.append(copy)

    def add_rows(total, ref, others, rows, chunk):
        def body(i, carry):
            at = pl.ds(pl.multiple_of(i * chunk, chunk), chunk)
            acc = ref(at)[...].astype(jnp.float32)
            for other in others:
                acc = acc + other(at)[...].astype(jnp.float32)
            total(at)[...] = acc.astype(jnp.bfloat16)
            return carry

        lax.fori_loop(0, rows // chunk, body, 0)

    for step in (1, 2, 3, 0):
        line = me.line_to(step)
        remote(s_got.at[line], s_got.at[line], ssib_s.at[step], ssib_r.at[step], sibling).wait_recv()
        own_s[step].wait()
        add_rows(
            lambda at: s_own.at[line, at], lambda at: s_own.at[line, at], [lambda at: s_got.at[line, at]], slot_len, 16
        )
        if step:
            go(remote(s_own.at[line], s_line.at[step - 1], sline_s.at[step], sline_r.at[step], me.at(line, g, k)))
    for step in (1, 2, 3, 0):
        line = me.line_to(step)
        remote(m_got.at[line], m_got.at[line], msib_s.at[step], msib_r.at[step], sibling).wait_recv()
        own_m[step].wait()
        for s in range(seqs):
            add_rows(
                lambda at: m_own.at[line, s, at],
                lambda at: m_own.at[line, s, at],
                [lambda at: m_got.at[line, s, at]],
                slot_len,
                64,
            )
        if step:
            go(remote(m_own.at[line], m_line.at[step - 1], mline_s.at[step], mline_r.at[step], me.at(line, g, k)))

    keep = []

    def sum_groups(m):
        for peer in range(1, groups):
            dst = g_got[m].at[peer - 1]
            remote(dst, dst, gp_s.at[m, peer], gp_r.at[m, peer], sibling).wait_recv()
        own_g[m].wait()
        rows = g_own[m].shape[1]
        width = pl.ds(pl.multiple_of(c * cols[m], 128), cols[m])
        for step in (1, 2, 3, 0):
            line = me.line_to(step)
            add_rows(
                partial(lambda m, line, at: g_own[m].at[line, at], m, line),
                partial(lambda m, line, at: g_own[m].at[line, at], m, line),
                [partial(lambda m, line, p, at: g_got[m].at[p, line, at], m, line, p) for p in range(groups - 1)],
                rows,
                16,
            )
            if step:
                go(remote(g_own[m].at[line], g_out[m].at[:, width], gl_s.at[m, step], gl_r.at[m, step], me.at(line, g, k)))
            else:
                copy = pltpu.make_async_copy(g_own[m].at[line], g_out[m].at[:, width], here.at[2, m])
                copy.start()
                keep.append(copy)

    def finish_inputs():
        for step in range(1, LINE):
            dst = s_line.at[step - 1]
            remote(dst, dst, sline_s.at[step], sline_r.at[step], sibling).wait_recv()
        add_rows(
            lambda at: s_own.at[c, at],
            lambda at: s_own.at[c, at],
            [partial(lambda step, at: s_line.at[step, at], step) for step in range(LINE - 1)],
            slot_len,
            16,
        )
        go(remote(s_own.at[c], ssum_ref.at[k], fin_s, fin_r, sibling))
        mine_s = pltpu.make_async_copy(s_own.at[c], ssum_ref.at[k], here.at[0, 0])
        mine_s.start()
        keep.append(mine_s)

    sum_groups(0)
    finish_inputs()
    sum_groups(1)
    for step in range(1, LINE):
        dst = m_line.at[step - 1]
        remote(dst, dst, mline_s.at[step], mline_r.at[step], sibling).wait_recv()
    ours = pl.ds(g * seqs, seqs)
    for s in range(seqs):
        add_rows(
            lambda at: m_all.at[g * seqs + s, at],
            lambda at: m_own.at[c, s, at],
            [partial(lambda step, at: m_line.at[step, s, at], step) for step in range(LINE - 1)],
            slot_len,
            64,
        )
    for peer in range(1, groups):
        go(remote(m_all.at[ours], m_all.at[ours], mall_s.at[peer], mall_r.at[peer], me.at(c, me.group_to(peer), k)))

    sum_groups(2)
    sum_groups(3)

    for peer in range(1, groups):
        dst = m_all.at[pl.ds(me.group_from(peer) * seqs, seqs)]
        remote(dst, dst, mall_s.at[peer], mall_r.at[peer], sibling).wait_recv()
    mixed_cols = pl.ds(pl.multiple_of((c * 2 + k) * feat, 128), feat)
    for step in (1, 2, 3, 0):
        line = me.line_to(step)
        for s in range(seq_dev):
            m_send[line, s] = m_all[pick[line * seq_dev + s]]
        if step:
            go(remote(m_send.at[line], mixed_ref.at[:, :, mixed_cols], mout_s.at[0, step], mout_r.at[0, step], me.at(line, g, k)))
        else:
            copy = pltpu.make_async_copy(m_send.at[line], mixed_ref.at[:, :, mixed_cols], here.at[1, 0])
            copy.start()
            keep.append(copy)
        go(remote(m_send.at[line], mixed_ref.at[:, :, mixed_cols], mout_s.at[1, step], mout_r.at[1, step], me.at(line, g, me.other)))
    for m in range(count):
        for step in range(1, LINE):
            dst = g_out[m].at[:, pl.ds(pl.multiple_of(me.line_from(step) * cols[m], 128), cols[m])]
            remote(dst, dst, gl_s.at[m, step], gl_r.at[m, step], sibling).wait_recv()
    for step in range(LINE):
        for core, way in ((k, 0), (me.other, 1)):
            if step or way:
                dst = mixed_ref.at[
                    :, :, pl.ds(pl.multiple_of((me.line_from(step) * 2 + core) * feat, 128), feat)
                ]
                remote(dst, dst, mout_s.at[way, step], mout_r.at[way, step], sibling).wait_recv()
    dst = ssum_ref.at[me.other]
    remote(dst, dst, fin_s, fin_r, sibling).wait_recv()
    for copy in sends:
        copy.wait_send()
    for copy in keep:
        copy.wait()


def scatter_all(groups, cols, pick, mixed_part, s_part, grads):
    seq_dev, slot_len = s_part.shape[1:3]
    rows = grads[0].shape[2]
    count = len(cols)
    feat = D // (2 * LINE)
    seqs = LINE * seq_dev
    dma = pltpu.SemaphoreType.DMA
    low = jnp.bfloat16
    return pl.pallas_call(
        partial(scatter_kernel, groups, cols, seq_dev, slot_len),
        out_shape=[
            jax.ShapeDtypeStruct((seq_dev, slot_len, D), low),
            jax.ShapeDtypeStruct((seq_dev, slot_len, D), low),
        ]
        + [jax.ShapeDtypeStruct((rows, LINE * width), low) for width in cols],
        in_specs=[SMEM] + [ANY] * (2 + count),
        out_specs=[ANY] * (2 + count),
        scratch_shapes=[
            pltpu.VMEM((LINE, seqs, slot_len, feat), low),
            pltpu.VMEM((LINE, seqs, slot_len, feat), low),
            pltpu.VMEM((LINE - 1, seqs, slot_len, feat), low),
            pltpu.VMEM((groups * seqs, slot_len, feat), low),
            pltpu.VMEM((LINE, seq_dev, slot_len, feat), low),
            pltpu.VMEM((LINE, slot_len, D), low),
            pltpu.VMEM((LINE, slot_len, D), low),
            pltpu.VMEM((LINE - 1, slot_len, D), low),
        ]
        + [pltpu.VMEM((LINE, rows, width), low) for width in cols]
        + [pltpu.VMEM((groups - 1, LINE, rows, width), low) for width in cols]
        + [
            dma((3, LINE)),
            dma((LINE,)),
            dma((LINE,)),
            dma((LINE,)),
            dma((LINE,)),
            dma((LINE,)),
            dma((LINE,)),
            dma((LINE,)),
            dma((LINE,)),
            dma(()),
            dma(()),
            dma((groups,)),
            dma((groups,)),
            dma((2, LINE)),
            dma((2, LINE)),
            dma((count, groups)),
            dma((count, groups)),
            dma((count, LINE)),
            dma((count, LINE)),
        ],
        compiler_params=pltpu.CompilerParams(
            collective_id=1, has_side_effects=True, vmem_limit_bytes=58 * 1024 * 1024
        ),
        name="scatter_all",
    )(pick, mixed_part, s_part, *grads)


def sums_kernel(groups, v_ref, r_ref, tot_ref, both_ref, by_group, by_line, gs, gr, ls, lr, ss, sr):
    me = Place(groups)
    c, g, k = me.line, me.group, me.core
    me.greet()
    sibling = me.at(c, g, me.other)
    sends = []

    def go(copy):
        copy.start()
        sends.append(copy)

    both_ref[k] = r_ref[...]
    go(remote(r_ref, both_ref.at[k], ss.at[0], sr.at[0], sibling))
    for peer in range(1, groups):
        go(remote(v_ref, by_group.at[g], gs.at[peer], gr.at[peer], me.at(c, me.group_to(peer), k)))
    by_group[g] = v_ref[...]
    for peer in range(1, groups):
        dst = by_group.at[me.group_from(peer)]
        remote(dst, dst, gs.at[peer], gr.at[peer], sibling).wait_recv()
    acc = by_group[0]
    for i in range(1, groups):
        acc = acc + by_group[i]
    by_line[c] = acc
    for step in range(1, LINE):
        go(remote(by_line.at[c], by_line.at[c], ls.at[step], lr.at[step], me.at(me.line_to(step), g, k)))
    for step in range(1, LINE):
        dst = by_line.at[me.line_from(step)]
        remote(dst, dst, ls.at[step], lr.at[step], sibling).wait_recv()
    acc = by_line[0]
    for i in range(1, LINE):
        acc = acc + by_line[i]
    tot_ref[k] = acc
    go(remote(tot_ref.at[k], tot_ref.at[k], ss.at[1], sr.at[1], sibling))
    remote(both_ref.at[me.other], both_ref.at[me.other], ss.at[0], sr.at[0], sibling).wait_recv()
    remote(tot_ref.at[me.other], tot_ref.at[me.other], ss.at[1], sr.at[1], sibling).wait_recv()
    for copy in sends:
        copy.wait_send()


def small_sums(groups, vector, row_part):
    dma = pltpu.SemaphoreType.DMA
    return pl.pallas_call(
        partial(sums_kernel, groups),
        out_shape=[
            jax.ShapeDtypeStruct((2,) + vector.shape, jnp.float32),
            jax.ShapeDtypeStruct((2,) + row_part.shape, jnp.float32),
        ],
        in_specs=[VMEM, VMEM],
        out_specs=[VMEM, VMEM],
        scratch_shapes=[
            pltpu.VMEM((groups,) + vector.shape, jnp.float32),
            pltpu.VMEM((LINE,) + vector.shape, jnp.float32),
            dma((groups,)),
            dma((groups,)),
            dma((LINE,)),
            dma((LINE,)),
            dma((2,)),
            dma((2,)),
        ],
        compiler_params=pltpu.CompilerParams(
            collective_id=2, has_side_effects=True, vmem_limit_bytes=32 * 1024 * 1024
        ),
        name="small_sums",
    )(vector, row_part)


def per_device(
    tokens,
    cotangent,
    lengths,
    permutation,
    w_qkv,
    w_dense,
    w_fc1,
    w_fc2,
    norm_vectors,
    split_biases,
    row_state,
    col_state,
    norm_moment,
    bias_moment,
):
    f32, low = jnp.float32, jnp.bfloat16
    n_data = lax.axis_size("dp")
    groups = n_data // LINE
    data = lax.axis_index("dp")
    core = lax.axis_index("tensor")
    line = data // groups
    group = data % groups
    seq_dev, slot_len, width = tokens.shape
    rows_own = w_qkv.shape[0]
    seqs = LINE * seq_dev
    rows = seqs * slot_len
    head_dim = D // HEADS
    rot_dims = head_dim // 4
    root = math.sqrt(head_dim)
    weights = (w_qkv, w_dense, w_fc1, w_fc2)
    cols = tuple(w.shape[1] // LINE for w in weights)
    order = (0, 2, 1, 3)
    lows = [weights[i].astype(low) for i in order]
    got = gather_all(groups, lows, tokens, cotangent)
    full = [None] * 4
    for place, i in enumerate(order):
        full[i] = got[place].reshape(D, cols[i])
    x_all, back_all = got[4], got[5]
    inputs = x_all.reshape(rows, width).astype(f32)
    mine = (jnp.arange(LINE)[:, None] * groups + group) * seq_dev + jnp.arange(seq_dev)[None, :]
    my_lengths = jnp.take(lengths, mine.reshape(-1))
    places = jnp.arange(slot_len, dtype=jnp.int32)
    valid = (places[None, :] < my_lengths[:, None]).reshape(rows, 1)
    back = jnp.where(valid, back_all.reshape(rows, width), jnp.zeros((), low))
    gain_one, shift_one, gain_two, shift_two, bias_dense, bias_out = (norm_vectors[i] for i in range(6))
    centre = inputs - jnp.mean(inputs, -1, keepdims=True)
    scale = lax.rsqrt(jnp.mean(centre * centre, -1, keepdims=True) + eps_norm)
    unit = centre * scale
    norm_one = (unit * gain_one + shift_one).astype(low)
    norm_two = (unit * gain_two + shift_two).astype(low)
    bias_qkv = lax.dynamic_slice_in_dim(split_biases[0], line * cols[0], cols[0])
    bias_mlp = lax.dynamic_slice_in_dim(split_biases[0], LINE * cols[0] + line * cols[2], cols[2])
    qkv = (jnp.dot(norm_one, full[0], preferred_element_type=f32) + bias_qkv).reshape(seqs, slot_len, 3 * head_dim)
    pre = jnp.dot(norm_two, full[2], preferred_element_type=f32) + bias_mlp
    cosine, sine = rotary_tables(slot_len, rot_dims)
    query = rotate(qkv[:, :, :head_dim], cosine, sine, rot_dims).astype(low)
    keys = rotate(qkv[:, :, head_dim : 2 * head_dim], cosine, sine, rot_dims).astype(low)
    values = qkv[:, :, 2 * head_dim :].astype(low)
    causal = places[:, None] >= places[None, :]
    raw = jnp.einsum("sqd,skd->sqk", query, keys, preferred_element_type=f32) / root
    scores = jnp.where(causal, raw, neg_large)
    peak = jnp.max(scores, -1, keepdims=True)
    expo = jnp.exp(scores - peak)
    probs = expo / jnp.sum(expo, -1, keepdims=True)
    probs_low = probs.astype(low)
    attn = (
        jnp.einsum("sqk,skd->sqd", probs_low, values, preferred_element_type=f32).astype(low).reshape(rows, cols[1])
    )
    hidden, gelu_pull = jax.vjp(partial(jax.nn.gelu, approximate=False), pre)
    hidden = hidden.astype(low)
    feat = D // (2 * LINE)
    mine_feat = (jnp.arange(D) // feat) == (line * 2 + core)
    residual = jnp.where(mine_feat, inputs + (bias_dense + bias_out), 0.0)
    mixed_part = contract_last(attn, full[1]) + contract_last(hidden, full[3]) + residual
    mixed_part = jnp.where(valid, mixed_part, 0.0).astype(low)
    attn_grad = jnp.dot(back, full[1], preferred_element_type=f32).astype(low).reshape(seqs, slot_len, head_dim)
    hidden_grad = jnp.dot(back, full[3], preferred_element_type=f32)
    pre_grad = gelu_pull(hidden_grad)[0].astype(low)
    prob_grad = jnp.einsum("sqd,skd->sqk", attn_grad, values, preferred_element_type=f32)
    row_dot = jnp.sum(probs * prob_grad, -1, keepdims=True)
    score_grad = (probs * (prob_grad - row_dot)).astype(low)
    value_grad = jnp.einsum("sqk,sqd->skd", probs_low, attn_grad, preferred_element_type=f32)
    query_grad = jnp.einsum("sqk,skd->sqd", score_grad, keys, preferred_element_type=f32) / root
    key_grad = jnp.einsum("sqk,sqd->skd", score_grad, query, preferred_element_type=f32) / root
    qkv_grad = (
        jnp.concatenate(
            [rotate(query_grad, cosine, -sine, rot_dims), rotate(key_grad, cosine, -sine, rot_dims), value_grad], -1
        )
        .astype(low)
        .reshape(rows, cols[0])
    )
    norm_one_grad = contract_last(qkv_grad, full[0])
    norm_two_grad = contract_last(pre_grad, full[2])
    s_part = (norm_one_grad * gain_one + norm_two_grad * gain_two).astype(low)
    grads_part = [
        contract_first(norm_one, qkv_grad),
        contract_first(back, attn),
        contract_first(norm_two, pre_grad),
        contract_first(back, hidden),
    ]
    grads_part = [part.astype(low).reshape(LINE, groups, rows_own, -1) for part in grads_part]
    source = jnp.take(permutation, mine.reshape(-1))
    chip, inside = source // seq_dev, source % seq_dev
    pick = ((chip % groups) * seqs + (chip // groups) * seq_dev + inside).astype(jnp.int32)
    outs = scatter_all(
        groups,
        tuple(cols[i] for i in order),
        pick,
        mixed_part.reshape(seqs, slot_len, width),
        s_part.reshape(LINE, seq_dev, slot_len, width),
        [grads_part[i] for i in order],
    )
    mixed, s_sum = outs[:2]
    grads = [None] * 4
    for place, i in enumerate(order):
        grads[i] = outs[2 + place].astype(f32)
    own_x = tokens.reshape(-1, width).astype(f32)
    own_centre = own_x - jnp.mean(own_x, -1, keepdims=True)
    own_scale = lax.rsqrt(jnp.mean(own_centre * own_centre, -1, keepdims=True) + eps_norm)
    own_unit = own_centre * own_scale
    own_valid = (places[None, :] < lax.dynamic_slice_in_dim(lengths, data * seq_dev, seq_dev)[:, None]).reshape(-1, 1)
    own_back = jnp.where(own_valid, cotangent.reshape(-1, width), jnp.zeros((), low)).astype(f32)
    flow = s_sum.reshape(-1, width).astype(f32)
    through = own_scale * (
        flow - jnp.mean(flow, -1, keepdims=True) - own_unit * jnp.mean(flow * own_unit, -1, keepdims=True)
    )
    grad_tokens = (own_back + through).astype(low).reshape(seq_dev, slot_len, width)
    own_out = jnp.where(core == 0, jnp.sum(own_back, 0), 0.0)
    norm_part = jnp.stack(
        [
            jnp.sum(norm_one_grad * unit, 0),
            jnp.sum(norm_one_grad, 0),
            jnp.sum(norm_two_grad * unit, 0),
            jnp.sum(norm_two_grad, 0),
            own_out,
        ]
    )
    bias_vec = jnp.zeros((split_biases.shape[1],), f32)
    bias_vec = lax.dynamic_update_slice_in_dim(bias_vec, jnp.sum(qkv_grad.astype(f32), 0), line * cols[0], 0)
    bias_vec = lax.dynamic_update_slice_in_dim(
        bias_vec, jnp.sum(pre_grad.astype(f32), 0), LINE * cols[0] + line * cols[2], 0
    )
    squares = [grad * grad + eps_second for grad in grads]
    row_part = jnp.stack([jnp.sum(square, 1) for square in squares])
    col_part = jnp.concatenate([jnp.sum(square, 0) for square in squares])
    row_old = jnp.where(core == 0, jnp.sum(row_state, 1), 0.0)
    pieces = [norm_part.reshape(-1), bias_vec, col_part, row_old]
    total_len = sum(piece.shape[0] for piece in pieces)
    padded = -(-total_len // 1024) * 1024
    vector = jnp.concatenate(pieces + [jnp.zeros((padded - total_len,), f32)]).reshape(-1, 128)
    row_pad = -(-rows_own // 128) * 128
    row_block = jnp.zeros((8, row_pad), f32).at[:4, :rows_own].set(row_part)
    totals, row_both = small_sums(groups, vector, row_block)
    totals = totals.reshape(2, -1)
    row_total = (row_both[0] + row_both[1])[:4, :rows_own]
    at_bias = 5 * D
    at_col = at_bias + split_biases.shape[1]
    at_row = at_col + col_state.shape[1]
    both = totals[0] + totals[1]
    norm_total = both[:at_bias].reshape(5, D)
    norm_total = jnp.concatenate([norm_total, norm_total[4:]], 0)
    mine_total = lax.dynamic_index_in_dim(totals, core, 0, False)
    bias_total = mine_total[at_bias:at_col][None, :]
    col_total = mine_total[at_col:at_row]
    all_cols = both[at_col:at_row]
    row_old_sum = both[at_row : at_row + 4]
    col_new = decay * col_state + (1.0 - decay) * (col_total[None, :] / D)
    full_cols = (3.0 * D, 1.0 * D, 1.0 * FF, 1.0 * FF)
    rates = (
        rate_scale / math.sqrt(D),
        rate_scale / math.sqrt(D // 8),
        rate_scale / math.sqrt(D),
        rate_scale / math.sqrt(FF),
    )
    new_list, row_list = [], []
    edge = 0
    for i in range(4):
        wide = weights[i].shape[1]
        row_new = decay * row_state[i] + (1.0 - decay) * (row_total[i] / full_cols[i])
        mass = jnp.sum(all_cols[edge : edge + wide])
        mean = (decay * row_old_sum[i] + (1.0 - decay) * (mass / full_cols[i])) / D
        second = row_new[:, None] * col_new[0, edge : edge + wide][None, :] / mean
        new_list.append(weights[i] - rates[i] * grads[i] * lax.rsqrt(second))
        row_list.append(row_new)
        edge += wide
    row_new = jnp.stack(row_list)
    norm_moment_new = decay * norm_moment + (1.0 - decay) * (norm_total * norm_total + eps_second)
    norm_new = norm_vectors - rate_norm * norm_total * lax.rsqrt(norm_moment_new)
    bias_moment_new = decay * bias_moment + (1.0 - decay) * (bias_total * bias_total + eps_second)
    bias_new = split_biases - rate_vector * bias_total * lax.rsqrt(bias_moment_new)
    return (
        mixed,
        grad_tokens,
        *grads,
        *new_list,
        *[new.astype(low) for new in new_list],
        row_new,
        col_new,
        norm_total,
        norm_moment_new,
        norm_new,
        bias_total,
        bias_moment_new,
        bias_new,
    )


def solution(mesh):
    halves = P("dp", "tensor")
    split = P("tensor", None)
    in_specs = (
        P("dp", None, None),
        P("dp", None, None),
        P(),
        P(),
        halves,
        halves,
        halves,
        halves,
        P(),
        split,
        P(None, "dp"),
        split,
        P(),
        split,
    )
    out_specs = (
        (P("dp", None, None),) * 2
        + (halves,) * 12
        + (P(None, "dp"), split)
        + (P(),) * 3
        + (split,) * 3
    )
    return jax.shard_map(
        per_device, mesh=mesh, in_specs=in_specs, out_specs=out_specs, check_vma=False
    )
```

time: 3760 us -> 701 us (0.19)
  waiting for transfers between devices: 3190 us -> 0 us
  Pallas kernels: 0 us -> 460 us
  local copies, waits for them, and re-layouts: 148 us -> 21.1 us
  other arithmetic: 158 us -> 68.4 us
  starting transfers between devices: 75.8 us -> 0 us
    unnamed x6 -> x0, waiting for transfers between devices: 2410 us -> none
    pallas_call x0 -> x3, Pallas kernels: none -> 460 us  [the longest x1 239 us: scatter_all(): pl.pallas_call(partial(scatter_kernel, groups, cols, seq_dev, slot_len),...]
    all_gather x2 -> x0, waiting for transfers between devices: 348 us -> none  [the longest x1 306 us: per_device(): part = lax.all_gather(in_local, 'dp', axis=0, tiled=True)]
    all_to_all x4 -> x0, waiting for transfers between devices: 332 us -> none  [the longest x2 170 us: route(): lax.all_to_all(ordered, 'dp', split_axis=1, concat_axis=2, tiled=True)]
    psum x2 -> x0, waiting for transfers between devices: 106 us -> none  [the longest x1 106 us: per_device(): lax.psum((col_part, jnp.sum(row_new, 1), norm_part, bias_part), 'dp')]
    all_to_all x4 -> x0, starting transfers between devices: 75.2 us -> none  [the longest x2 62.2 us: route(): lax.all_to_all(ordered, 'dp', split_axis=1, concat_axis=2, tiled=True)]
    concatenate x4 -> x0, other arithmetic: 68.3 us -> none  [the longest x1 65.1 us: per_device(): jnp.concatenate([inward[:, :qkv_cols], outward[:, :dense_cols], inward[:,...]
  transfers between devices with their start and end apart: 9 -> 0, of which waited for: 8 -> 0; matrix products, arithmetic and copies ran while one was open for 4% -> 0% of each run, Pallas kernels for 0% -> 0%
where the time goes in v1:
time: 701 us; the launch traced here: 694 us
  Pallas kernels  460 us (66%)
  matrix products  137 us (20%)
  other arithmetic  68.4 us (10%)
  local copies, waits for them, and re-layouts  21.1 us (3%)
  between operations  7.13 us (1%)
    pallas_call x1, Pallas kernels, scatter_all(): pl.pallas_call(partial(scatter_kernel, groups, cols, seq_dev, slot_len),...  239 us
    pallas_call x1, Pallas kernels, gather_all(): pl.pallas_call(partial(gather_kernel, groups, cols), out_shape=out_shape,...  192 us
    dot_general x4, matrix products, contract_last(): lax.dot_general(left, right, (((1,), (1,)), ((), ())), preferred_element_...  48.4 us
    dot_general x4, matrix products, contract_first(): lax.dot_general(left, right, (((0,), (0,)), ((), ())), preferred_element_...  35.7 us
    pallas_call x1, Pallas kernels, small_sums(): pl.pallas_call(partial(sums_kernel, groups), out_shape=[jax.ShapeDtypeStr...  28.8 us
    dot_general x1, matrix products, per_device(): hidden_grad = jnp.dot(back, full[3], preferred_element_type=f32)  24.9 us

profile of v1, /device:TPU:0, one launch (start us, length us, event | category | flops | bytes accessed | tf_op | source)
XLA Modules:
  0.0 693.7 jit_solution(7168732986455879440)
XLA Ops:
  6.7 2.0 fusion.36
  16.7 2.4 convert_element_type.133.refs_0_
  21.3 192.2 %gather_all.1 = (bf16[16,128,768]{2,1,0:T(8,128)(2,1)}, bf16[16,128,1024]{2,1,0:T(8,128)(2,1)}, bf16[16,128,256]{2,1,0:T(8,128)(2,1)}, bf16[16,128,1024]{2,1,0:T...) custom-call(bf16[128,3072]{1,0:T(8,128)(2,1)} %convert_element_type.133.refs_0_, ...), custom_call_target="tpu_custom_call" | custom-call | tf_op jit(solution)/shard_map/gather_all/pallas_call | solution.py:318
  213.5 3.7 convert_reduce_fusion
  217.9 4.6 fusion.9
  223.2 3.4 broadcast_select_fusion
  227.3 3.8 bitcast_select_fusion
  231.8 2.7 convolution_convert_fusion.4
  234.5 4.8 fusion.6
  239.3 5.2 convolution_add_fusion
  244.6 9.0 %fusion.77 = f32[1536,1024]{1,0:T(8,128)} fusion(bf16[1536,2048]{1,0:T(8,128)(2,1)S(1)} %bitcast.146, bf16[2048,1024]{1,0:T(8,128)(2,1)S(1)} %bitcast.191), kind=kOutput, calls=%fused_computation.199 | convolution fusion | flops 6442450944 | bytes 16777216 | tf_op jit(solution)/shard_map/dot_general | solution.py:700
  257.1 4.9 fusion.76
  262.0 3.0 convolution_convert_fusion.5
  272.8 4.1 concatenate.44
  277.7 6.0 convolution_convert_fusion.3
  283.7 24.9 %convert_reduce_fusion.1 = (f32[1024]{0:T(1024)S(1)}, bf16[1536,1024]{1,0:T(8,128)(2,1)}, f32[1536,1024]{1,0:T(8,128)}) fusion(f32[1536,1024]{1,0:T(8,128)} %fusion.77, f32[1024]{0:T(1024)S(1)} %bitcast.174, bf16[1536,2048]{1,0:T(8,128)(2,1)} %bitcast.141, bf16[2048,1024]{1,0:T(8,128)(2,1)S(1)} %bitcast.192), kind=kOutput, calls=%fused_computation.35 | convolution fusion | flops 6560414720 | bytes 26222592 | tf_op jit(solution)/shard_map/dot_general | solution.py:723
  308.6 4.0 multiply_convert_fusion
  312.6 11.4 %convolution_convert_fusion = bf16[2048,1024]{1,0:T(8,128)(2,1)} fusion(bf16[1536,2048]{1,0:T(8,128)(2,1)} %bitcast_select_fusion, bf16[1536,1024]{1,0:T(8,128)(2,1)S(1)} %multiply_convert_fusion), kind=kOutput, calls=%fused_computation.60 | convolution fusion | flops 6444548096 | bytes 13631488 | tf_op jit(solution)/shard_map/dot_general | solution.py:53
  324.2 9.1 %fusion.78 = f32[1536,2048]{1,0:T(8,128)} fusion(bf16[1536,1024]{1,0:T(8,128)(2,1)S(1)} %multiply_convert_fusion, bf16[2048,1024]{1,0:T(8,128)(2,1)S(1)} %bitcast.193), kind=kOutput, calls=%fused_computation.200 | convolution fusion | flops 6442450944 | bytes 19922944 | tf_op jit(solution)/shard_map/dot_general | solution.py:47
  333.4 8.5 %fusion.13 = bf16[1536,2048]{1,0:T(8,128)(2,1)} fusion(bf16[4,2,192,2048]{3,2,1,0:T(8,128)(2,1)S(1)} %bitcast.134, f32[1536,2048]{1,0:T(8,128)} %fusion.78, bf16[1536,256]{1,0:T(8,128)(2,1)S(1)} %bitcast.199, bf16[2048,256]{1,0:T(8,128)(2,1)S(1)} %bitcast.197, f32[2048]{0:T(1024)S(1)} %bitcast.177, pred[1536]{0:T(1024)(128)(4,1)S(1)} %copy-done.45, ...), kind=kOutput, calls=%fused_computation.19 | convolution fusion | flops 1632632832 | bytes 27012608 | tf_op jit(solution)/shard_map/dot_general | solution.py:47
  342.0 8.2 %fusion.79 = f32[1536,2048]{1,0:T(8,128)} fusion(bf16[1536,768]{1,0:T(8,128)(2,1)S(1)} %concatenate.44, bf16[2048,768]{1,0:T(8,128)(2,1)S(1)} %bitcast.195), kind=kOutput, calls=%fused_computation.201 | convolution fusion | flops 4831838208 | bytes 18087936 | tf_op jit(solution)/shard_map/dot_general | solution.py:47
  350.2 22.6 %fusion.66 = (f32[2048]{0:T(1024)S(1)}, f32[2048]{0:T(1024)S(1)}, bf16[1536,2048]{1,0:T(8,128)(2,1)}, f32[2048]{0:T(1024)S(1)}, f32[2048]{0:T(1024)S(1)}, /*inde...) fusion(f32[1536]{0:T(1024)S(1)} %copy-done.42, f32[1536]{0:T(1024)S(1)} %copy-done.41, ...), kind=kOutput, calls=%fused_computation.189 | convolution fusion | flops 6502211584 | bytes 45166592 | tf_op jit(solution)/shard_map/dot_general | solution.py:47
  372.7 9.8 %convolution_convert_fusion.2 = bf16[2048,768]{1,0:T(8,128)(2,1)} fusion(bf16[1536,2048]{1,0:T(8,128)(2,1)} %get-tuple-element.104, bf16[1536,768]{1,0:T(8,128)(2,1)S(1)} %concatenate.44), kind=kOutput, calls=%fused_computation.66 | convolution fusion | flops 4833411072 | bytes 11796480 | tf_op jit(solution)/shard_map/dot_general | solution.py:53
  382.6 8.6 %convolution_convert_fusion.1 = bf16[2048,1024]{1,0:T(8,128)(2,1)} fusion(bf16[1536,2048]{1,0:T(8,128)(2,1)S(1)} %copy-done.58, bf16[1536,1024]{1,0:T(8,128)(2,1)S(1)} %copy-done.59), kind=kOutput, calls=%fused_computation.61 | convolution fusion | flops 6444548096 | bytes 13631488 | tf_op jit(solution)/shard_map/dot_general | solution.py:53
  391.1 238.6 %scatter_all.1 = (bf16[2,192,2048]{2,1,0:T(8,128)(2,1)}, bf16[2,192,2048]{2,1,0:T(8,128)(2,1)}, bf16[128,3072]{1,0:T(8,128)(2,1)}, bf16[128,4096]{1,0:T(8,128)(2...) custom-call(s32[8]{0:T(128)} %get-tuple-element.140.refs_0_, bf16[8,192,2048]{2,1,0:T(8,128)(2,1)} %bitcast.144, ...), custom_call_target="tpu_custom_call" | custom-call | tf_op jit(solution)/shard_map/scatter_all/pallas_call | solution.py:531
  629.8 2.6 convert_reduce_fusion.2
  632.5 2.6 convert_reduce_fusion.5
  636.8 3.6 fusion.39
  640.6 28.8 %small_sums.1 = (f32[2,240,128]{2,1,0:T(8,128)S(1)}, f32[2,8,128]{2,1,0:T(8,128)S(1)}) custom-call(f32[240,128]{1,0:T(8,128)S(1)} %bitcast.130, f32[8,128]{1,0:T(8,128)S(1)} %select_maximum_fusion.r_ref), custom_call_target="tpu_custom_call" | custom-call | tf_op jit(solution)/shard_map/small_sums/pallas_call | solution.py:621
  684.7 1.9 fusion.71
  686.6 2.2 fusion.69
  689.9 2.2 fusion.68
  (218 shorter events, 45.2 us)
Async XLA Ops:
  0.7 9.9 %copy-start = (s32[32]{0:T(128)S(1)}, s32[32]{0:T(128)}, u32[]{:S(2)}) copy-start(s32[32]{0:T(128)} %param.21) | copy-start | bytes 388
  0.7 13.0 %copy-start.28 = (f32[6,2048]{1,0:T(8,128)S(1)}, f32[6,2048]{1,0:T(8,128)}, u32[]{:S(2)}) copy-start(f32[6,2048]{1,0:T(8,128)} %param.26) | copy-start | bytes 147460
  0.7 18.4 %copy-start.3 = (f32[128,4096]{1,0:T(8,128)S(1)}, f32[128,4096]{1,0:T(8,128)}, u32[]{:S(2)}) copy-start(f32[128,4096]{1,0:T(8,128)} %param.24) | copy-start | bytes 6291460
  0.7 14.2 %copy-start.15 = (f32[128,1024]{1,0:T(8,128)S(1)}, f32[128,1024]{1,0:T(8,128)}, u32[]{:S(2)}) copy-start(f32[128,1024]{1,0:T(8,128)} %param.23) | copy-start | bytes 1572868
  12.0 214.6 %copy-start.44 = (pred[1536]{0:T(1024)(128)(4,1)}, pred[1536]{0:T(1024)(128)(4,1)S(1)}, u32[]{:S(2)}) copy-start(pred[1536]{0:T(1024)(128)(4,1)S(1)} %lt.86) | copy-start | bytes 4612
  14.3 220.2 %copy-start.32 = (f32[1,2048]{1,0:T(1,128)}, f32[1,2048]{1,0:T(1,128)S(1)}, u32[]{:S(2)}) copy-start(f32[1,2048]{1,0:T(1,128)S(1)} %get-tuple-element.127) | copy-start | bytes 24580
  14.3 220.2 %copy-start.34 = (f32[1,2048]{1,0:T(1,128)}, f32[1,2048]{1,0:T(1,128)S(1)}, u32[]{:S(2)}) copy-start(f32[1,2048]{1,0:T(1,128)S(1)} %get-tuple-element.128) | copy-start | bytes 24580
  14.3 220.2 %copy-start.36 = (f32[1,2048]{1,0:T(1,128)}, f32[1,2048]{1,0:T(1,128)S(1)}, u32[]{:S(2)}) copy-start(f32[1,2048]{1,0:T(1,128)S(1)} %get-tuple-element.129) | copy-start | bytes 24580
  16.7 236.9 %copy-start.23 = (f32[192,32]{1,0:T(8,128)}, f32[192,32]{1,0:T(8,128)S(1)}, u32[]{:S(2)}) copy-start(f32[192,32]{1,0:T(8,128)S(1)} %get-tuple-element.138) | copy-start | bytes 73732
  283.6 24.9 %slice-start.6 = ((s8[6291456]{0:T(1024)(128)(4,1)}), s8[4194304]{0:T(1024)(128)(4,1)S(1)}, s32[]{:S(2)}) async-start(s8[6291456]{0:T(1024)(128)(4,1)} %bitcast.142), calls=%async_computation.6 | async-start | bytes 8388608
  283.7 24.9 %slice-start.7 = ((s8[6291456]{0:T(1024)(128)(4,1)}), s8[2097152]{0:T(1024)(128)(4,1)S(1)}, s32[]{:S(2)}) async-start(s8[6291456]{0:T(1024)(128)(4,1)} %bitcast.142), calls=%async_computation.7 | async-start | bytes 4194304
  308.6 24.8 %slice-start.2 = ((s8[6291456]{0:T(1024)(128)(4,1)}), s8[2097152]{0:T(1024)(128)(4,1)S(1)}, s32[]{:S(2)}) async-start(s8[6291456]{0:T(1024)(128)(4,1)} %bitcast.133), calls=%async_computation.2 | async-start | bytes 4194304
  312.6 11.6 %copy-start.51 = (bf16[16,128,1024]{2,1,0:T(8,128)(2,1)S(1)}, bf16[16,128,1024]{2,1,0:T(8,128)(2,1)}, u32[]{:S(2)}) copy-start(bf16[16,128,1024]{2,1,0:T(8,128)(2,1)} %get-tuple-element.53) | copy-start | bytes 12582916
  312.6 20.7 %slice-start.3 = ((s8[6291456]{0:T(1024)(128)(4,1)}), s8[4194304]{0:T(1024)(128)(4,1)S(1)}, s32[]{:S(2)}) async-start(s8[6291456]{0:T(1024)(128)(4,1)} %bitcast.133), calls=%async_computation.3 | async-start | bytes 8388608
  324.1 9.2 %copy-start.43 = (f32[1,2048]{1,0:T(1,128)S(1)}, f32[1,2048]{1,0:T(1,128)}, u32[]{:S(2)}) copy-start(f32[1,2048]{1,0:T(1,128)} %get-tuple-element.125) | copy-start | bytes 24580
  324.1 9.2 %copy-start.45 = (pred[1536]{0:T(1024)(128)(4,1)S(1)}, pred[1536]{0:T(1024)(128)(4,1)}, u32[]{:S(2)}) copy-start(pred[1536]{0:T(1024)(128)(4,1)} %copy-done.44) | copy-start | bytes 4612
  324.1 9.2 %copy-start.46 = (pred[2048]{0:T(1024)(128)(4,1)S(1)}, pred[2048]{0:T(1024)(128)(4,1)}, u32[]{:S(2)}) copy-start(pred[2048]{0:T(1024)(128)(4,1)} %fusion.58) | copy-start | bytes 6148
  324.2 9.2 %copy-start.55 = (bf16[16,128,256]{2,1,0:T(8,128)(2,1)S(1)}, bf16[16,128,256]{2,1,0:T(8,128)(2,1)}, u32[]{:S(2)}) copy-start(bf16[16,128,256]{2,1,0:T(8,128)(2,1)} %get-tuple-element.51) | copy-start | bytes 3145732
  324.2 9.2 %copy-start.56 = (bf16[8,192,256]{2,1,0:T(8,128)(2,1)S(1)}, bf16[8,192,256]{2,1,0:T(8,128)(2,1)}, u32[]{:S(2)}) copy-start(bf16[8,192,256]{2,1,0:T(8,128)(2,1)} %convolution_convert_fusion.6) | copy-start | bytes 2359300
  333.4 8.5 %copy-start.53 = (bf16[16,128,768]{2,1,0:T(8,128)(2,1)S(1)}, bf16[16,128,768]{2,1,0:T(8,128)(2,1)}, u32[]{:S(2)}) copy-start(bf16[16,128,768]{2,1,0:T(8,128)(2,1)} %get-tuple-element.50) | copy-start | bytes 9437188
  341.9 8.2 %copy-start.33 = (f32[1,2048]{1,0:T(1,128)S(1)}, f32[1,2048]{1,0:T(1,128)}, u32[]{:S(2)}) copy-start(f32[1,2048]{1,0:T(1,128)} %copy-done.32) | copy-start | bytes 24580
  341.9 8.2 %copy-start.35 = (f32[1,2048]{1,0:T(1,128)S(1)}, f32[1,2048]{1,0:T(1,128)}, u32[]{:S(2)}) copy-start(f32[1,2048]{1,0:T(1,128)} %copy-done.34) | copy-start | bytes 24580
  372.7 9.9 %copy-start.58 = (bf16[1536,2048]{1,0:T(8,128)(2,1)S(1)}, bf16[1536,2048]{1,0:T(8,128)(2,1)}, u32[]{:S(2)}) copy-start(bf16[1536,2048]{1,0:T(8,128)(2,1)} %get-tuple-element.103) | copy-start | bytes 18874372
  372.7 9.9 %copy-start.59 = (bf16[1536,1024]{1,0:T(8,128)(2,1)S(1)}, bf16[1536,1024]{1,0:T(8,128)(2,1)}, u32[]{:S(2)}) copy-start(bf16[1536,1024]{1,0:T(8,128)(2,1)} %get-tuple-element.98) | copy-start | bytes 9437188
  391.1 238.7 %copy-start.2 = (bf16[2,192,2048]{2,1,0:T(8,128)(2,1)S(1)}, bf16[2,192,2048]{2,1,0:T(8,128)(2,1)}, u32[]{:S(2)}) copy-start(bf16[2,192,2048]{2,1,0:T(8,128)(2,1)} %refs_4_.1) | copy-start | bytes 4718596
  391.1 238.7 %copy-start.31 = (f32[2,192]{1,0:T(2,128)S(1)}, f32[2,192]{1,0:T(2,128)}, u32[]{:S(2)}) copy-start(f32[2,192]{1,0:T(2,128)} %copy-done.30) | copy-start | bytes 4612
  391.1 238.7 %copy-start.38 = (f32[2,192]{1,0:T(2,128)S(1)}, f32[2,192]{1,0:T(2,128)}, u32[]{:S(2)}) copy-start(f32[2,192]{1,0:T(2,128)} %add_rsqrt_fusion.1) | copy-start | bytes 4612
  391.1 241.4 %copy-start.47 = (pred[2,192]{1,0:T(4,128)(4,1)S(1)}, pred[2,192]{1,0:T(4,128)(4,1)}, u32[]{:S(2)}) copy-start(pred[2,192]{1,0:T(4,128)(4,1)} %iota_compare_fusion.4) | copy-start | bytes 1156
  635.4 48.3 %copy-start.17 = (f32[128,1024]{1,0:T(8,128)}, f32[128,1024]{1,0:T(8,128)S(1)}, u32[]{:S(2)}) copy-start(f32[128,1024]{1,0:T(8,128)S(1)} %get-tuple-element.175) | copy-start | bytes 1572868
  635.4 34.0 %copy-start.40 = (f32[4,128]{1,0:T(4,128)S(1)}, f32[4,128]{1,0:T(4,128)}, u32[]{:S(2)}) copy-start(f32[4,128]{1,0:T(4,128)} %param.28) | copy-start | bytes 6148
  636.8 46.8 %copy-start.16 = (f32[128,1024]{1,0:T(8,128)S(1)}, f32[128,1024]{1,0:T(8,128)}, u32[]{:S(2)}) copy-start(f32[128,1024]{1,0:T(8,128)} %param.23) | copy-start | bytes 1572868
  640.4 46.2 %copy-start.7 = (f32[128,4096]{1,0:T(8,128)}, f32[128,4096]{1,0:T(8,128)S(1)}, u32[]{:S(2)}) copy-start(f32[128,4096]{1,0:T(8,128)S(1)} %get-tuple-element.176) | copy-start | bytes 6291460
  (36 other events, 150.5 us)

commit v2 on v1

v2 whole, which is shorter than its diff:
```python
from functools import partial
import math

import jax
import jax.numpy as jnp
from jax import lax
from jax.experimental import pallas as pl
from jax.experimental.pallas import tpu as pltpu
from jax.sharding import PartitionSpec as P

D = 2048
FF = 8192
HEADS = 8
LINE = 4

eps_norm = 1e-05
eps_second = 1e-30
decay = 0.5
rate_scale = 1.0
rate_norm = 0.5
rate_vector = 0.05
neg_large = -1e30

MESH = pl.DeviceIdType.MESH
ANY = pl.BlockSpec(memory_space=pl.ANY)
VMEM = pl.BlockSpec(memory_space=pltpu.VMEM)
SMEM = pl.BlockSpec(memory_space=pltpu.SMEM)


def turn_tables(slot_len, rot_dims, width):
    half = rot_dims // 2
    freq = 10000.0 ** (-2.0 * jnp.arange(half, dtype=jnp.float32) / rot_dims)
    angle = jnp.arange(slot_len, dtype=jnp.float32)[:, None] * freq[None, :]
    cosine, sine = jnp.cos(angle), jnp.sin(angle)
    none = jnp.zeros((slot_len, half), jnp.float32)
    rest = jnp.zeros((slot_len, width - rot_dims), jnp.float32)
    return jnp.stack(
        [
            jnp.concatenate([cosine, cosine, rest + 1.0], 1),
            jnp.concatenate([sine, none, rest], 1),
            jnp.concatenate([none, sine, rest], 1),
        ]
    )


class Place:
    def __init__(self, groups):
        self.groups = groups
        data = lax.axis_index("dp")
        self.core = lax.axis_index("tensor")
        self.other = 1 - self.core
        self.line = data // groups
        self.group = data % groups

    def at(self, line, group, core):
        return (line * self.groups + group, core)

    def line_to(self, step):
        return (self.line + step) % LINE

    def line_from(self, step):
        return (self.line + LINE - step) % LINE

    def group_to(self, step):
        g = self.group
        if self.groups == 4:
            if step == 1:
                return g + 1 - 2 * (g % 2)
            if step == 2:
                return (g + 2) % 4
            return 3 - g
        return (g + step) % self.groups

    def group_from(self, step):
        if self.groups == 4:
            return self.group_to(step)
        return (self.group + self.groups - step) % self.groups

    def greet(self):
        barrier = pltpu.get_barrier_semaphore()
        count = 0
        for step in range(1, LINE):
            for core in (self.core, self.other):
                pl.semaphore_signal(
                    barrier, inc=1, device_id=self.at(self.line_to(step), self.group, core), device_id_type=MESH
                )
                count += 1
        for step in range(1, self.groups):
            pl.semaphore_signal(
                barrier, inc=1, device_id=self.at(self.line, self.group_to(step), self.core), device_id_type=MESH
            )
            count += 1
        pl.semaphore_signal(
            barrier, inc=1, device_id=self.at(self.line, self.group, self.other), device_id_type=MESH
        )
        pl.semaphore_wait(barrier, count + 1)


def remote(src, dst, send, recv, device):
    return pltpu.make_async_remote_copy(
        src_ref=src, dst_ref=dst, send_sem=send, recv_sem=recv, device_id=device, device_id_type=MESH
    )


def dot(left, right):
    return jnp.dot(left, right, preferred_element_type=jnp.float32)


def gather_kernel(groups, cols, seq_dev, slot_len, *refs):
    count = len(cols)
    f32, low = jnp.float32, jnp.bfloat16
    w_in = refs[:count]
    acts_in = refs[count : count + 2]
    vec_ref, bias_ref, valid_ref, turn_ref = refs[count + 2 : count + 6]
    outs = refs[count + 6 : count + 16]
    n1_out, n2_out, back_out, qg_out, pg_out, attn_out, hid_out, m_out, s_out, early_ref = outs
    rest = refs[count + 16 :]
    w_out = rest[:count]
    acts_out = rest[count : count + 2]
    (qkv_keep, prob_keep, attn_keep, hid_keep, pg_keep, one_buf, two_buf, back_buf, m_buf, m_got, s_got, qkv_now,
     pre_now, stat_keep, norm_acc, bias_acc) = rest[count + 2 : count + 18]
    (one_s, one_r, two_s, two_r, three_s, three_r, up_s, up_r, down_s, down_r, sib_s, sib_r, here, out_a, out_b,
     out_c, out_d, msib_s, msib_r, ssib_s, ssib_r, mline_s, mline_r, s_here) = rest[count + 18 :]
    me = Place(groups)
    c, g, k = me.line, me.group, me.core
    me.greet()
    sibling = me.at(c, g, me.other)
    rows_own = w_in[0].shape[0]
    block_rows = seq_dev * slot_len
    near = groups == 4
    START, SENT = "start", "wait_send"

    def block(ref, line, width):
        return ref.at[:, pl.ds(pl.multiple_of(line * width, 128), width)]

    def place(m, line, group):
        return w_out[m].at[pl.ds(pl.multiple_of((line * groups + group) * rows_own, 32), rows_own)]

    def rows_of(which, line, core):
        return acts_out[which].at[pl.ds(pl.multiple_of((line * seq_dev + core) * slot_len, 32), slot_len)]

    def hop_up(which, hop, act):
        origin = c - (hop - 1)
        copy = remote(
            acts_in[which].at[k] if hop == 1 else rows_of(which, origin, k),
            rows_of(which, origin, k),
            up_s.at[which, hop - 1],
            up_r.at[which, hop - 1],
            me.at(c + 1, g, k),
        )
        pl.when((c < LINE - 1) & (origin >= 0))(getattr(copy, act))

    def hop_down(which, hop, act):
        origin = c + (hop - 1)
        copy = remote(
            acts_in[which].at[k] if hop == 1 else rows_of(which, origin, k),
            rows_of(which, origin, k),
            down_s.at[which, hop - 1],
            down_r.at[which, hop - 1],
            me.at(c - 1, g, k),
        )
        pl.when((c > 0) & (origin < LINE))(getattr(copy, act))

    def from_way(way, hop):
        origin = c - hop if way == 0 else c + hop
        return origin, (origin >= 0) if way == 0 else (origin < LINE)

    def to_sibling(which, way, hop, act):
        origin, ok = from_way(way, hop)
        rows = rows_of(which, origin, k)
        copy = remote(rows, rows, sib_s.at[which, way, hop - 1], sib_r.at[which, way, hop - 1], sibling)
        pl.when(ok)(getattr(copy, act))

    def arrive(which, way, hop):
        origin, ok = from_way(way, hop)
        sem = (up_r if way == 0 else down_r).at[which, hop - 1]
        rows = rows_of(which, origin, k)
        pl.when(ok)(remote(rows, rows, sem, sem, sibling).wait_recv)

    def arrive_sibling(which):
        for hop in range(1, LINE):
            for way in range(2):
                origin, ok = from_way(way, hop)
                sem = sib_r.at[which, way, hop - 1]
                rows = rows_of(which, origin, me.other)
                pl.when(ok)(remote(rows, rows, sem, sem, sibling).wait_recv)

    def pass_on(which, hop):
        for way in range(2):
            arrive(which, way, hop)
            if hop < LINE - 1:
                (hop_up if way == 0 else hop_down)(which, hop + 1, START)
            to_sibling(which, way, hop, START)

    def local_acts(which, act):
        for s in range(seq_dev):
            copy = pltpu.make_async_copy(acts_in[which].at[s], rows_of(which, c, s), here.at[count + which, s])
            getattr(copy, act)()

    def local_weight(m, act):
        copy = pltpu.make_async_copy(block(w_in[m], c, cols[m]), place(m, c, g), here.at[m, 0])
        getattr(copy, act)()

    def stage_one(m, act):
        for step in range(1, LINE):
            to = me.line_to(step)
            copy = remote(
                block(w_in[m], to, cols[m]),
                place(m, c, g),
                one_s.at[m, step],
                one_r.at[m, step],
                me.at(to, g, k),
            )
            getattr(copy, act)()

    def stage_two(m, step, act):
        where = place(m, me.line_from(step), g)
        src = block(w_in[m], c, cols[m]) if step == 0 else where
        for peer in range(1, 3 if near else groups):
            copy = remote(
                src, where, two_s.at[m, step, peer], two_r.at[m, step, peer], me.at(c, me.group_to(peer), k)
            )
            getattr(copy, act)()

    def first_half(m):
        for step in range(1, LINE):
            dst = place(m, me.line_from(step), g)
            remote(dst, dst, one_s.at[m, step], one_r.at[m, step], sibling).wait_recv()
            stage_two(m, step, START)

    def wait_two(m, step, peer):
        dst = place(m, me.line_from(step), me.group_from(peer))
        remote(dst, dst, two_s.at[m, step, peer], two_r.at[m, step, peer], sibling).wait_recv()

    def stage_three(m, step, act):
        source, target = (1, 2) if step % 2 == 0 else (2, 1)
        where = place(m, me.line_from(step), me.group_to(source))
        copy = remote(where, where, three_s.at[m, step], three_r.at[m, step], me.at(c, me.group_to(target), k))
        getattr(copy, act)()

    def relay(m):
        for step in range(LINE):
            for peer in range(1, 3 if near else groups):
                wait_two(m, step, peer)
            if near:
                stage_three(m, step, START)

    def last(m):
        if near:
            for step in range(LINE):
                dst = place(m, me.line_from(step), me.group_to(3))
                remote(dst, dst, three_s.at[m, step], three_r.at[m, step], sibling).wait_recv()

    hop_up(0, 1, START)
    hop_down(0, 1, START)
    for m in (0, 1):
        stage_one(m, START)
        stage_two(m, 0, START)
    local_acts(0, START)
    local_weight(0, START)
    local_weight(1, START)
    norm_acc[...] = jnp.zeros_like(norm_acc)
    bias_acc[...] = jnp.zeros_like(bias_acc)
    first_half(0)
    pass_on(0, 1)
    hop_up(1, 1, START)
    hop_down(1, 1, START)
    for m in (2, 3):
        stage_one(m, START)
        stage_two(m, 0, START)
    local_acts(1, START)
    local_weight(2, START)
    local_weight(3, START)
    first_half(1)
    relay(0)
    pass_on(0, 2)
    relay(1)
    pass_on(0, 3)
    local_acts(0, "wait")
    local_weight(0, "wait")
    local_weight(1, "wait")
    last(0)
    last(1)
    arrive_sibling(0)

    wq, w1, wd, w2 = w_out
    x_all, ct_all = acts_out
    head = cols[0] // 3
    half = head // 2
    chunk = 16
    wide = 512
    ways = D // wide
    root = math.sqrt(head)
    causal = lax.broadcasted_iota(jnp.int32, (slot_len, slot_len), 0) >= lax.broadcasted_iota(
        jnp.int32, (slot_len, slot_len), 1
    )

    def turn(v, sign):
        left = pltpu.roll(v, half - 32, 1)
        right = pltpu.roll(v, 32, 1)
        if sign > 0:
            return v * turn_ref[0] - left * turn_ref[1] + right * turn_ref[2]
        return v * turn_ref[0] + left * turn_ref[1] - right * turn_ref[2]

    def contract(left, right, dims):
        return lax.dot_general(left, right, ((dims[0], dims[1]), ((), ())), preferred_element_type=f32)

    def put_one(i, line, act):
        rows = pl.ds(pl.multiple_of(line * block_rows, 128), block_rows)
        getattr(pltpu.make_async_copy(one_buf, n1_out.at[rows], out_a), act)()
        getattr(pltpu.make_async_copy(two_buf.at[0], n2_out.at[rows], out_b.at[0]), act)()

    @pl.loop(0, LINE)
    def forward(i):
        line = (c + i) % LINE
        base = pl.multiple_of(line * block_rows, 128)

        @pl.when(i == 0)
        def _():
            first_half(2)
            first_half(3)

        @pl.when(i == 1)
        def _():
            pass_on(1, 1)
            relay(2)

        @pl.when(i == 2)
        def _():
            pass_on(1, 2)
            relay(3)

        @pl.when(i == 3)
        def _():
            pass_on(1, 3)

        @pl.when(i >= 1)
        def _():
            put_one(i, line, "wait")

        @pl.loop(0, block_rows // chunk)
        def norm(j):
            at = pl.ds(pl.multiple_of(base + j * chunk, chunk), chunk)
            to = pl.ds(pl.multiple_of(j * chunk, chunk), chunk)
            x = x_all[at, :].astype(f32)
            mean = jnp.mean(x, -1, keepdims=True)
            centre = x - mean
            scale = lax.rsqrt(jnp.mean(centre * centre, -1, keepdims=True) + eps_norm)
            stat_keep[at, 0:1] = mean
            stat_keep[at, 1:2] = scale
            unit = centre * scale
            one_buf[to, :] = (unit * vec_ref[0:1, :] + vec_ref[1:2, :]).astype(low)
            two_buf[0, to, :] = (unit * vec_ref[2:3, :] + vec_ref[3:4, :]).astype(low)

        put_one(i, line, "start")
        qkv_now[...] = dot(one_buf[...], wq[...]) + bias_ref[0:1, : cols[0]]
        pre_now[...] = dot(two_buf[0], w1[...]) + bias_ref[0:1, cols[0] :]

        for s in range(seq_dev):
            part = slice(s * slot_len, (s + 1) * slot_len)
            rows = pl.ds(pl.multiple_of(base + s * slot_len, 32), slot_len)
            qkv_keep[rows, 0:half] = turn(qkv_now[part, 0:half], 1).astype(low)
            qkv_keep[rows, half:head] = qkv_now[part, half:head].astype(low)
            qkv_keep[rows, head : head + half] = turn(qkv_now[part, head : head + half], 1).astype(low)
            qkv_keep[rows, head + half :] = qkv_now[part, head + half :].astype(low)
            query = qkv_keep[rows, :head]
            keys = qkv_keep[rows, head : 2 * head]
            values = qkv_keep[rows, 2 * head :]
            scores = jnp.where(causal, contract(query, keys, ((1,), (1,))) / root, neg_large)
            expo = jnp.exp(scores - jnp.max(scores, -1, keepdims=True))
            probs = expo / jnp.sum(expo, -1, keepdims=True)
            prob_keep[line * seq_dev + s] = probs
            attn_keep[rows, :] = dot(probs.astype(low), values).astype(low)

        @pl.loop(0, block_rows // chunk)
        def act(j):
            at = pl.ds(pl.multiple_of(base + j * chunk, chunk), chunk)
            pre = pre_now[pl.ds(pl.multiple_of(j * chunk, chunk), chunk), :]
            area = 0.5 * (1.0 + lax.erf(pre * math.sqrt(0.5)))
            hid_keep[at, :] = (pre * area).astype(low)
            pg_keep[at, :] = (area + pre * (jnp.exp(-0.5 * pre * pre) * (1.0 / math.sqrt(2.0 * math.pi)))).astype(low)

    put_one(LINE - 1, (c + LINE - 1) % LINE, "wait")
    local_acts(1, "wait")
    local_weight(2, "wait")
    local_weight(3, "wait")
    last(2)
    last(3)
    arrive_sibling(1)

    def put_back(line, act):
        rows = pl.ds(pl.multiple_of(line * block_rows, 128), block_rows)
        getattr(pltpu.make_async_copy(back_buf, back_out.at[rows], out_c), act)()

    def pair_m(i, act):
        line = (c + i) % LINE
        copy = remote(m_buf.at[i % 2, me.other], m_got.at[line], msib_s.at[i], msib_r.at[i], sibling)
        getattr(copy, act)()

    def line_m(i, act):
        line = (c + i) % LINE
        for step in range(1, LINE):
            to = me.line_to(step)
            copy = remote(
                m_buf.at[i % 2, k, to], m_out.at[c, line], mline_s.at[i, step], mline_r.at[i, step], me.at(to, g, k)
            )
            getattr(copy, act)()
        copy = pltpu.make_async_copy(m_buf.at[i % 2, k, c], m_out.at[c, line], mline_s.at[i, 0])
        getattr(copy, "wait" if act == SENT else act)()

    def pair_s(i, act):
        line = (c + i) % LINE
        rows = pl.ds(pl.multiple_of(me.other * slot_len, 32), slot_len)
        copy = remote(two_buf.at[i % 2, rows], s_got.at[line], ssib_s.at[i], ssib_r.at[i], sibling)
        getattr(copy, act)()

    def put_s(i, act):
        line = (c + i) % LINE
        rows = pl.ds(pl.multiple_of(k * slot_len, 32), slot_len)
        getattr(pltpu.make_async_copy(two_buf.at[i % 2, rows], s_out.at[line], s_here.at[i]), act)()

    def finish_s(i):
        line = (c + i) % LINE
        pair_s(i, "wait_recv")

        @pl.loop(0, slot_len // chunk)
        def add(j):
            at = pl.ds(pl.multiple_of(k * slot_len + j * chunk, chunk), chunk)
            to = pl.ds(pl.multiple_of(j * chunk, chunk), chunk)
            total = two_buf[i % 2, at, :].astype(f32) + s_got[line, to, :].astype(f32)
            two_buf[i % 2, at, :] = total.astype(low)

        put_s(i, START)

    def put_rest(line, act):
        rows = pl.ds(pl.multiple_of(line * block_rows, 128), block_rows)
        for place_at, (buf, out) in enumerate(
            ((qkv_keep, qg_out), (pg_keep, pg_out), (attn_keep, attn_out), (hid_keep, hid_out))
        ):
            getattr(pltpu.make_async_copy(buf.at[rows], out.at[rows], out_d.at[place_at, line]), act)()

    mine = c * 2 + k

    @pl.loop(0, LINE)
    def backward(i):
        line = (c + i) % LINE
        base = pl.multiple_of(line * block_rows, 128)
        whole = pl.ds(base, block_rows)
        slot = i % 2

        @pl.when(i >= 2)
        def _():
            line_m(i - 2, SENT)

        live = valid_ref[whole, :]

        @pl.loop(0, ways)
        def output(j):
            at = pl.ds(pl.multiple_of(j * wide, 128), wide)
            total = contract(attn_keep[whole, :], wd[at, :], ((1,), (1,)))
            total = total + contract(hid_keep[whole, :], w2[at, :], ((1,), (1,)))
            feature = (lax.broadcasted_iota(jnp.int32, (1, wide), 1) + j * wide) // (D // (2 * LINE))
            mask = jnp.where(feature == mine, 1.0, 0.0)
            extra = x_all[whole, at].astype(f32) + (vec_ref[4:5, at] + vec_ref[5:6, at])
            total = ((total + mask * extra) * live).astype(low)
            m_buf[slot, 0, j] = total[:, : wide // 2]
            m_buf[slot, 1, j] = total[:, wide // 2 :]

        pair_m(i, START)

        @pl.when(i >= 1)
        def _():
            put_back(line, "wait")

        back_buf[...] = (ct_all[whole, :].astype(f32) * live).astype(low)
        put_back(line, "start")
        attn_grad = dot(back_buf[...], wd[...]).astype(low)
        pre_now[...] = dot(back_buf[...], w2[...])

        @pl.when(i == 0)
        def _():
            rows = pl.ds(pl.multiple_of(k * slot_len, 32), slot_len)
            total = jnp.sum(back_buf[rows, :].astype(f32).reshape(slot_len // 8, 8, D), 0)
            norm_acc[4] = total

        @pl.loop(0, block_rows // chunk)
        def act(j):
            at = pl.ds(pl.multiple_of(base + j * chunk, chunk), chunk)
            grad = pre_now[pl.ds(pl.multiple_of(j * chunk, chunk), chunk), :] * pg_keep[at, :].astype(f32)
            grad = grad.astype(low)
            pg_keep[at, :] = grad
            grad = grad.astype(f32)
            bias_acc[:, cols[0] :] += grad[:8] + grad[8:]

        for s in range(seq_dev):
            rows = pl.ds(pl.multiple_of(base + s * slot_len, 32), slot_len)
            grad = attn_grad[s * slot_len : (s + 1) * slot_len]
            query = qkv_keep[rows, :head]
            keys = qkv_keep[rows, head : 2 * head]
            values = qkv_keep[rows, 2 * head :]
            probs = prob_keep[line * seq_dev + s]
            prob_grad = contract(grad, values, ((1,), (1,)))
            row_dot = jnp.sum(probs * prob_grad, -1, keepdims=True)
            score_grad = (probs * (prob_grad - row_dot)).astype(low)
            value_grad = contract(probs.astype(low), grad, ((0,), (0,)))
            query_grad = dot(score_grad, keys) / root
            key_grad = contract(score_grad, query, ((0,), (0,))) / root
            qkv_keep[rows, 0:half] = turn(query_grad[:, :half], -1).astype(low)
            qkv_keep[rows, half:head] = query_grad[:, half:].astype(low)
            qkv_keep[rows, head : head + half] = turn(key_grad[:, :half], -1).astype(low)
            qkv_keep[rows, head + half : 2 * head] = key_grad[:, half:].astype(low)
            qkv_keep[rows, 2 * head :] = value_grad.astype(low)
            summed = qkv_keep[rows, :].astype(f32).reshape(slot_len // 8, 8, cols[0])
            bias_acc[:, : cols[0]] += jnp.sum(summed, 0)

        put_rest(line, "start")
        mean = stat_keep[whole, 0:1]
        scale = stat_keep[whole, 1:2]

        @pl.when(i >= 2)
        def _():
            pair_s(i - 2, SENT)
            put_s(i - 2, "wait")

        @pl.loop(0, ways)
        def inputs(j):
            at = pl.ds(pl.multiple_of(j * wide, 128), wide)
            first = contract(qkv_keep[whole, :], wq[at, :], ((1,), (1,)))
            second = contract(pg_keep[whole, :], w1[at, :], ((1,), (1,)))
            two_buf[slot, :, at] = (first * vec_ref[0:1, at] + second * vec_ref[2:3, at]).astype(low)
            unit = (x_all[whole, at].astype(f32) - mean) * scale
            for place_at, value in enumerate((first * unit, first, second * unit, second)):
                norm_acc[place_at, :, at] += jnp.sum(value.reshape(block_rows // 8, 8, wide), 0)

        pair_s(i, START)
        pair_m(i, "wait_recv")

        @pl.loop(0, LINE)
        def add_outer(p):
            @pl.loop(0, block_rows // 64)
            def add(j):
                at = pl.ds(pl.multiple_of(j * 64, 64), 64)
                total = m_buf[slot, k, p, at, :].astype(f32) + m_got[line, p, at, :].astype(f32)
                m_buf[slot, k, p, at, :] = total.astype(low)

        line_m(i, START)
        pair_m(i, SENT)

        @pl.when(i >= 1)
        def _():
            finish_s(i - 1)

    finish_s(LINE - 1)
    for r in range(5):
        total = jnp.sum(norm_acc[r], 0, keepdims=True)
        for t in range(D // 128):
            early_ref[r * (D // 128) + t : r * (D // 128) + t + 1, :] = total[:, t * 128 : (t + 1) * 128]
    at_bias = 5 * (D // 128)
    total = jnp.sum(bias_acc[...], 0, keepdims=True)
    for t in range((cols[0] + cols[1]) // 128):
        early_ref[at_bias + t : at_bias + t + 1, :] = total[:, t * 128 : (t + 1) * 128]
    at_row = at_bias + (cols[0] + cols[1]) // 128
    early_ref[at_row : at_row + 1, :] = vec_ref[6:7, :128]
    early_ref[at_row + 1 :, :] = jnp.zeros((early_ref.shape[0] - at_row - 1, 128), f32)
    put_back(0, "wait")
    for i in range(LINE):
        put_rest(i, "wait")
    for i in (LINE - 2, LINE - 1):
        line_m(i, SENT)
        pair_s(i, SENT)
        put_s(i, "wait")
    for step in range(1, LINE):
        source = me.line_from(step)
        for i in range(LINE):
            dst = m_out.at[source, (source + i) % LINE]
            remote(dst, dst, mline_s.at[i, step], mline_r.at[i, step], sibling).wait_recv()
    for m in range(count):
        stage_one(m, SENT)
        for step in range(LINE):
            stage_two(m, step, SENT)
            if near:
                stage_three(m, step, SENT)
    for which in range(2):
        for hop in range(1, LINE):
            hop_up(which, hop, SENT)
            hop_down(which, hop, SENT)
            for way in range(2):
                to_sibling(which, way, hop, SENT)


def gather_all(groups, weights, tokens, cotangent, vectors, biases, valid, turns):
    rows_own = weights[0].shape[0]
    seq_dev, slot_len, width = tokens.shape
    cols = tuple(w.shape[1] // LINE for w in weights)
    count = len(weights)
    block_rows = seq_dev * slot_len
    rows = LINE * block_rows
    f32, low = jnp.float32, jnp.bfloat16
    dma = pltpu.SemaphoreType.DMA
    peers = 3 if groups == 4 else groups
    out_widths = (D, D, D, cols[0], cols[1], cols[2], cols[3])
    feat = D // (2 * LINE)
    early_rows = -(-(5 * D + cols[0] + cols[1] + 128) // 1024) * 8
    return pl.pallas_call(
        partial(gather_kernel, groups, cols, seq_dev, slot_len),
        out_shape=[jax.ShapeDtypeStruct((rows, w), low) for w in out_widths]
        + [
            jax.ShapeDtypeStruct((LINE, LINE, block_rows, feat), low),
            jax.ShapeDtypeStruct((LINE, slot_len, D), low),
            jax.ShapeDtypeStruct((early_rows, 128), f32),
        ],
        in_specs=[ANY] * (count + 2) + [VMEM] * 4,
        out_specs=[ANY] * 9 + [VMEM],
        scratch_shapes=[pltpu.VMEM((D, w), low) for w in cols]
        + [pltpu.VMEM((rows, D), low)] * 2
        + [
            pltpu.VMEM((rows, cols[0]), low),
            pltpu.VMEM((LINE * seq_dev, slot_len, slot_len), f32),
            pltpu.VMEM((rows, cols[2]), low),
            pltpu.VMEM((rows, cols[3]), low),
            pltpu.VMEM((rows, cols[1]), low),
            pltpu.VMEM((block_rows, D), low),
            pltpu.VMEM((2, block_rows, D), low),
            pltpu.VMEM((block_rows, D), low),
            pltpu.VMEM((2, 2, LINE, block_rows, feat), low),
            pltpu.VMEM((LINE, LINE, block_rows, feat), low),
            pltpu.VMEM((LINE, slot_len, D), low),
            pltpu.VMEM((block_rows, cols[0]), f32),
            pltpu.VMEM((block_rows, cols[1]), f32),
            pltpu.VMEM((rows, 2), f32),
            pltpu.VMEM((5, 8, D), f32),
            pltpu.VMEM((8, cols[0] + cols[1]), f32),
            dma((count, LINE)),
            dma((count, LINE)),
            dma((count, LINE, peers)),
            dma((count, LINE, peers)),
            dma((count, LINE)),
            dma((count, LINE)),
            dma((2, LINE)),
            dma((2, LINE)),
            dma((2, LINE)),
            dma((2, LINE)),
            dma((2, 2, LINE)),
            dma((2, 2, LINE)),
            dma((count + 2, seq_dev)),
            dma(()),
            dma((2,)),
            dma(()),
            dma((4, LINE)),
            dma((LINE,)),
            dma((LINE,)),
            dma((LINE,)),
            dma((LINE,)),
            dma((LINE, LINE)),
            dma((LINE, LINE)),
            dma((LINE,)),
        ],
        compiler_params=pltpu.CompilerParams(
            collective_id=0, has_side_effects=True, vmem_limit_bytes=62 * 1024 * 1024
        ),
        name="gather_all",
    )(*weights, tokens, cotangent, vectors, biases, valid, turns)


def scatter_kernel(groups, cols, seq_dev, slot_len, rows_own, *refs):
    count = len(cols)
    f32, low = jnp.float32, jnp.bfloat16
    pick, m_ref, s_ref = refs[:3]
    lefts_in = refs[3:6]
    rights_in = refs[6 : 6 + count]
    early_ref = refs[6 + count]
    mixed_ref, ssum_ref = refs[7 + count : 9 + count]
    g_out = refs[9 + count : 9 + 2 * count]
    early_out, col_out, row_out = refs[9 + 2 * count : 12 + 2 * count]
    rest = refs[12 + 2 * count :]
    left_buf, right_a, right_b, right_c = rest[:4]
    g_own = rest[4 : 4 + count]
    g_got = rest[4 + count : 4 + 2 * count]
    (m_in, m_all, m_send, s_own, s_line, early_group, col_now, col_group, row_keep, row_turn) = rest[
        4 + 2 * count : 14 + 2 * count
    ]
    (here, sline_s, sline_r, fin_s, fin_r, mall_s, mall_r, mout_s, mout_r, gp_s, gp_r, gl_s, gl_r, eg_s, eg_r, el_s,
     el_r, es_s, es_r, cg_s, cg_r, cl_s, cl_r, cs_s, cs_r, rl_s, rl_r, keep_sem) = rest[14 + 2 * count :]
    me = Place(groups)
    c, g, k = me.line, me.group, me.core
    me.greet()
    sibling = me.at(c, g, me.other)
    feat = D // (2 * LINE)
    seqs = LINE * seq_dev
    rows = seqs * slot_len
    double = groups == 4
    sends = []

    def go(copy):
        copy.start()
        sends.append(copy)

    def to_group(step):
        return (g + step) % groups

    def from_group(step):
        return (g + groups - step) % groups

    def arrived(dst, send, recv):
        remote(dst, dst, send, recv, sibling).wait_recv()

    def add_rows(total, parts, count_rows, chunk):
        @pl.loop(0, count_rows // chunk)
        def body(i):
            at = pl.ds(pl.multiple_of(i * chunk, chunk), chunk)
            acc = parts[0](at)[...].astype(f32)
            for part in parts[1:]:
                acc = acc + part(at)[...].astype(f32)
            total(at)[...] = acc.astype(low)

    def load(src, dst, sem):
        copy = pltpu.make_async_copy(src, dst, sem)
        copy.start()
        return copy

    got_m = load(m_ref, m_in, here.at[0])
    got_back = load(lefts_in[2], left_buf.at[0], here.at[1])
    got_d = load(rights_in[2], right_c, here.at[2])
    got_2 = load(rights_in[3], right_a, here.at[3])
    for step in range(1, LINE):
        line = me.line_to(step)
        go(remote(s_ref.at[line], s_line.at[step - 1], sline_s.at[step], sline_r.at[step], me.at(line, g, k)))
    got_s = load(s_ref.at[c], s_own, here.at[4])
    for step in range(1, groups):
        go(remote(early_ref, early_group.at[g], eg_s.at[step], eg_r.at[step], me.at(c, to_group(step), k)))
    early_group[g] = early_ref[...]
    if double:
        got_one = load(lefts_in[0], left_buf.at[1], here.at[5])
        got_q = load(rights_in[0], right_b, here.at[6])

    got_m.wait()
    ours = pl.ds(g * seqs, seqs)
    for s in range(seqs):
        line, part = s // seq_dev, s % seq_dev
        add_rows(
            lambda at: m_all.at[g * seqs + s, at],
            [partial(lambda p, at: m_in.at[p, s, at], p) for p in range(LINE)],
            slot_len,
            64,
        )
    for step in range(1, groups):
        go(remote(m_all.at[ours], m_all.at[ours], mall_s.at[step], mall_r.at[step], me.at(c, to_group(step), k)))

    per = 128 // rows_own

    def tile_products(m, left, right, tiles):
        lhs = jnp.concatenate(
            [left[:, pl.ds(pl.multiple_of((l * groups + p) * rows_own, 128), 128)] for l, p in tiles], 1
        )
        wide = 256 if cols[m] % 512 else 512
        for n in range(cols[m] // wide):
            at = slice(n * wide, (n + 1) * wide)
            out = lax.dot_general(lhs, right[:, at], (((0,), (0,)), ((), ())), preferred_element_type=f32).astype(low)
            for t, (l, p) in enumerate(tiles):
                for q in range(per):
                    row = t * 128 + q * rows_own
                    g_own[m][l, p + q, :, at] = out[row : row + rows_own]

    def send_group(m, step, act):
        to = to_group(step)
        copy = remote(
            g_own[m].at[:, to], g_got[m].at[step - 1], gp_s.at[m, step], gp_r.at[m, step], me.at(c, to, k)
        )
        getattr(copy, act)()

    def products(left, pairs):
        if groups == 4:

            @pl.loop(0, groups)
            def body(t):
                step = (t + 1) % groups
                to = to_group(step)
                for m, right in pairs:
                    tile_products(m, left, right, [(l, to) for l in range(LINE)])

                    @pl.when(step > 0)
                    def _():
                        send_group(m, step, "start")
        else:

            @pl.loop(0, LINE)
            def body(l):
                for m, right in pairs:
                    tile_products(m, left, right, [(l, t * per) for t in range(4)])

            for m, _ in pairs:
                for step in range(1, groups):
                    send_group(m, step, "start")

    got_back.wait()
    got_d.wait()
    got_2.wait()
    products(left_buf.at[0], ((3, right_a), (2, right_c)))
    if double:
        got_two = load(lefts_in[1], left_buf.at[0], here.at[1])
        got_1 = load(rights_in[1], right_a, here.at[3])
        got_one.wait()
        got_q.wait()
        products(left_buf.at[1], ((0, right_b),))
    else:
        got_one = load(lefts_in[0], left_buf.at[0], here.at[1])
        got_q = load(rights_in[0], right_b, here.at[2])
        got_1 = load(rights_in[1], right_a, here.at[3])
        got_one.wait()
        got_q.wait()
        products(left_buf.at[0], ((0, right_b),))
        got_two = load(lefts_in[1], left_buf.at[0], here.at[1])

    for step in range(1, groups):
        arrived(early_group.at[from_group(step)], eg_s.at[step], eg_r.at[step])
    acc = early_group[0]
    for i in range(1, groups):
        acc = acc + early_group[i]
    early_out[k, c] = acc
    for step in range(1, LINE):
        go(remote(early_out.at[k, c], early_out.at[k, c], el_s.at[step], el_r.at[step], me.at(me.line_to(step), g, k)))

    got_two.wait()
    got_1.wait()
    products(left_buf.at[0], ((1, right_a),))

    got_s.wait()
    for step in range(1, LINE):
        arrived(s_line.at[step - 1], sline_s.at[step], sline_r.at[step])
    add_rows(
        lambda at: s_own.at[at],
        [lambda at: s_own.at[at]] + [partial(lambda p, at: s_line.at[p, at], p) for p in range(LINE - 1)],
        slot_len,
        16,
    )
    go(remote(s_own, ssum_ref.at[k], fin_s, fin_r, sibling))
    keep = [load(s_own, ssum_ref.at[k], keep_sem.at[0])]

    row_keep[...] = jnp.zeros_like(row_keep)

    def sum_groups(m, first):
        for step in range(1, groups):
            arrived(g_got[m].at[step - 1], gp_s.at[m, step], gp_r.at[m, step])
        width = pl.ds(pl.multiple_of(c * cols[m], 128), cols[m])
        total = jnp.zeros((8, cols[m]), f32)
        for step in (1, 2, 3, 0):
            line = me.line_to(step)

            def body(i, carry, line=line):
                at = pl.ds(pl.multiple_of(i * 16, 16), 16)
                acc = g_own[m][line, g, at, :].astype(f32)
                for p in range(groups - 1):
                    acc = acc + g_got[m][p, line, at, :].astype(f32)
                g_own[m][line, g, at, :] = acc.astype(low)
                square = acc * acc + eps_second
                row_keep[line, at, m : m + 1] = jnp.sum(square, 1, keepdims=True)
                return carry + square[:8] + square[8:]

            total = lax.fori_loop(0, rows_own // 16, body, total)
            if step:
                go(
                    remote(
                        g_own[m].at[line, g], g_out[m].at[:, width], gl_s.at[m, step], gl_r.at[m, step],
                        me.at(line, g, k),
                    )
                )
            else:
                keep.append(load(g_own[m].at[line, g], g_out[m].at[:, width], keep_sem.at[2 + m]))
        total = jnp.sum(total, 0, keepdims=True)
        for t in range(cols[m] // 128):
            col_now[first + t : first + t + 1, :] = total[:, t * 128 : (t + 1) * 128]

    firsts = []
    edge = 0
    for m in range(count):
        firsts.append(edge)
        edge += cols[m] // 128
    sum_groups(3, firsts[3])
    sum_groups(2, firsts[2])

    for step in range(1, groups):
        arrived(m_all.at[pl.ds(from_group(step) * seqs, seqs)], mall_s.at[step], mall_r.at[step])
    mixed_cols = pl.ds(pl.multiple_of((c * 2 + k) * feat, 128), feat)
    for step in (1, 2, 3, 0):
        line = me.line_to(step)
        for s in range(seq_dev):
            m_send[line, s] = m_all[pick[line * seq_dev + s]]
        where = mixed_ref.at[:, :, mixed_cols]
        if step:
            go(remote(m_send.at[line], where, mout_s.at[0, step], mout_r.at[0, step], me.at(line, g, k)))
        else:
            keep.append(load(m_send.at[line], where, keep_sem.at[1]))
        go(remote(m_send.at[line], where, mout_s.at[1, step], mout_r.at[1, step], me.at(line, g, me.other)))

    sum_groups(0, firsts[0])
    sum_groups(1, firsts[1])

    for step in range(1, groups):
        go(remote(col_now, col_group.at[g], cg_s.at[step], cg_r.at[step], me.at(c, to_group(step), k)))
    col_group[g] = col_now[...]
    for step in (1, 2, 3, 0):
        line = me.line_to(step)
        row_turn[line] = jnp.transpose(row_keep[line])[:8]
        if step:
            go(remote(row_turn.at[line], row_out.at[k, c], rl_s.at[0, step], rl_r.at[0, step], me.at(line, g, k)))
        else:
            row_out[k, c] = row_turn[line]
        go(remote(row_turn.at[line], row_out.at[k, c], rl_s.at[1, step], rl_r.at[1, step], me.at(line, g, me.other)))
    for step in range(1, groups):
        arrived(col_group.at[from_group(step)], cg_s.at[step], cg_r.at[step])
    acc = col_group[0]
    for i in range(1, groups):
        acc = acc + col_group[i]
    col_out[k, c] = acc
    for step in range(1, LINE):
        go(remote(col_out.at[k, c], col_out.at[k, c], cl_s.at[step], cl_r.at[step], me.at(me.line_to(step), g, k)))
    for step in range(1, LINE):
        arrived(early_out.at[k, me.line_from(step)], el_s.at[step], el_r.at[step])
    go(remote(early_out.at[k], early_out.at[k], es_s, es_r, sibling))
    for step in range(1, LINE):
        arrived(col_out.at[k, me.line_from(step)], cl_s.at[step], cl_r.at[step])
    go(remote(col_out.at[k], col_out.at[k], cs_s, cs_r, sibling))

    for m in range(count):
        for step in range(1, LINE):
            dst = g_out[m].at[:, pl.ds(pl.multiple_of(me.line_from(step) * cols[m], 128), cols[m])]
            arrived(dst, gl_s.at[m, step], gl_r.at[m, step])
    for step in range(LINE):
        source = me.line_from(step)
        for core, way in ((k, 0), (me.other, 1)):
            if step or way:
                dst = mixed_ref.at[:, :, pl.ds(pl.multiple_of((source * 2 + core) * feat, 128), feat)]
                arrived(dst, mout_s.at[way, step], mout_r.at[way, step])
                arrived(row_out.at[core, source], rl_s.at[way, step], rl_r.at[way, step])
    arrived(ssum_ref.at[me.other], fin_s, fin_r)
    arrived(early_out.at[me.other], es_s, es_r)
    arrived(col_out.at[me.other], cs_s, cs_r)
    for copy in sends:
        copy.wait_send()
    for m in range(count):
        for step in range(1, groups):
            send_group(m, step, "wait_send")
    for copy in keep:
        copy.wait()


def scatter_all(groups, cols, seq_dev, rows_own, pick, m_line, s_pair, lefts, rights, early):
    slot_len = s_pair.shape[1]
    rows = lefts[0].shape[0]
    count = len(cols)
    feat = D // (2 * LINE)
    seqs = LINE * seq_dev
    dma = pltpu.SemaphoreType.DMA
    f32, low = jnp.float32, jnp.bfloat16
    col_rows = sum(cols) // 128
    return pl.pallas_call(
        partial(scatter_kernel, groups, cols, seq_dev, slot_len, rows_own),
        out_shape=[
            jax.ShapeDtypeStruct((seq_dev, slot_len, D), low),
            jax.ShapeDtypeStruct((seq_dev, slot_len, D), low),
        ]
        + [jax.ShapeDtypeStruct((rows_own, LINE * width), low) for width in cols]
        + [
            jax.ShapeDtypeStruct((2, LINE) + early.shape, f32),
            jax.ShapeDtypeStruct((2, LINE, col_rows, 128), f32),
            jax.ShapeDtypeStruct((2, LINE, 8, 128), f32),
        ],
        in_specs=[SMEM] + [ANY] * (5 + count) + [VMEM],
        out_specs=[ANY] * (2 + count) + [VMEM] * 3,
        scratch_shapes=[
            pltpu.VMEM((2 if groups == 4 else 1, rows, D), low),
            pltpu.VMEM((rows, cols[1]), low),
            pltpu.VMEM((rows, cols[0]), low),
            pltpu.VMEM((rows, cols[2]), low),
        ]
        + [pltpu.VMEM((LINE, groups, rows_own, width), low) for width in cols]
        + [pltpu.VMEM((groups - 1, LINE, rows_own, width), low) for width in cols]
        + [
            pltpu.VMEM((LINE, seqs, slot_len, feat), low),
            pltpu.VMEM((groups * seqs, slot_len, feat), low),
            pltpu.VMEM((LINE, seq_dev, slot_len, feat), low),
            pltpu.VMEM((slot_len, D), low),
            pltpu.VMEM((LINE - 1, slot_len, D), low),
            pltpu.VMEM((groups,) + early.shape, f32),
            pltpu.VMEM((col_rows, 128), f32),
            pltpu.VMEM((groups, col_rows, 128), f32),
            pltpu.VMEM((LINE, 128, 128), f32),
            pltpu.VMEM((LINE, 8, 128), f32),
            dma((7,)),
            dma((LINE,)),
            dma((LINE,)),
            dma(()),
            dma(()),
            dma((groups,)),
            dma((groups,)),
            dma((2, LINE)),
            dma((2, LINE)),
            dma((count, groups)),
            dma((count, groups)),
            dma((count, LINE)),
            dma((count, LINE)),
            dma((groups,)),
            dma((groups,)),
            dma((LINE,)),
            dma((LINE,)),
            dma(()),
            dma(()),
            dma((groups,)),
            dma((groups,)),
            dma((LINE,)),
            dma((LINE,)),
            dma(()),
            dma(()),
            dma((2, LINE)),
            dma((2, LINE)),
            dma((2 + count,)),
        ],
        compiler_params=pltpu.CompilerParams(
            collective_id=1, has_side_effects=True, vmem_limit_bytes=62 * 1024 * 1024
        ),
        name="scatter_all",
    )(pick, m_line.reshape(LINE, seqs, slot_len, feat), s_pair, *lefts, *rights, early)


def per_device(
    tokens,
    cotangent,
    lengths,
    permutation,
    w_qkv,
    w_dense,
    w_fc1,
    w_fc2,
    norm_vectors,
    split_biases,
    row_state,
    col_state,
    norm_moment,
    bias_moment,
):
    f32, low = jnp.float32, jnp.bfloat16
    n_data = lax.axis_size("dp")
    groups = n_data // LINE
    data = lax.axis_index("dp")
    core = lax.axis_index("tensor")
    line = data // groups
    group = data % groups
    seq_dev, slot_len, width = tokens.shape
    rows_own = w_qkv.shape[0]
    seqs = LINE * seq_dev
    rows = seqs * slot_len
    head_dim = D // HEADS
    rot_dims = head_dim // 4
    weights = (w_qkv, w_dense, w_fc1, w_fc2)
    cols = tuple(w.shape[1] // LINE for w in weights)
    order = (0, 2, 1, 3)
    lows = [weights[i].astype(low) for i in order]
    mine = (jnp.arange(LINE)[:, None] * groups + group) * seq_dev + jnp.arange(seq_dev)[None, :]
    my_lengths = jnp.take(lengths, mine.reshape(-1))
    places = jnp.arange(slot_len, dtype=jnp.int32)
    valid = (places[None, :] < my_lengths[:, None]).astype(f32).reshape(rows, 1)
    bias_qkv = lax.dynamic_slice_in_dim(split_biases, line * cols[0], cols[0], 1)
    bias_mlp = lax.dynamic_slice_in_dim(split_biases, LINE * cols[0] + line * cols[2], cols[2], 1)
    row_old = jnp.where(core == 0, jnp.sum(row_state, 1), 0.0)
    extra = jnp.zeros((2, D), f32).at[0, :4].set(row_old)
    vectors = jnp.concatenate([norm_vectors, extra], 0)
    (norm_one, norm_two, back, qkv_grad, pre_grad, attn, hidden, m_line, s_pair, early) = gather_all(
        groups, lows, tokens, cotangent, vectors, jnp.concatenate([bias_qkv, bias_mlp], 1), valid,
        turn_tables(slot_len, rot_dims, head_dim // 2),
    )
    source = jnp.take(permutation, mine.reshape(-1))
    chip, inside = source // seq_dev, source % seq_dev
    pick = ((chip % groups) * seqs + (chip // groups) * seq_dev + inside).astype(jnp.int32)
    outs = scatter_all(
        groups,
        tuple(cols[i] for i in order),
        seq_dev,
        rows_own,
        pick,
        m_line,
        s_pair,
        (norm_one, norm_two, back),
        (qkv_grad, pre_grad, attn, hidden),
        early,
    )
    mixed, s_sum = outs[:2]
    early_all, col_all, row_all = outs[6:]
    grads = [None] * 4
    for place, i in enumerate(order):
        grads[i] = outs[2 + place].astype(f32)
    own_x = tokens.reshape(-1, width).astype(f32)
    own_centre = own_x - jnp.mean(own_x, -1, keepdims=True)
    own_scale = lax.rsqrt(jnp.mean(own_centre * own_centre, -1, keepdims=True) + eps_norm)
    own_unit = own_centre * own_scale
    own_valid = (places[None, :] < lax.dynamic_slice_in_dim(lengths, data * seq_dev, seq_dev)[:, None]).reshape(-1, 1)
    own_back = jnp.where(own_valid, cotangent.reshape(-1, width), jnp.zeros((), low)).astype(f32)
    flow = s_sum.reshape(-1, width).astype(f32)
    through = own_scale * (
        flow - jnp.mean(flow, -1, keepdims=True) - own_unit * jnp.mean(flow * own_unit, -1, keepdims=True)
    )
    grad_tokens = (own_back + through).astype(low).reshape(seq_dev, slot_len, width)
    early_all = early_all.reshape(2, LINE, -1)
    at_bias = 5 * D
    at_row = at_bias + cols[0] + cols[2]
    both = jnp.sum(early_all, (0, 1))
    norm_total = both[:at_bias].reshape(5, D)
    norm_total = jnp.concatenate([norm_total, norm_total[4:]], 0)
    bias_mine = lax.dynamic_index_in_dim(early_all, core, 0, False)[:, at_bias:at_row]
    bias_total = jnp.concatenate([bias_mine[:, : cols[0]].reshape(-1), bias_mine[:, cols[0] :].reshape(-1)])[None, :]
    row_old_sum = both[at_row : at_row + 4]
    row_total = jnp.sum(row_all, (0, 1))[:, :rows_own]
    col_mine = lax.dynamic_index_in_dim(col_all, core, 0, False).reshape(LINE, -1)
    mass_all = jnp.sum(col_all, (0, 1)).reshape(-1)
    row_at, col_at, mass_at, edge = [None] * 4, [None] * 4, [None] * 4, 0
    for place, i in enumerate(order):
        row_at[i] = row_total[place]
        col_at[i] = col_mine[:, edge : edge + cols[i]].reshape(-1)
        mass_at[i] = jnp.sum(mass_all[edge : edge + cols[i]])
        edge += cols[i]
    col_total = jnp.concatenate(col_at)
    col_new = decay * col_state + (1.0 - decay) * (col_total[None, :] / D)
    full_cols = (3.0 * D, 1.0 * D, 1.0 * FF, 1.0 * FF)
    rates = (
        rate_scale / math.sqrt(D),
        rate_scale / math.sqrt(D // 8),
        rate_scale / math.sqrt(D),
        rate_scale / math.sqrt(FF),
    )
    new_list, row_list = [], []
    edge = 0
    for i in range(4):
        wide = weights[i].shape[1]
        row_new = decay * row_state[i] + (1.0 - decay) * (row_at[i] / full_cols[i])
        mean = (decay * row_old_sum[i] + (1.0 - decay) * (mass_at[i] / full_cols[i])) / D
        second = row_new[:, None] * col_new[0, edge : edge + wide][None, :] / mean
        new_list.append(weights[i] - rates[i] * grads[i] * lax.rsqrt(second))
        row_list.append(row_new)
        edge += wide
    row_new = jnp.stack(row_list)
    norm_moment_new = decay * norm_moment + (1.0 - decay) * (norm_total * norm_total + eps_second)
    norm_new = norm_vectors - rate_norm * norm_total * lax.rsqrt(norm_moment_new)
    bias_moment_new = decay * bias_moment + (1.0 - decay) * (bias_total * bias_total + eps_second)
    bias_new = split_biases - rate_vector * bias_total * lax.rsqrt(bias_moment_new)
    return (
        mixed,
        grad_tokens,
        *grads,
        *new_list,
        *[new.astype(low) for new in new_list],
        row_new,
        col_new,
        norm_total,
        norm_moment_new,
        norm_new,
        bias_total,
        bias_moment_new,
        bias_new,
    )


def solution(mesh):
    halves = P("dp", "tensor")
    split = P("tensor", None)
    in_specs = (
        P("dp", None, None),
        P("dp", None, None),
        P(),
        P(),
        halves,
        halves,
        halves,
        halves,
        P(),
        split,
        P(None, "dp"),
        split,
        P(),
        split,
    )
    out_specs = (
        (P("dp", None, None),) * 2
        + (halves,) * 12
        + (P(None, "dp"), split)
        + (P(),) * 3
        + (split,) * 3
    )
    return jax.shard_map(
        per_device, mesh=mesh, in_specs=in_specs, out_specs=out_specs, check_vma=False
    )
```

time: 701 us -> 517 us (0.74)
  matrix products: 137 us -> 0 us
  other arithmetic: 68.4 us -> 33.8 us
  local copies, waits for them, and re-layouts: 21.1 us -> 10.1 us
    dot_general x17 -> x0, matrix products: 133 us -> none  [the longest x4 48.4 us: contract_last(): lax.dot_general(left, right, (((1,), (1,)), ((), ())), preferred_element_...]
    reduce_sum x10 -> x6, other arithmetic: 18.3 us -> 2.85 us  [the longest x3 1.8 us: per_device(): mass_at[i] = jnp.sum(mass_all[edge:edge + cols[i]])]
    select_n x3 -> x0, other arithmetic: 7.25 us -> none  [the longest x2 7.24 us: per_device(): back = jnp.where(valid, back_all.reshape(rows, width), jnp.zeros((), low))]
    pallas_call x3 -> x2, Pallas kernels: 460 us -> 466 us  [the longest x1 256 us: gather_all(): pl.pallas_call(partial(gather_kernel, groups, cols, seq_dev, slot_len), o...]
where the time goes in v2:
time: 517 us; the launch traced here: 516 us
  Pallas kernels  466 us (90%)
  other arithmetic  33.8 us (7%)
  local copies, waits for them, and re-layouts  10.1 us (2%)
  between operations  6.49 us (1%)
    pallas_call x1, Pallas kernels, gather_all(): pl.pallas_call(partial(gather_kernel, groups, cols, seq_dev, slot_len), o...  256 us
    pallas_call x1, Pallas kernels, scatter_all(): pl.pallas_call(partial(scatter_kernel, groups, cols, seq_dev, slot_len, r...  209 us
    convert_element_type x4, other arithmetic, per_device(): new.astype(low)  13.8 us

profile of v2, /device:TPU:0, one launch (start us, length us, event | category | flops | bytes accessed | tf_op | source)
XLA Modules:
  0.0 516.2 jit_solution(14376906517146170372)
XLA Ops:
  1.3 0.6 gather_fusion
  2.0 1.3 gather_fusion.1
  3.9 1.5 reshape.489.refs_8_
  5.4 0.7 constant_dynamic-slice_fusion
  6.1 0.7 constant_dynamic-slice_fusion.1
  6.7 0.6 pad_maximum_fusion.3.refs_7_
  8.1 0.7 pad_maximum_fusion.refs_9_
  8.9 0.6 select_maximum_fusion.refs_6_
  9.6 2.7 convert_element_type.71.refs_1_
  12.3 1.1 convert_element_type.73.refs_3_
  13.4 0.7 copy-done.6
  14.1 1.0 convert_element_type.70.refs_0_
  15.0 0.7 convert_element_type.72.refs_2_
  15.8 256.4 %gather_all.1 = (bf16[1536,2048]{1,0:T(8,128)(2,1)}, bf16[1536,2048]{1,0:T(8,128)(2,1)}, bf16[1536,2048]{1,0:T(8,128)(2,1)}, bf16[1536,768]{1,0:T(8,128)(2,1)}, ...) custom-call(bf16[128,3072]{1,0:T(8,128)(2,1)} %convert_element_type., ...), custom_call_target="tpu_custom_call" | custom-call | tf_op jit(solution)/shard_map/gather_all/pallas_call | solution.py:604
  272.2 209.4 %scatter_all.1 = (bf16[2,192,2048]{2,1,0:T(8,128)(2,1)}, bf16[2,192,2048]{2,1,0:T(8,128)(2,1)}, bf16[128,3072]{1,0:T(8,128)(2,1)}, bf16[128,4096]{1,0:T(8,128)(2...) custom-call(s32[8]{0:T(128)} %get-tuple-element.115.refs_0_, ...), custom_call_target="tpu_custom_call" | custom-call | tf_op jit(solution)/shard_map/scatter_all/pallas_call | solution.py:956
  481.7 1.3 reshape.463
  483.1 0.7 multiply_subtract_fusion.5
  483.8 0.6 pad_maximum_fusion.2
  484.5 1.0 reduce_sum.116
  485.5 0.7 multiply_subtract_fusion.4
  486.3 0.6 pad_maximum_fusion.4
  486.8 0.6 fusion.22
  488.1 0.6 slice_reduce_fusion
  489.7 4.2 fusion.17
  495.1 4.8 fusion.18
  500.8 0.6 slice_reduce_fusion.3
  502.0 1.2 fusion.19
  503.9 0.6 slice_reduce_fusion.2
  505.2 3.6 fusion.20
  510.2 1.1 convert_reduce_fusion
  511.5 3.6 fusion.6
  515.1 1.1 copy.52
  (94 shorter events, 4.0 us)
Async XLA Ops:
  0.7 0.7 copy-start
  0.7 8.1 %copy-start.20 = (f32[4,128]{1,0:T(4,128)S(1)}, f32[4,128]{1,0:T(4,128)}, u32[]{:S(2)}) copy-start(f32[4,128]{1,0:T(4,128)} %param.28) | copy-start | bytes 6148
  0.7 8.3 %copy-start.11 = (f32[6,2048]{1,0:T(8,128)S(1)}, f32[6,2048]{1,0:T(8,128)}, u32[]{:S(2)}) copy-start(f32[6,2048]{1,0:T(8,128)} %param.26) | copy-start | bytes 147460
  7.9 4.4 copy-start.4
  12.3 1.8 copy-start.6
  12.3 2.8 copy-start.9
  272.2 210.9 %copy-start.17 = (f32[1,7168]{1,0:T(1,128)S(1)}, f32[1,7168]{1,0:T(1,128)}, u32[]{:S(2)}) copy-start(f32[1,7168]{1,0:T(1,128)} %param.27) | copy-start | bytes 86020
  272.2 210.9 %copy-start.19 = (f32[1,7168]{1,0:T(1,128)S(1)}, f32[1,7168]{1,0:T(1,128)}, u32[]{:S(2)}) copy-start(f32[1,7168]{1,0:T(1,128)} %param.31) | copy-start | bytes 86020
  481.6 3.9 copy-start.15
  481.6 4.6 copy-start.18
  481.6 6.5 %copy-start.13 = (f32[2,4,24,128]{3,2,1,0:T(8,128)S(1)}, f32[2,4,24,128]{3,2,1,0:T(8,128)}, u32[]{:S(2)}) copy-start(f32[2,4,24,128]{3,2,1,0:T(8,128)} %get-tuple-element.71) | copy-start | bytes 294916
  481.6 7.9 %copy-start.16 = (f32[1,12288]{1,0:T(1,128)S(1)}, f32[1,12288]{1,0:T(1,128)}, u32[]{:S(2)}) copy-start(f32[1,12288]{1,0:T(1,128)} %param.29) | copy-start | bytes 147460
  481.6 8.0 %copy-start.5 = (f32[128,4096]{1,0:T(8,128)S(1)}, f32[128,4096]{1,0:T(8,128)}, u32[]{:S(2)}) copy-start(f32[128,4096]{1,0:T(8,128)} %param.25) | copy-start | bytes 6291460
  489.6 13.6 %copy-start.14 = (f32[1,12288]{1,0:T(1,128)}, f32[1,12288]{1,0:T(1,128)S(1)}, u32[]{:S(2)}) copy-start(f32[1,12288]{1,0:T(1,128)S(1)} %fusion.11) | copy-start | bytes 147460
  495.1 6.9 %copy-start.12 = (bf16[128,1024]{1,0:T(8,128)(2,1)S(1)}, bf16[128,1024]{1,0:T(8,128)(2,1)}, u32[]{:S(2)}) copy-start(bf16[128,1024]{1,0:T(8,128)(2,1)} %get-tuple-element.67) | copy-start | bytes 786436
  500.0 5.2 %copy-start.7 = (f32[128,3072]{1,0:T(8,128)S(1)}, f32[128,3072]{1,0:T(8,128)}, u32[]{:S(2)}) copy-start(f32[128,3072]{1,0:T(8,128)} %param.22) | copy-start | bytes 4718596
  505.2 3.6 copy-start.3
  508.8 1.4 copy-start.8
  509.1 2.2 copy-start.2
  511.5 3.6 copy-start.10
  511.5 4.7 copy-start.1

commit v3 on v2

v3 whole, which is shorter than its diff:
```python
from functools import partial
import math

import jax
import jax.numpy as jnp
import numpy as np
from jax import lax
from jax.experimental import pallas as pl
from jax.experimental.pallas import tpu as pltpu
from jax.sharding import PartitionSpec as P

D = 2048
FF = 8192
HEADS = 8
LINE = 4

eps_norm = 1e-05
eps_second = 1e-30
decay = 0.5
rate_scale = 1.0
rate_norm = 0.5
rate_vector = 0.05
neg_large = -1e30

MESH = pl.DeviceIdType.MESH
ANY = pl.BlockSpec(memory_space=pl.ANY)
VMEM = pl.BlockSpec(memory_space=pltpu.VMEM)
SMEM = pl.BlockSpec(memory_space=pltpu.SMEM)


def turn_tables(slot_len, rot_dims, width):
    half = rot_dims // 2
    freq = np.float32(10000.0) ** (np.float32(-2.0) * np.arange(half, dtype=np.float32) / np.float32(rot_dims))
    angle = np.arange(slot_len, dtype=np.float32)[:, None] * freq[None, :].astype(np.float32)
    tables = np.zeros((3, slot_len, width), np.float32)
    tables[0] = 1.0
    tables[0, :, :half] = tables[0, :, half:rot_dims] = np.cos(angle)
    tables[1, :, :half] = tables[2, :, half:rot_dims] = np.sin(angle)
    return tables


class Place:
    def __init__(self, groups):
        self.groups = groups
        data = lax.axis_index("dp")
        self.core = lax.axis_index("tensor")
        self.other = 1 - self.core
        self.line = data // groups
        self.group = data % groups

    def at(self, line, group, core):
        return (line * self.groups + group, core)

    def line_to(self, step):
        return (self.line + step) % LINE

    def line_from(self, step):
        return (self.line + LINE - step) % LINE

    def group_to(self, step):
        g = self.group
        if self.groups == 4:
            if step == 1:
                return g + 1 - 2 * (g % 2)
            if step == 2:
                return (g + 2) % 4
            return 3 - g
        return (g + step) % self.groups

    def group_from(self, step):
        if self.groups == 4:
            return self.group_to(step)
        return (self.group + self.groups - step) % self.groups

    def greet(self):
        barrier = pltpu.get_barrier_semaphore()
        count = 0
        for step in range(1, LINE):
            for core in (self.core, self.other):
                pl.semaphore_signal(
                    barrier, inc=1, device_id=self.at(self.line_to(step), self.group, core), device_id_type=MESH
                )
                count += 1
        for step in range(1, self.groups):
            pl.semaphore_signal(
                barrier, inc=1, device_id=self.at(self.line, self.group_to(step), self.core), device_id_type=MESH
            )
            count += 1
        pl.semaphore_signal(
            barrier, inc=1, device_id=self.at(self.line, self.group, self.other), device_id_type=MESH
        )
        pl.semaphore_wait(barrier, count + 1)


def remote(src, dst, send, recv, device):
    return pltpu.make_async_remote_copy(
        src_ref=src, dst_ref=dst, send_sem=send, recv_sem=recv, device_id=device, device_id_type=MESH
    )


def dot(left, right):
    return jnp.dot(left, right, preferred_element_type=jnp.float32)


def gather_kernel(groups, cols, seq_dev, slot_len, *refs):
    count = len(cols)
    f32, low = jnp.float32, jnp.bfloat16
    w_in = refs[:count]
    acts_in = refs[count : count + 2]
    vec_ref, bias_ref, valid_ref, turn_ref = refs[count + 2 : count + 6]
    outs = refs[count + 6 : count + 18]
    (n1_out, n2_out, qg_out, pg_out, near_out, far_out, s_out, gd_own, g2_own, gd_got, g2_got, early_ref) = outs
    rest = refs[count + 18 :]
    w_out = rest[:count]
    acts_out = rest[count : count + 2]
    (qkv_keep, prob_keep, attn_keep, hid_keep, pg_keep, one_buf, two_buf, back_buf, m_buf, m_got, m_half, s_got,
     qkv_now, pre_now, stat_keep, norm_acc, bias_acc) = rest[count + 2 : count + 19]
    (one_s, one_r, two_s, two_r, three_s, three_r, row_s, row_r, sib_s, sib_r, here, out_a, out_b,
     out_d, msib_s, msib_r, ssib_s, ssib_r, half_s, half_r, far_s, far_r, near_sem, s_here, gp_s, gp_r,
     g_here) = rest[count + 19 :]
    me = Place(groups)
    c, g, k = me.line, me.group, me.core
    me.greet()
    sibling = me.at(c, g, me.other)
    rows_own = w_in[0].shape[0]
    block_rows = seq_dev * slot_len
    near = groups == 4
    START, SENT = "start", "wait_send"

    def block(ref, line, width):
        return ref.at[:, pl.ds(pl.multiple_of(line * width, 128), width)]

    def place(m, line, group):
        return w_out[m].at[pl.ds(pl.multiple_of((line * groups + group) * rows_own, 32), rows_own)]

    def rows_of(which, line, core):
        return acts_out[which].at[pl.ds(pl.multiple_of((line * seq_dev + core) * slot_len, 32), slot_len)]

    partner = c + 1 - 2 * (c % 2)
    beyond = (c + 2) % LINE

    def row_send(which, q, act):
        origin = beyond if q == 2 else c
        copy = remote(
            rows_of(which, beyond, k) if q == 2 else acts_in[which].at[k],
            rows_of(which, origin, k),
            row_s.at[which, q],
            row_r.at[which, q],
            me.at(beyond if q == 1 else partner, g, k),
        )
        getattr(copy, act)()

    def row_origin(q):
        return (partner, beyond, (partner + 2) % LINE)[q]

    def to_sibling(which, q, act):
        rows = rows_of(which, row_origin(q), k)
        copy = remote(rows, rows, sib_s.at[which, q], sib_r.at[which, q], sibling)
        getattr(copy, act)()

    def pass_on(which, q):
        rows = rows_of(which, row_origin(q), k)
        remote(rows, rows, row_s.at[which, q], row_r.at[which, q], sibling).wait_recv()
        if q == 1:
            row_send(which, 2, START)
        to_sibling(which, q, START)

    def arrive_sibling(which):
        for q in range(3):
            rows = rows_of(which, row_origin(q), me.other)
            remote(rows, rows, sib_s.at[which, q], sib_r.at[which, q], sibling).wait_recv()

    def local_acts(which, act):
        for s in range(seq_dev):
            copy = pltpu.make_async_copy(acts_in[which].at[s], rows_of(which, c, s), here.at[count + which, s])
            getattr(copy, act)()

    def local_weight(m, act):
        copy = pltpu.make_async_copy(block(w_in[m], c, cols[m]), place(m, c, g), here.at[m, 0])
        getattr(copy, act)()

    def stage_one(m, act):
        for step in range(1, LINE):
            to = me.line_to(step)
            copy = remote(
                block(w_in[m], to, cols[m]),
                place(m, c, g),
                one_s.at[m, step],
                one_r.at[m, step],
                me.at(to, g, k),
            )
            getattr(copy, act)()

    def stage_two(m, step, act):
        where = place(m, me.line_from(step), g)
        src = block(w_in[m], c, cols[m]) if step == 0 else where
        for peer in range(1, 3 if near else groups):
            copy = remote(
                src, where, two_s.at[m, step, peer], two_r.at[m, step, peer], me.at(c, me.group_to(peer), k)
            )
            getattr(copy, act)()

    def first_half(m):
        for step in range(1, LINE):
            dst = place(m, me.line_from(step), g)
            remote(dst, dst, one_s.at[m, step], one_r.at[m, step], sibling).wait_recv()
            stage_two(m, step, START)

    def wait_two(m, step, peer):
        dst = place(m, me.line_from(step), me.group_from(peer))
        remote(dst, dst, two_s.at[m, step, peer], two_r.at[m, step, peer], sibling).wait_recv()

    def stage_three(m, step, act):
        source, target = (1, 2) if step % 2 == 0 else (2, 1)
        where = place(m, me.line_from(step), me.group_to(source))
        copy = remote(where, where, three_s.at[m, step], three_r.at[m, step], me.at(c, me.group_to(target), k))
        getattr(copy, act)()

    def relay(m):
        for step in range(LINE):
            for peer in range(1, 3 if near else groups):
                wait_two(m, step, peer)
            if near:
                stage_three(m, step, START)

    def last(m):
        if near:
            for step in range(LINE):
                dst = place(m, me.line_from(step), me.group_to(3))
                remote(dst, dst, three_s.at[m, step], three_r.at[m, step], sibling).wait_recv()

    row_send(0, 1, START)
    row_send(0, 0, START)
    for m in (0, 1):
        stage_one(m, START)
        stage_two(m, 0, START)
    local_acts(0, START)
    local_weight(0, START)
    local_weight(1, START)
    norm_acc[...] = jnp.zeros_like(norm_acc)
    bias_acc[...] = jnp.zeros_like(bias_acc)
    first_half(0)
    pass_on(0, 1)
    for m in (2, 3):
        stage_one(m, START)
        stage_two(m, 0, START)
    local_acts(1, START)
    local_weight(2, START)
    local_weight(3, START)
    pass_on(0, 0)
    first_half(1)
    row_send(1, 1, START)
    row_send(1, 0, START)
    relay(0)
    pass_on(0, 2)
    relay(1)
    local_acts(0, "wait")
    local_weight(0, "wait")
    local_weight(1, "wait")
    last(0)
    last(1)
    arrive_sibling(0)

    wq, w1, wd, w2 = w_out
    x_all, ct_all = acts_out
    head = cols[0] // 3
    half = head // 2
    chunk = 16
    wide = 512
    ways = D // wide
    root = math.sqrt(head)
    causal = lax.broadcasted_iota(jnp.int32, (slot_len, slot_len), 0) >= lax.broadcasted_iota(
        jnp.int32, (slot_len, slot_len), 1
    )

    def turn(v, sign):
        left = pltpu.roll(v, half - 32, 1)
        right = pltpu.roll(v, 32, 1)
        if sign > 0:
            return v * turn_ref[0] - left * turn_ref[1] + right * turn_ref[2]
        return v * turn_ref[0] + left * turn_ref[1] - right * turn_ref[2]

    def contract(left, right, dims):
        return lax.dot_general(left, right, ((dims[0], dims[1]), ((), ())), preferred_element_type=f32)

    def put_one(i, line, act):
        rows = pl.ds(pl.multiple_of(line * block_rows, 128), block_rows)
        getattr(pltpu.make_async_copy(one_buf, n1_out.at[rows], out_a), act)()
        getattr(pltpu.make_async_copy(two_buf.at[0], n2_out.at[rows], out_b.at[0]), act)()

    @pl.loop(0, LINE)
    def forward(i):
        line = (c + i) % LINE
        base = pl.multiple_of(line * block_rows, 128)

        @pl.when(i == 0)
        def _():
            first_half(2)
            first_half(3)

        @pl.when(i == 1)
        def _():
            relay(2)
            pass_on(1, 1)

        @pl.when(i == 2)
        def _():
            relay(3)
            pass_on(1, 0)

        @pl.when(i >= 1)
        def _():
            put_one(i, line, "wait")

        @pl.loop(0, block_rows // chunk)
        def norm(j):
            at = pl.ds(pl.multiple_of(base + j * chunk, chunk), chunk)
            to = pl.ds(pl.multiple_of(j * chunk, chunk), chunk)
            x = x_all[at, :].astype(f32)
            mean = jnp.mean(x, -1, keepdims=True)
            centre = x - mean
            scale = lax.rsqrt(jnp.mean(centre * centre, -1, keepdims=True) + eps_norm)
            stat_keep[at, 0:1] = mean
            stat_keep[at, 1:2] = scale
            unit = centre * scale
            one_buf[to, :] = (unit * vec_ref[0:1, :] + vec_ref[1:2, :]).astype(low)
            two_buf[0, to, :] = (unit * vec_ref[2:3, :] + vec_ref[3:4, :]).astype(low)

        put_one(i, line, "start")
        qkv_now[...] = dot(one_buf[...], wq[...]) + bias_ref[0:1, : cols[0]]
        pre_now[...] = dot(two_buf[0], w1[...]) + bias_ref[0:1, cols[0] :]

        for s in range(seq_dev):
            part = slice(s * slot_len, (s + 1) * slot_len)
            rows = pl.ds(pl.multiple_of(base + s * slot_len, 32), slot_len)
            qkv_keep[rows, 0:half] = turn(qkv_now[part, 0:half], 1).astype(low)
            qkv_keep[rows, half:head] = qkv_now[part, half:head].astype(low)
            qkv_keep[rows, head : head + half] = turn(qkv_now[part, head : head + half], 1).astype(low)
            qkv_keep[rows, head + half :] = qkv_now[part, head + half :].astype(low)
            query = qkv_keep[rows, :head]
            keys = qkv_keep[rows, head : 2 * head]
            values = qkv_keep[rows, 2 * head :]
            scores = jnp.where(causal, contract(query, keys, ((1,), (1,))) / root, neg_large)
            expo = jnp.exp(scores - jnp.max(scores, -1, keepdims=True))
            probs = expo / jnp.sum(expo, -1, keepdims=True)
            prob_keep[line * seq_dev + s] = probs
            attn_keep[rows, :] = (dot(probs.astype(low), values) * valid_ref[rows, :]).astype(low)

        @pl.loop(0, block_rows // chunk)
        def act(j):
            at = pl.ds(pl.multiple_of(base + j * chunk, chunk), chunk)
            pre = pre_now[pl.ds(pl.multiple_of(j * chunk, chunk), chunk), :]
            area = 0.5 * (1.0 + lax.erf(pre * math.sqrt(0.5)))
            hid_keep[at, :] = (pre * area * valid_ref[at, :]).astype(low)
            pg_keep[at, :] = (area + pre * (jnp.exp(-0.5 * pre * pre) * (1.0 / math.sqrt(2.0 * math.pi)))).astype(low)

    put_one(LINE - 1, (c + LINE - 1) % LINE, "wait")
    local_weight(2, "wait")
    local_weight(3, "wait")
    last(2)
    last(3)
    mine = c * 2 + k

    def pair_m(i, act):
        copy = remote(m_buf.at[i % 2, me.other], m_got.at[i], msib_s.at[i], msib_r.at[i], sibling)
        getattr(copy, act)()

    def half_m(i, act):
        for q, to in enumerate((partner, (partner + 2) % LINE)):
            copy = remote(
                m_got.at[i, to], m_half.at[i, q], half_s.at[i, q], half_r.at[i, q], me.at(partner, g, k)
            )
            getattr(copy, act)()

    def far_m(i, act):
        copy = remote(m_got.at[i, beyond], far_out.at[i], far_s.at[i], far_r.at[i], me.at(beyond, g, k))
        getattr(copy, act)()

    def near_m(i, act):
        getattr(pltpu.make_async_copy(m_got.at[i, c], near_out.at[i], near_sem.at[i]), act)()

    def sent_m(i):
        half_m(i, SENT)
        far_m(i, SENT)
        near_m(i, "wait")

    def second_m(i):
        half_m(i, "wait_recv")

        @pl.loop(0, block_rows // 64)
        def add(j):
            at = pl.ds(pl.multiple_of(j * 64, 64), 64)
            for q, to in enumerate((c, beyond)):
                total = m_got[i, to, at, :].astype(f32) + m_half[i, q, at, :].astype(f32)
                m_got[i, to, at, :] = total.astype(low)

        far_m(i, START)
        near_m(i, START)

    def pair_add(i):
        pair_m(i, "wait_recv")

        @pl.loop(0, LINE)
        def add_outer(p):
            @pl.loop(0, block_rows // 64)
            def add(j):
                at = pl.ds(pl.multiple_of(j * 64, 64), 64)
                total = m_buf[i % 2, k, p, at, :].astype(f32) + m_got[i, p, at, :].astype(f32)
                m_got[i, p, at, :] = total.astype(low)

        half_m(i, START)

    @pl.loop(0, LINE)
    def outputs(i):
        base = pl.multiple_of(i * block_rows, 128)
        whole = pl.ds(base, block_rows)
        slot = i % 2

        @pl.when(i == 1)
        def _():
            pass_on(1, 2)

        @pl.when(i >= 2)
        def _():
            pair_m(i - 2, SENT)

        live = valid_ref[whole, :]

        @pl.loop(0, ways)
        def output(j):
            at = pl.ds(pl.multiple_of(j * wide, 128), wide)
            total = contract(attn_keep[whole, :], wd[at, :], ((1,), (1,)))
            total = total + contract(hid_keep[whole, :], w2[at, :], ((1,), (1,)))
            feature = (lax.broadcasted_iota(jnp.int32, (1, wide), 1) + j * wide) // (D // (2 * LINE))
            mask = jnp.where(feature == mine, 1.0, 0.0)
            extra = x_all[whole, at].astype(f32) + (vec_ref[4:5, at] + vec_ref[5:6, at])
            total = ((total + mask * extra) * live).astype(low)
            m_buf[slot, 0, j] = total[:, : wide // 2]
            m_buf[slot, 1, j] = total[:, wide // 2 :]

        pair_m(i, START)

        @pl.when(i >= 1)
        def _():
            pair_add(i - 1)

    local_acts(1, "wait")
    arrive_sibling(1)

    per = 128 // rows_own
    part_cols = 256
    fits = block_rows // 128
    pieces = (cols[2] + cols[3]) // part_cols
    dense_pieces = cols[2] // part_cols

    def out_group(i):
        flip_x, flip_y = 1 - i % 2, 1 - i // 2
        return (g // 2 + flip_y) % 2 * 2 + (g % 2 + flip_x) % 2

    def out_products(i):
        slot = i % 2
        if near:
            to = out_group(i)
            tiles = [(l, to) for l in range(LINE)]
        else:
            tiles = [(i, t * per) for t in range(LINE)]
        lhs = jnp.concatenate(
            [ct_all[:, pl.ds(pl.multiple_of((l * groups + p) * rows_own, 128), 128)] for l, p in tiles], 1
        )
        first = 0
        for right in (attn_keep, hid_keep):
            out = contract(lhs, right[...], ((0,), (0,))).astype(low)
            for n in range(right.shape[1] // part_cols):
                nb = first + n
                for t in range(LINE):
                    m_buf[slot, nb // fits, t, (nb % fits) * 128 : (nb % fits + 1) * 128, :] = out[
                        t * 128 : (t + 1) * 128, n * part_cols : (n + 1) * part_cols
                    ]
            first += right.shape[1] // part_cols

    def out_piece(i, nb, to):
        row = (nb % fits) * 128
        if near:
            return m_buf.at[i % 2, nb // fits, :, pl.ds(row, 128), :]
        return m_buf.at[i % 2, nb // fits, to // per, pl.ds(pl.multiple_of(row + (to % per) * rows_own, 32), rows_own), :]

    def out_place(refs, i, nb, step):
        ref, n = (refs[0], nb) if nb < dense_pieces else (refs[1], nb - dense_pieces)
        at = pl.ds(n * part_cols, part_cols)
        if step is not None:
            ref = ref.at[step - 1]
        return ref.at[:, :, at] if near else ref.at[i, :, at]

    def out_send(i, step, act):
        to = out_group(i) if near else (g + step) % groups
        for nb in range(pieces):
            sem = (0 if near else i, step, nb)
            copy = remote(
                out_piece(i, nb, to), out_place((gd_got, g2_got), i, nb, step), gp_s.at[sem], gp_r.at[sem],
                me.at(c, to, k),
            )
            getattr(copy, act)()

    def out_keep(i, act):
        for nb in range(pieces):
            copy = pltpu.make_async_copy(
                out_piece(i, nb, g), out_place((gd_own, g2_own), i, nb, None), g_here.at[0 if near else i, nb]
            )
            getattr(copy, act)()

    def out_sends(i, act):
        local = "wait" if act == SENT else act
        if near:

            @pl.when(i < groups - 1)
            def _():
                out_send(i, groups - 1 - i, act)

            @pl.when(i == groups - 1)
            def _():
                out_keep(i, local)
        else:
            for step in range(1, groups):
                out_send(i, step, act)
            out_keep(i, local)

    def pair_s(i, act):
        line = (c + i) % LINE
        rows = pl.ds(pl.multiple_of(me.other * slot_len, 32), slot_len)
        copy = remote(two_buf.at[i % 2, rows], s_got.at[line], ssib_s.at[i], ssib_r.at[i], sibling)
        getattr(copy, act)()

    def put_s(i, act):
        line = (c + i) % LINE
        rows = pl.ds(pl.multiple_of(k * slot_len, 32), slot_len)
        getattr(pltpu.make_async_copy(two_buf.at[i % 2, rows], s_out.at[line], s_here.at[i]), act)()

    def finish_s(i):
        line = (c + i) % LINE
        pair_s(i, "wait_recv")

        @pl.loop(0, slot_len // chunk)
        def add(j):
            at = pl.ds(pl.multiple_of(k * slot_len + j * chunk, chunk), chunk)
            to = pl.ds(pl.multiple_of(j * chunk, chunk), chunk)
            total = two_buf[i % 2, at, :].astype(f32) + s_got[line, to, :].astype(f32)
            two_buf[i % 2, at, :] = total.astype(low)

        put_s(i, START)

    def put_rest(line, act):
        rows = pl.ds(pl.multiple_of(line * block_rows, 128), block_rows)
        for place_at, (buf, out) in enumerate(((qkv_keep, qg_out), (pg_keep, pg_out))):
            getattr(pltpu.make_async_copy(buf.at[rows], out.at[rows], out_d.at[place_at, line]), act)()

    @pl.loop(0, LINE)
    def backward(i):
        line = (c + i) % LINE
        base = pl.multiple_of(line * block_rows, 128)
        whole = pl.ds(base, block_rows)
        slot = i % 2

        @pl.when(i == 0)
        def _():
            pair_m(LINE - 2, SENT)

        @pl.when(i == 1)
        def _():
            pair_m(LINE - 1, SENT)

        @pl.when(i >= 2)
        def _():
            out_sends(i - 2, SENT)

        out_products(i)
        out_sends(i, START)

        @pl.when(i == 0)
        def _():
            pair_add(LINE - 1)

        @pl.when((i == 1) | (i == 2))
        def _():
            second_m(i * 2 - 2)
            second_m(i * 2 - 1)

        live = valid_ref[whole, :]
        back_buf[...] = (ct_all[whole, :].astype(f32) * live).astype(low)
        attn_grad = dot(back_buf[...], wd[...]).astype(low)
        pre_now[...] = dot(back_buf[...], w2[...])

        @pl.when(i == 0)
        def _():
            rows = pl.ds(pl.multiple_of(k * slot_len, 32), slot_len)
            total = jnp.sum(back_buf[rows, :].astype(f32).reshape(slot_len // 8, 8, D), 0)
            norm_acc[4] = total

        @pl.loop(0, block_rows // chunk)
        def act(j):
            at = pl.ds(pl.multiple_of(base + j * chunk, chunk), chunk)
            grad = pre_now[pl.ds(pl.multiple_of(j * chunk, chunk), chunk), :] * pg_keep[at, :].astype(f32)
            grad = grad.astype(low)
            pg_keep[at, :] = grad
            grad = grad.astype(f32)
            bias_acc[:, cols[0] :] += grad[:8] + grad[8:]

        for s in range(seq_dev):
            rows = pl.ds(pl.multiple_of(base + s * slot_len, 32), slot_len)
            grad = attn_grad[s * slot_len : (s + 1) * slot_len]
            query = qkv_keep[rows, :head]
            keys = qkv_keep[rows, head : 2 * head]
            values = qkv_keep[rows, 2 * head :]
            probs = prob_keep[line * seq_dev + s]
            prob_grad = contract(grad, values, ((1,), (1,)))
            row_dot = jnp.sum(probs * prob_grad, -1, keepdims=True)
            score_grad = (probs * (prob_grad - row_dot)).astype(low)
            value_grad = contract(probs.astype(low), grad, ((0,), (0,)))
            query_grad = dot(score_grad, keys) / root
            key_grad = contract(score_grad, query, ((0,), (0,))) / root
            qkv_keep[rows, 0:half] = turn(query_grad[:, :half], -1).astype(low)
            qkv_keep[rows, half:head] = query_grad[:, half:].astype(low)
            qkv_keep[rows, head : head + half] = turn(key_grad[:, :half], -1).astype(low)
            qkv_keep[rows, head + half : 2 * head] = key_grad[:, half:].astype(low)
            qkv_keep[rows, 2 * head :] = value_grad.astype(low)
            summed = qkv_keep[rows, :].astype(f32).reshape(slot_len // 8, 8, cols[0])
            bias_acc[:, : cols[0]] += jnp.sum(summed, 0)

        put_rest(line, "start")
        mean = stat_keep[whole, 0:1]
        scale = stat_keep[whole, 1:2]

        @pl.when(i >= 2)
        def _():
            pair_s(i - 2, SENT)
            put_s(i - 2, "wait")

        @pl.loop(0, ways)
        def inputs(j):
            at = pl.ds(pl.multiple_of(j * wide, 128), wide)
            first = contract(qkv_keep[whole, :], wq[at, :], ((1,), (1,)))
            second = contract(pg_keep[whole, :], w1[at, :], ((1,), (1,)))
            two_buf[slot, :, at] = (first * vec_ref[0:1, at] + second * vec_ref[2:3, at]).astype(low)
            unit = (x_all[whole, at].astype(f32) - mean) * scale
            for place_at, value in enumerate((first * unit, first, second * unit, second)):
                norm_acc[place_at, :, at] += jnp.sum(value.reshape(block_rows // 8, 8, wide), 0)

        pair_s(i, START)

        @pl.when(i >= 1)
        def _():
            finish_s(i - 1)

    finish_s(LINE - 1)
    for r in range(5):
        total = jnp.sum(norm_acc[r], 0, keepdims=True)
        for t in range(D // 128):
            early_ref[r * (D // 128) + t : r * (D // 128) + t + 1, :] = total[:, t * 128 : (t + 1) * 128]
    at_bias = 5 * (D // 128)
    total = jnp.sum(bias_acc[...], 0, keepdims=True)
    for t in range((cols[0] + cols[1]) // 128):
        early_ref[at_bias + t : at_bias + t + 1, :] = total[:, t * 128 : (t + 1) * 128]
    at_row = at_bias + (cols[0] + cols[1]) // 128
    early_ref[at_row : at_row + 1, :] = vec_ref[6:7, :128]
    early_ref[at_row + 1 :, :] = jnp.zeros((early_ref.shape[0] - at_row - 1, 128), f32)
    for i in range(LINE):
        put_rest(i, "wait")
        sent_m(i)
        far_m(i, "wait_recv")
    for i in (LINE - 2, LINE - 1):
        pair_s(i, SENT)
        put_s(i, "wait")
        out_sends(i, SENT)
    for step in range(1, groups):
        for nb in range(pieces):
            for i in range(1 if near else LINE):
                dst = out_place((gd_got, g2_got), i, nb, step)
                sem = (i, step, nb)
                remote(dst, dst, gp_s.at[sem], gp_r.at[sem], sibling).wait_recv()
    for m in range(count):
        stage_one(m, SENT)
        for step in range(LINE):
            stage_two(m, step, SENT)
            if near:
                stage_three(m, step, SENT)
    for which in range(2):
        for q in range(3):
            row_send(which, q, SENT)
            to_sibling(which, q, SENT)


def gather_all(groups, weights, tokens, cotangent, vectors, biases, valid, turns):
    rows_own = weights[0].shape[0]
    seq_dev, slot_len, width = tokens.shape
    cols = tuple(w.shape[1] // LINE for w in weights)
    count = len(weights)
    block_rows = seq_dev * slot_len
    rows = LINE * block_rows
    f32, low = jnp.float32, jnp.bfloat16
    dma = pltpu.SemaphoreType.DMA
    peers = 3 if groups == 4 else groups
    out_widths = (D, D, cols[0], cols[1])
    pieces = (cols[2] + cols[3]) // 256
    feat = D // (2 * LINE)
    early_rows = -(-(5 * D + cols[0] + cols[1] + 128) // 1024) * 8
    return pl.pallas_call(
        partial(gather_kernel, groups, cols, seq_dev, slot_len),
        out_shape=[jax.ShapeDtypeStruct((rows, w), low) for w in out_widths]
        + [
            jax.ShapeDtypeStruct((LINE, block_rows, feat), low),
            jax.ShapeDtypeStruct((LINE, block_rows, feat), low),
            jax.ShapeDtypeStruct((LINE, slot_len, D), low),
            jax.ShapeDtypeStruct((LINE, rows_own, cols[2]), low),
            jax.ShapeDtypeStruct((LINE, rows_own, cols[3]), low),
            jax.ShapeDtypeStruct((groups - 1, LINE, rows_own, cols[2]), low),
            jax.ShapeDtypeStruct((groups - 1, LINE, rows_own, cols[3]), low),
            jax.ShapeDtypeStruct((early_rows, 128), f32),
        ],
        in_specs=[ANY] * (count + 2) + [VMEM] * 4,
        out_specs=[ANY] * 11 + [VMEM],
        scratch_shapes=[pltpu.VMEM((D, w), low) for w in cols]
        + [pltpu.VMEM((rows, D), low)] * 2
        + [
            pltpu.VMEM((rows, cols[0]), low),
            pltpu.VMEM((LINE * seq_dev, slot_len, slot_len), f32),
            pltpu.VMEM((rows, cols[2]), low),
            pltpu.VMEM((rows, cols[3]), low),
            pltpu.VMEM((rows, cols[1]), low),
            pltpu.VMEM((block_rows, D), low),
            pltpu.VMEM((2, block_rows, D), low),
            pltpu.VMEM((block_rows, D), low),
            pltpu.VMEM((2, 2, LINE, block_rows, feat), low),
            pltpu.VMEM((LINE, LINE, block_rows, feat), low),
            pltpu.VMEM((LINE, 2, block_rows, feat), low),
            pltpu.VMEM((LINE, slot_len, D), low),
            pltpu.VMEM((block_rows, cols[0]), f32),
            pltpu.VMEM((block_rows, cols[1]), f32),
            pltpu.VMEM((rows, 2), f32),
            pltpu.VMEM((5, 8, D), f32),
            pltpu.VMEM((8, cols[0] + cols[1]), f32),
            dma((count, LINE)),
            dma((count, LINE)),
            dma((count, LINE, peers)),
            dma((count, LINE, peers)),
            dma((count, LINE)),
            dma((count, LINE)),
            dma((2, 3)),
            dma((2, 3)),
            dma((2, 3)),
            dma((2, 3)),
            dma((count + 2, seq_dev)),
            dma(()),
            dma((2,)),
            dma((2, LINE)),
            dma((LINE,)),
            dma((LINE,)),
            dma((LINE,)),
            dma((LINE,)),
            dma((LINE, 2)),
            dma((LINE, 2)),
            dma((LINE,)),
            dma((LINE,)),
            dma((LINE,)),
            dma((LINE,)),
            dma((LINE, groups, pieces)),
            dma((LINE, groups, pieces)),
            dma((LINE, pieces)),
        ],
        compiler_params=pltpu.CompilerParams(
            collective_id=0, has_side_effects=True, vmem_limit_bytes=62 * 1024 * 1024
        ),
        name="gather_all",
    )(*weights, tokens, cotangent, vectors, biases, valid, turns)


def scatter_kernel(groups, cols, seq_dev, slot_len, rows_own, *refs):
    count = len(cols)
    f32, low = jnp.float32, jnp.bfloat16
    pick = refs[0]
    lefts_in = refs[1:3]
    rights_in = refs[3:5]
    near_ref, far_ref, s_ref = refs[5:8]
    done_own, done_got = refs[8:10], refs[10:12]
    early_ref = refs[12]
    mixed_ref, ssum_ref = refs[13:15]
    g_out = refs[15 : 15 + count]
    early_out, col_out, row_out = refs[15 + count : 18 + count]
    rest = refs[18 + count :]
    left_buf, right_a, right_b = rest[:3]
    g_own = rest[3 : 3 + count]
    g_got = rest[3 + count : 3 + 2 * count]
    (m_in, m_all, m_send, s_own, s_half, s_far, early_group, col_now, col_group, row_keep, row_turn) = rest[
        3 + 2 * count : 14 + 2 * count
    ]
    (here, half_s, half_r, far_s, far_r, fin_s, fin_r, mall_s, mall_r, mout_s, mout_r, gp_s, gp_r, gl_s, gl_r, eg_s,
     eg_r, el_s, el_r, es_s, es_r, cg_s, cg_r, cl_s, cl_r, cs_s, cs_r, rl_s, rl_r, keep_sem) = rest[14 + 2 * count :]
    me = Place(groups)
    c, g, k = me.line, me.group, me.core
    me.greet()
    sibling = me.at(c, g, me.other)
    feat = D // (2 * LINE)
    seqs = LINE * seq_dev
    rows = seqs * slot_len
    double = groups == 4
    sends = []

    def go(copy):
        copy.start()
        sends.append(copy)

    def to_group(step):
        return (g + step) % groups

    def from_group(step):
        return (g + groups - step) % groups

    def arrived(dst, send, recv):
        remote(dst, dst, send, recv, sibling).wait_recv()

    def add_rows(total, parts, count_rows, chunk):
        @pl.loop(0, count_rows // chunk)
        def body(i):
            at = pl.ds(pl.multiple_of(i * chunk, chunk), chunk)
            acc = parts[0](at)[...].astype(f32)
            for part in parts[1:]:
                acc = acc + part(at)[...].astype(f32)
            total(at)[...] = acc.astype(low)

    def load(src, dst, sem):
        copy = pltpu.make_async_copy(src, dst, sem)
        copy.start()
        return copy

    partner = c + 1 - 2 * (c % 2)
    beyond = (c + 2) % LINE
    for q, to in enumerate((partner, (partner + 2) % LINE)):
        go(remote(s_ref.at[to], s_half.at[q], half_s.at[q], half_r.at[q], me.at(partner, g, k)))
    got_one = load(lefts_in[0], left_buf.at[0], here.at[0])
    got_q = load(rights_in[0], right_b, here.at[1])
    got_done = []
    for q in range(2):
        got_done.append(load(done_own[q], g_own[2 + q].at[:, 0], here.at[2 + 2 * q]))
        got_done.append(load(done_got[q], g_got[2 + q], here.at[3 + 2 * q]))
    if double:
        got_two = load(lefts_in[1], left_buf.at[1], here.at[6])
        got_1 = load(rights_in[1], right_a, here.at[7])
    got_s = [load(s_ref.at[c], s_own.at[0], here.at[8]), load(s_ref.at[beyond], s_own.at[1], here.at[9])]
    got_m = [load(near_ref, m_in.at[0], here.at[10]), load(far_ref, m_in.at[1], here.at[11])]
    for step in range(1, groups):
        go(remote(early_ref, early_group.at[g], eg_s.at[step], eg_r.at[step], me.at(c, to_group(step), k)))
    early_group[g] = early_ref[...]

    per = 128 // rows_own

    def tile_products(m, left, right, tiles):
        lhs = jnp.concatenate(
            [left[:, pl.ds(pl.multiple_of((l * groups + p) * rows_own, 128), 128)] for l, p in tiles], 1
        )
        for n in range(1):
            at = slice(0, cols[m])
            out = lax.dot_general(lhs, right[:, at], (((0,), (0,)), ((), ())), preferred_element_type=f32).astype(low)
            for t, (l, p) in enumerate(tiles):
                for q in range(per):
                    row = t * 128 + q * rows_own
                    g_own[m][l, p + q, :, at] = out[row : row + rows_own]

    def send_group(m, step, act):
        to = to_group(step)
        copy = remote(
            g_own[m].at[:, to], g_got[m].at[step - 1], gp_s.at[m, step], gp_r.at[m, step], me.at(c, to, k)
        )
        getattr(copy, act)()

    across, beside, above = me.group_to(3), me.group_to(1), me.group_to(2)
    two_phase = groups == 4

    def phase_one(m, way, act):
        lines = pl.ds(0, 2) if way == 0 else pl.ds(2, 2)
        to = beside if way == 0 else above
        for q, block in enumerate((to, across)):
            copy = remote(
                g_own[m].at[lines, block], g_got[m].at[q, lines], gp_s.at[m, way * 2 + q], gp_r.at[m, way * 2 + q],
                me.at(c, to, k),
            )
            getattr(copy, act)()

    def phase_two(m, way, act):
        lines = pl.ds(0, 2) if way == 0 else pl.ds(2, 2)
        to = above if way == 0 else beside
        copy = remote(
            g_own[m].at[lines, to], g_got[m].at[2, lines], gp_s.at[m, 4 + way], gp_r.at[m, 4 + way], me.at(c, to, k)
        )
        getattr(copy, act)()

    def between_phases(m):
        for way in range(2):
            phase_one(m, way, "wait_recv")
            to = above if way == 0 else beside
            for line in (way * 2, way * 2 + 1):
                add_rows(
                    lambda at: g_own[m].at[line, to, at],
                    [lambda at: g_own[m].at[line, to, at], lambda at: g_got[m].at[1, line, at]],
                    rows_own,
                    16,
                )
            phase_two(m, way, "start")

    def products(left, pairs):
        if two_phase:

            @pl.loop(0, groups)
            def body(t):
                flip_x, flip_y = (t + 1) % 2, (3 - t) // 2 * (1 - t // 3)
                to = (g // 2 + flip_y) % 2 * 2 + (g % 2 + flip_x) % 2
                for m, right in pairs:
                    tile_products(m, left, right, [(l, to) for l in range(LINE)])
                    for way in range(2):

                        @pl.when(t == 2 - way)
                        def _():
                            phase_one(m, way, "start")
        else:

            @pl.loop(0, LINE)
            def body(l):
                for m, right in pairs:
                    tile_products(m, left, right, [(l, t * per) for t in range(4)])

            for m, _ in pairs:
                for step in range(1, groups):
                    send_group(m, step, "start")

    def sum_groups(m, first):
        got = range(groups - 1)
        if m < 2 and two_phase:
            for way in range(2):
                phase_two(m, way, "wait_recv")
            got = (0, 2)
        elif m < 2:
            for step in range(1, groups):
                arrived(g_got[m].at[step - 1], gp_s.at[m, step], gp_r.at[m, step])
        mine = g if m < 2 else 0
        width = pl.ds(pl.multiple_of(c * cols[m], 128), cols[m])
        total = jnp.zeros((8, cols[m]), f32)
        for step in (2, 1, 3, 0):
            line = me.line_to(step)

            def body(i, carry, line=line):
                at = pl.ds(pl.multiple_of(i * 16, 16), 16)
                acc = g_own[m][line, mine, at, :].astype(f32)
                for p in got:
                    acc = acc + g_got[m][p, line, at, :].astype(f32)
                g_own[m][line, mine, at, :] = acc.astype(low)
                square = acc * acc + eps_second
                row_keep[line, at, m : m + 1] = jnp.sum(square, 1, keepdims=True)
                return carry + square[:8] + square[8:]

            total = lax.fori_loop(0, rows_own // 16, body, total)
            src = g_own[m].at[line, mine]
            if step:
                go(remote(src, g_out[m].at[:, width], gl_s.at[m, step], gl_r.at[m, step], me.at(line, g, k)))
            else:
                keep.append(load(src, g_out[m].at[:, width], keep_sem.at[2 + m]))
        total = jnp.sum(total, 0, keepdims=True)
        for t in range(cols[m] // 128):
            col_now[first + t : first + t + 1, :] = total[:, t * 128 : (t + 1) * 128]

    keep = []
    row_keep[...] = jnp.zeros_like(row_keep)
    got_one.wait()
    got_q.wait()
    products(left_buf.at[0], ((0, right_b),))
    if not double:
        got_two = load(lefts_in[1], left_buf.at[0], here.at[6])
        got_1 = load(rights_in[1], right_a, here.at[7])
    got_two.wait()
    got_1.wait()
    products(left_buf.at[1 if double else 0], ((1, right_a),))

    firsts = []
    edge = 0
    for m in range(count):
        firsts.append(edge)
        edge += cols[m] // 128
    for copy in got_done:
        copy.wait()
    if two_phase:
        between_phases(0)
    sum_groups(3, firsts[3])
    sum_groups(2, firsts[2])
    if two_phase:
        between_phases(1)

    for q in range(2):
        got_s[q].wait()
        arrived(s_half.at[q], half_s.at[q], half_r.at[q])
        add_rows(
            lambda at: s_own.at[q, at], [lambda at: s_own.at[q, at], lambda at: s_half.at[q, at]], slot_len, 16
        )
    go(remote(s_own.at[1], s_far, far_s, far_r, me.at(beyond, g, k)))

    for copy in got_m:
        copy.wait()
    ours = pl.ds(g * seqs, seqs)
    for s in range(seqs):
        add_rows(
            lambda at: m_all.at[g * seqs + s, at],
            [lambda at: m_in.at[0, s, at], lambda at: m_in.at[1, s, at]],
            slot_len,
            64,
        )
    for step in range(1, groups):
        go(remote(m_all.at[ours], m_all.at[ours], mall_s.at[step], mall_r.at[step], me.at(c, to_group(step), k)))

    for step in range(1, groups):
        arrived(early_group.at[from_group(step)], eg_s.at[step], eg_r.at[step])
    acc = early_group[0]
    for i in range(1, groups):
        acc = acc + early_group[i]
    early_out[k, c] = acc
    for step in range(1, LINE):
        go(remote(early_out.at[k, c], early_out.at[k, c], el_s.at[step], el_r.at[step], me.at(me.line_to(step), g, k)))

    sum_groups(0, firsts[0])
    arrived(s_far, far_s, far_r)
    add_rows(lambda at: s_own.at[0, at], [lambda at: s_own.at[0, at], lambda at: s_far.at[at]], slot_len, 16)
    go(remote(s_own.at[0], ssum_ref.at[k], fin_s, fin_r, sibling))
    keep.append(load(s_own.at[0], ssum_ref.at[k], keep_sem.at[0]))
    sum_groups(1, firsts[1])

    for step in range(1, groups):
        go(remote(col_now, col_group.at[g], cg_s.at[step], cg_r.at[step], me.at(c, to_group(step), k)))
    col_group[g] = col_now[...]
    for step in (1, 2, 3, 0):
        line = me.line_to(step)
        row_turn[line] = jnp.transpose(row_keep[line])[:8]
        if step:
            go(remote(row_turn.at[line], row_out.at[k, c], rl_s.at[0, step], rl_r.at[0, step], me.at(line, g, k)))
        else:
            row_out[k, c] = row_turn[line]
        go(remote(row_turn.at[line], row_out.at[k, c], rl_s.at[1, step], rl_r.at[1, step], me.at(line, g, me.other)))
    for step in range(1, groups):
        arrived(col_group.at[from_group(step)], cg_s.at[step], cg_r.at[step])
    acc = col_group[0]
    for i in range(1, groups):
        acc = acc + col_group[i]
    col_out[k, c] = acc
    for step in range(1, LINE):
        go(remote(col_out.at[k, c], col_out.at[k, c], cl_s.at[step], cl_r.at[step], me.at(me.line_to(step), g, k)))
    for step in range(1, groups):
        arrived(m_all.at[pl.ds(from_group(step) * seqs, seqs)], mall_s.at[step], mall_r.at[step])
    mixed_cols = pl.ds(pl.multiple_of((c * 2 + k) * feat, 128), feat)
    for step in (1, 2, 3, 0):
        line = me.line_to(step)
        for s in range(seq_dev):
            m_send[line, s] = m_all[pick[line * seq_dev + s]]
        where = mixed_ref.at[:, :, mixed_cols]
        if step:
            go(remote(m_send.at[line], where, mout_s.at[0, step], mout_r.at[0, step], me.at(line, g, k)))
        else:
            keep.append(load(m_send.at[line], where, keep_sem.at[1]))
            go(remote(m_send.at[line], where, mout_s.at[1, 0], mout_r.at[1, 0], sibling))
    for step in range(1, LINE):
        arrived(early_out.at[k, me.line_from(step)], el_s.at[step], el_r.at[step])
    go(remote(early_out.at[k], early_out.at[k], es_s, es_r, sibling))
    for step in range(1, LINE):
        arrived(col_out.at[k, me.line_from(step)], cl_s.at[step], cl_r.at[step])
    go(remote(col_out.at[k], col_out.at[k], cs_s, cs_r, sibling))

    for step in range(1, LINE):
        where = mixed_ref.at[:, :, pl.ds(pl.multiple_of((me.line_from(step) * 2 + k) * feat, 128), feat)]
        arrived(where, mout_s.at[0, step], mout_r.at[0, step])
        go(remote(where, where, mout_s.at[1, step], mout_r.at[1, step], sibling))
    for m in range(count):
        for step in range(1, LINE):
            dst = g_out[m].at[:, pl.ds(pl.multiple_of(me.line_from(step) * cols[m], 128), cols[m])]
            arrived(dst, gl_s.at[m, step], gl_r.at[m, step])
    for step in range(LINE):
        source = me.line_from(step)
        dst = mixed_ref.at[:, :, pl.ds(pl.multiple_of((source * 2 + me.other) * feat, 128), feat)]
        arrived(dst, mout_s.at[1, step], mout_r.at[1, step])
        for core, way in ((k, 0), (me.other, 1)):
            if step or way:
                arrived(row_out.at[core, source], rl_s.at[way, step], rl_r.at[way, step])
    arrived(ssum_ref.at[me.other], fin_s, fin_r)
    arrived(early_out.at[me.other], es_s, es_r)
    arrived(col_out.at[me.other], cs_s, cs_r)
    for copy in sends:
        copy.wait_send()
    for m in range(2):
        if two_phase:
            for way in range(2):
                phase_one(m, way, "wait_send")
                phase_two(m, way, "wait_send")
        else:
            for step in range(1, groups):
                send_group(m, step, "wait_send")
    for copy in keep:
        copy.wait()


def scatter_all(groups, cols, seq_dev, rows_own, pick, lefts, rights, between):
    near, far, s_pair, *done, early = between
    slot_len = s_pair.shape[1]
    rows = lefts[0].shape[0]
    count = len(cols)
    feat = D // (2 * LINE)
    seqs = LINE * seq_dev
    blocks = (seqs, slot_len, feat)
    dma = pltpu.SemaphoreType.DMA
    f32, low = jnp.float32, jnp.bfloat16
    col_rows = sum(cols) // 128
    return pl.pallas_call(
        partial(scatter_kernel, groups, cols, seq_dev, slot_len, rows_own),
        out_shape=[
            jax.ShapeDtypeStruct((seq_dev, slot_len, D), low),
            jax.ShapeDtypeStruct((seq_dev, slot_len, D), low),
        ]
        + [jax.ShapeDtypeStruct((rows_own, LINE * width), low) for width in cols]
        + [
            jax.ShapeDtypeStruct((2, LINE) + early.shape, f32),
            jax.ShapeDtypeStruct((2, LINE, col_rows, 128), f32),
            jax.ShapeDtypeStruct((2, LINE, 8, 128), f32),
        ],
        in_specs=[SMEM] + [ANY] * 11 + [VMEM],
        out_specs=[ANY] * (2 + count) + [VMEM] * 3,
        scratch_shapes=[
            pltpu.VMEM((2 if groups == 4 else 1, rows, D), low),
            pltpu.VMEM((rows, cols[1]), low),
            pltpu.VMEM((rows, cols[0]), low),
        ]
        + [pltpu.VMEM((LINE, groups if m < 2 else 1, rows_own, width), low) for m, width in enumerate(cols)]
        + [pltpu.VMEM((groups - 1, LINE, rows_own, width), low) for width in cols]
        + [
            pltpu.VMEM((2, seqs, slot_len, feat), low),
            pltpu.VMEM((groups * seqs, slot_len, feat), low),
            pltpu.VMEM((LINE, seq_dev, slot_len, feat), low),
            pltpu.VMEM((2, slot_len, D), low),
            pltpu.VMEM((2, slot_len, D), low),
            pltpu.VMEM((slot_len, D), low),
            pltpu.VMEM((groups,) + early.shape, f32),
            pltpu.VMEM((col_rows, 128), f32),
            pltpu.VMEM((groups, col_rows, 128), f32),
            pltpu.VMEM((LINE, 128, 128), f32),
            pltpu.VMEM((LINE, 8, 128), f32),
            dma((12,)),
            dma((2,)),
            dma((2,)),
            dma(()),
            dma(()),
            dma(()),
            dma(()),
            dma((groups,)),
            dma((groups,)),
            dma((2, LINE)),
            dma((2, LINE)),
            dma((count, max(groups, 6))),
            dma((count, max(groups, 6))),
            dma((count, LINE)),
            dma((count, LINE)),
            dma((groups,)),
            dma((groups,)),
            dma((LINE,)),
            dma((LINE,)),
            dma(()),
            dma(()),
            dma((groups,)),
            dma((groups,)),
            dma((LINE,)),
            dma((LINE,)),
            dma(()),
            dma(()),
            dma((2, LINE)),
            dma((2, LINE)),
            dma((2 + count,)),
        ],
        compiler_params=pltpu.CompilerParams(
            collective_id=1, has_side_effects=True, vmem_limit_bytes=62 * 1024 * 1024
        ),
        name="scatter_all",
    )(pick, *lefts, *rights, near.reshape(blocks), far.reshape(blocks), s_pair, *done, early)


def prepare_kernel(groups, cols, seq_dev, slot_len, *refs):
    (spot, lengths, permutation, wq, w1, wd, w2, vectors, biases, rows_state) = refs[:10]
    lows = refs[10:14]
    valid, own_valid, all_vectors, all_biases, pick = refs[14:]
    f32 = jnp.float32
    for src, dst in zip((wq, w1, wd, w2), lows):
        dst[...] = src[...].astype(jnp.bfloat16)

    @pl.when(pl.program_id(0) == 0)
    def _():
        data, core = spot[0], spot[1]
        line, group = data // groups, data % groups
        times = lax.broadcasted_iota(jnp.int32, (slot_len, 1), 0)
        for place in range(LINE):
            for s in range(seq_dev):
                slot = (place * groups + group) * seq_dev + s
                at = place * seq_dev + s
                valid[at * slot_len : (at + 1) * slot_len, :] = jnp.where(times < lengths[slot], 1.0, 0.0)
                source = permutation[slot]
                chip = source // seq_dev
                pick[at] = (chip % groups) * (LINE * seq_dev) + (chip // groups) * seq_dev + source % seq_dev
        for s in range(seq_dev):
            own_valid[s * slot_len : (s + 1) * slot_len, :] = jnp.where(
                times < lengths[data * seq_dev + s], 1.0, 0.0
            )
        all_vectors[0:6, :] = vectors[...]
        all_vectors[6:8, :] = jnp.zeros((2, D), f32)
        lane = lax.broadcasted_iota(jnp.int32, (1, 128), 1)
        total = jnp.zeros((1, 128), f32)
        for m in range(4):
            total = total + jnp.where(lane == m, jnp.sum(rows_state[m : m + 1, :], 1, keepdims=True), 0.0)
        all_vectors[6:7, 0:128] = jnp.where(core == 0, total, jnp.zeros_like(total))
        all_biases[:, : cols[0]] = biases[:, pl.ds(pl.multiple_of(line * cols[0], 128), cols[0])]
        all_biases[:, cols[0] :] = biases[:, pl.ds(pl.multiple_of(LINE * cols[0] + line * cols[1], 128), cols[1])]


def prepare(groups, seq_dev, slot_len, spot, lengths, permutation, weights, vectors, biases, rows_state):
    f32, low = jnp.float32, jnp.bfloat16
    rows_own = weights[0].shape[0]
    cols = tuple(w.shape[1] // LINE for w in weights)
    tall = 32
    steps = rows_own // tall
    seqs = LINE * seq_dev

    def whole(shape):
        return pl.BlockSpec(shape, lambda i: (0,) * len(shape))

    blocks = [pl.BlockSpec((tall, w.shape[1]), lambda i: (i, 0)) for w in weights]
    return pl.pallas_call(
        partial(prepare_kernel, groups, cols, seq_dev, slot_len),
        grid=(steps,),
        out_shape=[jax.ShapeDtypeStruct(w.shape, low) for w in weights]
        + [
            jax.ShapeDtypeStruct((seqs * slot_len, 1), f32),
            jax.ShapeDtypeStruct((seq_dev * slot_len, 1), f32),
            jax.ShapeDtypeStruct((8, D), f32),
            jax.ShapeDtypeStruct((1, cols[0] + cols[1]), f32),
            jax.ShapeDtypeStruct((seqs,), jnp.int32),
        ],
        in_specs=[SMEM] * 3 + blocks + [whole(vectors.shape), whole(biases.shape), whole(rows_state.shape)],
        out_specs=blocks
        + [
            whole((seqs * slot_len, 1)),
            whole((seq_dev * slot_len, 1)),
            whole((8, D)),
            whole((1, cols[0] + cols[1])),
            SMEM,
        ],
        compiler_params=pltpu.CompilerParams(vmem_limit_bytes=60 * 1024 * 1024),
        name="prepare",
    )(spot, lengths, permutation, *weights, vectors, biases, rows_state)


def finish_kernel(order, cols, rows_own, *refs):
    f32, low = jnp.float32, jnp.bfloat16
    spot = refs[0]
    g_in, w_in = refs[1:5], refs[5:9]
    (s_sum, tokens, cotangent, own_valid, early, col_all, row_all, row_state, col_state, vectors, moments, biases,
     bias_moments) = refs[9:22]
    grads, news, copies = refs[22:26], refs[26:30], refs[30:34]
    (grad_tokens, row_new, col_new, norm_total, norm_moment_new, norm_new, bias_total, bias_moment_new,
     bias_new) = refs[34:43]
    row_factor, col_factor, turn = refs[43:]
    step = pl.program_id(0)
    widths = [w.shape[1] for w in w_in]
    edges = [sum(widths[:i]) for i in range(5)]
    tiles = D // 128

    @pl.when(step == 0)
    def _():
        core = spot[1]
        both = early[0, 0]
        rows_all = row_all[0, 0]
        mass_all = col_all[0, 0]
        for n in range(1, 2 * LINE):
            both = both + early[n // LINE, n % LINE]
            rows_all = rows_all + row_all[n // LINE, n % LINE]
            mass_all = mass_all + col_all[n // LINE, n % LINE]
        for r in range(6):
            for t in range(tiles):
                at = min(r, 4) * tiles + t
                norm_total[r : r + 1, t * 128 : (t + 1) * 128] = both[at : at + 1]
        grad = norm_total[...]
        moment = decay * moments[...] + (1.0 - decay) * (grad * grad + eps_second)
        norm_moment_new[...] = moment
        norm_new[...] = vectors[...] - rate_norm * grad * lax.rsqrt(moment)
        first = 5 * tiles
        parts = ((cols[0] // 128, 0), (cols[1] // 128, LINE * cols[0]))
        for line in range(LINE):
            at = first
            for count, base in parts:
                for t in range(count):
                    to = base + (line * count + t) * 128
                    bias_total[:, to : to + 128] = early[core, line, at : at + 1, :]
                    at += 1
        grad = bias_total[...]
        moment = decay * bias_moments[...] + (1.0 - decay) * (grad * grad + eps_second)
        bias_moment_new[...] = moment
        bias_new[...] = biases[...] - rate_vector * grad * lax.rsqrt(moment)
        at_row = first + (cols[0] + cols[1]) // 128
        full_cols = (3.0 * D, 1.0 * D, 1.0 * FF, 1.0 * FF)
        rates = (
            rate_scale / math.sqrt(D),
            rate_scale / math.sqrt(D // 8),
            rate_scale / math.sqrt(D),
            rate_scale / math.sqrt(FF),
        )
        turn[...] = jnp.zeros_like(turn)
        at = 0
        for m, i in enumerate(order):
            count = cols[m] // 128
            new = decay * row_state[i : i + 1, :] + (1.0 - decay) * (rows_all[m : m + 1, :rows_own] / full_cols[i])
            row_new[i : i + 1, :] = new
            mass = jnp.sum(jnp.sum(mass_all[at : at + count], 1, keepdims=True), 0, keepdims=True)
            mean = (decay * both[at_row : at_row + 1, i : i + 1] + (1.0 - decay) * (mass / full_cols[i])) / D
            turn[i : i + 1, :rows_own] = rates[i] * lax.rsqrt(new / mean)
            for line in range(LINE):
                for t in range(count):
                    to = edges[i] + (line * count + t) * 128
                    col_new[:, to : to + 128] = col_all[core, line, at + t : at + t + 1, :]
            at += count
        row_factor[...] = jnp.transpose(turn[...])
        new = decay * col_state[...] + (1.0 - decay) * (col_new[...] / D)
        col_new[...] = new
        col_factor[...] = lax.rsqrt(new)

    tall = w_in[0].shape[0]
    for half in range(tall // 16):
        rows = pl.ds(pl.multiple_of(step * tall + half * 16, 16), 16)
        part = slice(half * 16, half * 16 + 16)
        for i in range(4):
            factor = row_factor[rows, i : i + 1]
            for n in range(widths[i] // 1024):
                at = slice(n * 1024, (n + 1) * 1024)
                grad = g_in[i][part, at].astype(f32)
                new = w_in[i][part, at] - grad * factor * col_factor[:, edges[i] + n * 1024 : edges[i] + (n + 1) * 1024]
                grads[i][part, at] = grad
                news[i][part, at] = new
                copies[i][part, at] = new.astype(low)

    @pl.loop(0, tokens.shape[0] // 16)
    def body(j):
        at = pl.ds(pl.multiple_of(j * 16, 16), 16)
        x = tokens[at, :].astype(f32)
        centre = x - jnp.mean(x, -1, keepdims=True)
        scale = lax.rsqrt(jnp.mean(centre * centre, -1, keepdims=True) + eps_norm)
        unit = centre * scale
        flow = s_sum[at, :].astype(f32)
        through = flow - jnp.mean(flow, -1, keepdims=True) - unit * jnp.mean(flow * unit, -1, keepdims=True)
        grad_tokens[at, :] = (cotangent[at, :].astype(f32) * own_valid[at, :] + scale * through).astype(low)


def finish(order, spot, grads, weights, s_sum, tokens, cotangent, own_valid, *small):
    f32, low = jnp.float32, jnp.bfloat16
    rows_own = weights[0].shape[0]
    tall = 32
    steps = rows_own // tall
    cols = tuple(weights[i].shape[1] // LINE for i in order)
    rows = tokens.shape[0]
    row_state, col_state, vectors, _, biases = small[3:8]

    def whole(shape):
        return pl.BlockSpec(shape, lambda i: (0,) * len(shape))

    blocks = [pl.BlockSpec((tall, w.shape[1]), lambda i: (i, 0)) for w in weights]
    acts = pl.BlockSpec((rows // steps, D), lambda i: (i, 0))
    small_out = [row_state.shape, col_state.shape] + [vectors.shape] * 3 + [biases.shape] * 3
    return pl.pallas_call(
        partial(finish_kernel, order, cols, rows_own),
        grid=(steps,),
        out_shape=[jax.ShapeDtypeStruct(w.shape, f32) for w in weights] * 2
        + [jax.ShapeDtypeStruct(w.shape, low) for w in weights]
        + [jax.ShapeDtypeStruct((rows, D), low)]
        + [jax.ShapeDtypeStruct(shape, f32) for shape in small_out],
        in_specs=[SMEM]
        + blocks * 2
        + [acts] * 3
        + [pl.BlockSpec((rows // steps, 1), lambda i: (i, 0))]
        + [whole(a.shape) for a in small],
        out_specs=blocks * 3 + [acts] + [whole(shape) for shape in small_out],
        scratch_shapes=[
            pltpu.VMEM((128, 128), f32),
            pltpu.VMEM(col_state.shape, f32),
            pltpu.VMEM((128, 128), f32),
        ],
        compiler_params=pltpu.CompilerParams(vmem_limit_bytes=60 * 1024 * 1024),
        name="finish",
    )(spot, *grads, *weights, s_sum, tokens, cotangent, own_valid, *small)


def per_device(
    tokens,
    cotangent,
    lengths,
    permutation,
    w_qkv,
    w_dense,
    w_fc1,
    w_fc2,
    norm_vectors,
    split_biases,
    row_state,
    col_state,
    norm_moment,
    bias_moment,
):
    groups = lax.axis_size("dp") // LINE
    seq_dev, slot_len, width = tokens.shape
    rows_own = w_qkv.shape[0]
    head_dim = D // HEADS
    weights = (w_qkv, w_dense, w_fc1, w_fc2)
    order = (0, 2, 1, 3)
    cols = tuple(weights[i].shape[1] // LINE for i in order)
    spot = jnp.stack([lax.axis_index("dp"), lax.axis_index("tensor")]).astype(jnp.int32)
    *lows, valid, own_valid, vectors, biases, pick = prepare(
        groups, seq_dev, slot_len, spot, lengths, permutation, [weights[i] for i in order], norm_vectors,
        split_biases, row_state,
    )
    turns = jnp.asarray(turn_tables(slot_len, head_dim // 4, head_dim // 2))
    norm_one, norm_two, qkv_grad, pre_grad, *between = gather_all(
        groups, lows, tokens, cotangent, vectors, biases, valid, turns
    )
    mixed, s_sum, *outs = scatter_all(
        groups, cols, seq_dev, rows_own, pick, (norm_one, norm_two), (qkv_grad, pre_grad), between
    )
    grads = [outs[order.index(i)] for i in range(4)]
    early_all, col_all, row_all = outs[4:]
    results = finish(
        order, spot, grads, weights, s_sum.reshape(-1, width), tokens.reshape(-1, width),
        cotangent.reshape(-1, width), own_valid, early_all, col_all, row_all, row_state, col_state, norm_vectors,
        norm_moment, split_biases, bias_moment,
    )
    return (mixed, results[12].reshape(tokens.shape), *results[:12], *results[13:])


def solution(mesh):
    halves = P("dp", "tensor")
    split = P("tensor", None)
    in_specs = (
        P("dp", None, None),
        P("dp", None, None),
        P(),
        P(),
        halves,
        halves,
        halves,
        halves,
        P(),
        split,
        P(None, "dp"),
        split,
        P(),
        split,
    )
    out_specs = (
        (P("dp", None, None),) * 2
        + (halves,) * 12
        + (P(None, "dp"), split)
        + (P(),) * 3
        + (split,) * 3
    )
    return jax.shard_map(
        per_device, mesh=mesh, in_specs=in_specs, out_specs=out_specs, check_vma=False
    )
```

time: 517 us -> 452 us (0.87)
  other arithmetic: 33.8 us -> 0.66 us
  Pallas kernels: 466 us -> 449 us
  local copies, waits for them, and re-layouts: 10.1 us -> 1.15 us
  between operations: 6.49 us -> 0.71 us
    pallas_call x1, Pallas kernels: 209 us -> 158 us  [scatter_all(): pl.pallas_call(partial(scatter_kernel, groups, cols, seq_dev, slot_len, r...]
    convert_element_type x10 -> x0, other arithmetic: 23 us -> none  [the longest x4 13.8 us: per_device(): new.astype(low)]
    pallas_call x0 -> x2, Pallas kernels: none -> 22.1 us  [the longest x1 16.5 us: finish(): pl.pallas_call(partial(finish_kernel, order, cols, rows_own), grid=(steps...]
    pallas_call x1, Pallas kernels: 256 us -> 269 us  [gather_all(): pl.pallas_call(partial(gather_kernel, groups, cols, seq_dev, slot_len), o...]
where the time goes in v3:
time: 452 us; the launch traced here: 451 us
  Pallas kernels  449 us (99%)
    pallas_call x1, Pallas kernels, gather_all(): pl.pallas_call(partial(gather_kernel, groups, cols, seq_dev, slot_len), o...  269 us
    pallas_call x1, Pallas kernels, scatter_all(): pl.pallas_call(partial(scatter_kernel, groups, cols, seq_dev, slot_len, r...  158 us
    pallas_call x1, Pallas kernels, finish(): pl.pallas_call(partial(finish_kernel, order, cols, rows_own), grid=(steps...  16.5 us

profile of v3, /device:TPU:0, one launch (start us, length us, event | category | flops | bytes accessed | tf_op | source)
XLA Modules:
  0.0 451.2 jit_solution(7566197399311074668)
XLA Ops:
  0.7 0.7 pad_add_fusion.refs_0_
  1.3 5.6 %prepare.1 = (bf16[128,3072]{1,0:T(8,128)(2,1)}, bf16[128,4096]{1,0:T(8,128)(2,1)}, bf16[128,1024]{1,0:T(8,128)(2,1)}, bf16[128,4096]{1,0:T(8,128)(2,1)}, f32[15...) custom-call(s32[2]{0:T(128)} %pad_add_fusion.refs_0_, s32[32]{0:T(128)} %refs_1_.1, ...), custom_call_target="tpu_custom_call" | custom-call | tf_op jit(solution)/shard_map/prepare/pallas_call | solution.py:1231
  6.9 268.8 %gather_all.1 = (bf16[1536,2048]{1,0:T(8,128)(2,1)}, bf16[1536,2048]{1,0:T(8,128)(2,1)}, bf16[1536,768]{1,0:T(8,128)(2,1)}, bf16[1536,1024]{1,0:T(8,128)(2,1)}, ...) custom-call(bf16[128,3072]{1,0:T(8,128)(2,1)} %get-tuple-element.74., ...), custom_call_target="tpu_custom_call" | custom-call | tf_op jit(solution)/shard_map/gather_all/pallas_call | solution.py:705
  275.8 157.7 %scatter_all.1 = (bf16[2,192,2048]{2,1,0:T(8,128)(2,1)}, bf16[2,192,2048]{2,1,0:T(8,128)(2,1)}, bf16[128,3072]{1,0:T(8,128)(2,1)}, bf16[128,4096]{1,0:T(8,128)(2...) custom-call(s32[8]{0:T(128)} %get-tuple-element.73.refs_0_, ...), custom_call_target="tpu_custom_call" | custom-call | tf_op jit(solution)/shard_map/scatter_all/pallas_call | solution.py:1112
  433.5 0.0 copy-start
  433.5 16.5 %finish.1 = (f32[128,3072]{1,0:T(8,128)}, f32[128,1024]{1,0:T(8,128)}, f32[128,4096]{1,0:T(8,128)}, f32[128,4096]{1,0:T(8,128)}, f32[128,3072]{1,0:T(8,128)}, /*...) custom-call(s32[2]{0:T(128)} %pad_add_fusion.refs_0_, ...), custom_call_target="tpu_custom_call" | custom-call | tf_op jit(solution)/shard_map/finish/pallas_call | solution.py:1370
  450.0 0.0 copy-done
  450.0 1.1 copy.38
Async XLA Ops:
  433.5 16.6 %copy-start = (bf16[2,192,2048]{2,1,0:T(8,128)(2,1)S(1)}, bf16[2,192,2048]{2,1,0:T(8,128)(2,1)}, u32[]{:S(2)}) copy-start(bf16[2,192,2048]{2,1,0:T(8,128)(2,1)} %get-tuple-element.146) | copy-start | bytes 4718596

commit v4 on v3

--- a/solution.py
+++ b/solution.py
@@ -100,6 +100,17 @@
 
 def dot(left, right):
     return jnp.dot(left, right, preferred_element_type=jnp.float32)
+
+
+def turned(blocks):
+    eye = lax.broadcasted_iota(jnp.int32, (256, 256), 0) == lax.broadcasted_iota(jnp.int32, (256, 256), 1)
+    eye = jnp.where(eye, 1.0, 0.0).astype(jnp.bfloat16)
+    parts = []
+    for n in range(0, len(blocks), 2):
+        pair = jnp.concatenate(blocks[n : n + 2], 1)
+        part = lax.dot_general(eye, pair, (((1,), (1,)), ((), ())), preferred_element_type=jnp.float32)
+        parts.append(part.astype(jnp.bfloat16))
+    return jnp.concatenate(parts, 0)
 
 
 def gather_kernel(groups, cols, seq_dev, slot_len, *refs):
@@ -464,12 +475,10 @@
             tiles = [(l, to) for l in range(LINE)]
         else:
             tiles = [(i, t * per) for t in range(LINE)]
-        lhs = jnp.concatenate(
-            [ct_all[:, pl.ds(pl.multiple_of((l * groups + p) * rows_own, 128), 128)] for l, p in tiles], 1
-        )
+        lhs = turned([ct_all[:, pl.ds(pl.multiple_of((l * groups + p) * rows_own, 128), 128)] for l, p in tiles])
         first = 0
         for right in (attn_keep, hid_keep):
-            out = contract(lhs, right[...], ((0,), (0,))).astype(low)
+            out = dot(lhs, right[...]).astype(low)
             for n in range(right.shape[1] // part_cols):
                 nb = first + n
                 for t in range(LINE):
@@ -834,17 +843,17 @@
     beyond = (c + 2) % LINE
     for q, to in enumerate((partner, (partner + 2) % LINE)):
         go(remote(s_ref.at[to], s_half.at[q], half_s.at[q], half_r.at[q], me.at(partner, g, k)))
-    got_one = load(lefts_in[0], left_buf.at[0], here.at[0])
-    got_q = load(rights_in[0], right_b, here.at[1])
+    got_m = [load(near_ref, m_in.at[0], here.at[10]), load(far_ref, m_in.at[1], here.at[11])]
     got_done = []
     for q in range(2):
         got_done.append(load(done_own[q], g_own[2 + q].at[:, 0], here.at[2 + 2 * q]))
         got_done.append(load(done_got[q], g_got[2 + q], here.at[3 + 2 * q]))
+    got_two = load(lefts_in[1], left_buf.at[0], here.at[6])
+    got_1 = load(rights_in[1], right_a, here.at[7])
     if double:
-        got_two = load(lefts_in[1], left_buf.at[1], here.at[6])
-        got_1 = load(rights_in[1], right_a, here.at[7])
+        got_one = load(lefts_in[0], left_buf.at[1], here.at[0])
+        got_q = load(rights_in[0], right_b, here.at[1])
     got_s = [load(s_ref.at[c], s_own.at[0], here.at[8]), load(s_ref.at[beyond], s_own.at[1], here.at[9])]
-    got_m = [load(near_ref, m_in.at[0], here.at[10]), load(far_ref, m_in.at[1], here.at[11])]
     for step in range(1, groups):
         go(remote(early_ref, early_group.at[g], eg_s.at[step], eg_r.at[step], me.at(c, to_group(step), k)))
     early_group[g] = early_ref[...]
@@ -852,16 +861,12 @@
     per = 128 // rows_own
 
     def tile_products(m, left, right, tiles):
-        lhs = jnp.concatenate(
-            [left[:, pl.ds(pl.multiple_of((l * groups + p) * rows_own, 128), 128)] for l, p in tiles], 1
-        )
-        for n in range(1):
-            at = slice(0, cols[m])
-            out = lax.dot_general(lhs, right[:, at], (((0,), (0,)), ((), ())), preferred_element_type=f32).astype(low)
-            for t, (l, p) in enumerate(tiles):
-                for q in range(per):
-                    row = t * 128 + q * rows_own
-                    g_own[m][l, p + q, :, at] = out[row : row + rows_own]
+        lhs = turned([left[:, pl.ds(pl.multiple_of((l * groups + p) * rows_own, 128), 128)] for l, p in tiles])
+        out = dot(lhs, right[...]).astype(low)
+        for t, (l, p) in enumerate(tiles):
+            for q in range(per):
+                row = t * 128 + q * rows_own
+                g_own[m][l, p + q] = out[row : row + rows_own]
 
     def send_group(m, step, act):
         to = to_group(step)
@@ -966,38 +971,11 @@
 
     keep = []
     row_keep[...] = jnp.zeros_like(row_keep)
-    got_one.wait()
-    got_q.wait()
-    products(left_buf.at[0], ((0, right_b),))
-    if not double:
-        got_two = load(lefts_in[1], left_buf.at[0], here.at[6])
-        got_1 = load(rights_in[1], right_a, here.at[7])
-    got_two.wait()
-    got_1.wait()
-    products(left_buf.at[1 if double else 0], ((1, right_a),))
-
     firsts = []
     edge = 0
     for m in range(count):
         firsts.append(edge)
         edge += cols[m] // 128
-    for copy in got_done:
-        copy.wait()
-    if two_phase:
-        between_phases(0)
-    sum_groups(3, firsts[3])
-    sum_groups(2, firsts[2])
-    if two_phase:
-        between_phases(1)
-
-    for q in range(2):
-        got_s[q].wait()
-        arrived(s_half.at[q], half_s.at[q], half_r.at[q])
-        add_rows(
-            lambda at: s_own.at[q, at], [lambda at: s_own.at[q, at], lambda at: s_half.at[q, at]], slot_len, 16
-        )
-    go(remote(s_own.at[1], s_far, far_s, far_r, me.at(beyond, g, k)))
-
     for copy in got_m:
         copy.wait()
     ours = pl.ds(g * seqs, seqs)
@@ -1011,6 +989,30 @@
     for step in range(1, groups):
         go(remote(m_all.at[ours], m_all.at[ours], mall_s.at[step], mall_r.at[step], me.at(c, to_group(step), k)))
 
+    for copy in got_done:
+        copy.wait()
+    sum_groups(3, firsts[3])
+    sum_groups(2, firsts[2])
+    got_two.wait()
+    got_1.wait()
+    products(left_buf.at[0], ((1, right_a),))
+    if not double:
+        got_one = load(lefts_in[0], left_buf.at[0], here.at[0])
+        got_q = load(rights_in[0], right_b, here.at[1])
+
+    for q in range(2):
+        got_s[q].wait()
+        arrived(s_half.at[q], half_s.at[q], half_r.at[q])
+        add_rows(
+            lambda at: s_own.at[q, at], [lambda at: s_own.at[q, at], lambda at: s_half.at[q, at]], slot_len, 16
+        )
+    go(remote(s_own.at[1], s_far, far_s, far_r, me.at(beyond, g, k)))
+
+    got_one.wait()
+    got_q.wait()
+    products(left_buf.at[1 if double else 0], ((0, right_b),))
+    if two_phase:
+        between_phases(1)
     for step in range(1, groups):
         arrived(early_group.at[from_group(step)], eg_s.at[step], eg_r.at[step])
     acc = early_group[0]
@@ -1020,12 +1022,23 @@
     for step in range(1, LINE):
         go(remote(early_out.at[k, c], early_out.at[k, c], el_s.at[step], el_r.at[step], me.at(me.line_to(step), g, k)))
 
+    for step in range(1, groups):
+        arrived(m_all.at[pl.ds(from_group(step) * seqs, seqs)], mall_s.at[step], mall_r.at[step])
+    mixed_cols = pl.ds(pl.multiple_of((c * 2 + k) * feat, 128), feat)
+    for step in (1, 2, 3, 0):
+        line = me.line_to(step)
+        for s in range(seq_dev):
+            m_send[line, s] = m_all[pick[line * seq_dev + s]]
+        where = mixed_ref.at[:, :, mixed_cols]
+        if step:
+            go(remote(m_send.at[line], where, mout_s.at[0, step], mout_r.at[0, step], me.at(line, g, k)))
+        else:
+            keep.append(load(m_send.at[line], where, keep_sem.at[1]))
+            go(remote(m_send.at[line], where, mout_s.at[1, 0], mout_r.at[1, 0], sibling))
+    if two_phase:
+        between_phases(0)
+    sum_groups(1, firsts[1])
     sum_groups(0, firsts[0])
-    arrived(s_far, far_s, far_r)
-    add_rows(lambda at: s_own.at[0, at], [lambda at: s_own.at[0, at], lambda at: s_far.at[at]], slot_len, 16)
-    go(remote(s_own.at[0], ssum_ref.at[k], fin_s, fin_r, sibling))
-    keep.append(load(s_own.at[0], ssum_ref.at[k], keep_sem.at[0]))
-    sum_groups(1, firsts[1])
 
     for step in range(1, groups):
         go(remote(col_now, col_group.at[g], cg_s.at[step], cg_r.at[step], me.at(c, to_group(step), k)))
@@ -1046,19 +1059,10 @@
     col_out[k, c] = acc
     for step in range(1, LINE):
         go(remote(col_out.at[k, c], col_out.at[k, c], cl_s.at[step], cl_r.at[step], me.at(me.line_to(step), g, k)))
-    for step in range(1, groups):
-        arrived(m_all.at[pl.ds(from_group(step) * seqs, seqs)], mall_s.at[step], mall_r.at[step])
-    mixed_cols = pl.ds(pl.multiple_of((c * 2 + k) * feat, 128), feat)
-    for step in (1, 2, 3, 0):
-        line = me.line_to(step)
-        for s in range(seq_dev):
-            m_send[line, s] = m_all[pick[line * seq_dev + s]]
-        where = mixed_ref.at[:, :, mixed_cols]
-        if step:
-            go(remote(m_send.at[line], where, mout_s.at[0, step], mout_r.at[0, step], me.at(line, g, k)))
-        else:
-            keep.append(load(m_send.at[line], where, keep_sem.at[1]))
-            go(remote(m_send.at[line], where, mout_s.at[1, 0], mout_r.at[1, 0], sibling))
+    arrived(s_far, far_s, far_r)
+    add_rows(lambda at: s_own.at[0, at], [lambda at: s_own.at[0, at], lambda at: s_far.at[at]], slot_len, 16)
+    go(remote(s_own.at[0], ssum_ref.at[k], fin_s, fin_r, sibling))
+    keep.append(load(s_own.at[0], ssum_ref.at[k], keep_sem.at[0]))
     for step in range(1, LINE):
         arrived(early_out.at[k, me.line_from(step)], el_s.at[step], el_r.at[step])
     go(remote(early_out.at[k], early_out.at[k], es_s, es_r, sibling))

time: 452 us -> 449 us (level)
  no operation moved by 1% of the time
where the time goes in v4:
time: 449 us; the launch traced here: 448 us
  Pallas kernels  446 us (99%)
    pallas_call x1, Pallas kernels, gather_all(): pl.pallas_call(partial(gather_kernel, groups, cols, seq_dev, slot_len), o...  270 us
    pallas_call x1, Pallas kernels, scatter_all(): pl.pallas_call(partial(scatter_kernel, groups, cols, seq_dev, slot_len, r...  154 us
    pallas_call x1, Pallas kernels, finish(): pl.pallas_call(partial(finish_kernel, order, cols, rows_own), grid=(steps...  16.5 us

profile of v4, /device:TPU:0, one launch (start us, length us, event | category | flops | bytes accessed | tf_op | source)
XLA Modules:
  0.0 448.4 jit_solution(1482527505125570804)
XLA Ops:
  0.7 0.7 pad_add_fusion.refs_0_
  1.3 5.6 %prepare.1 = (bf16[128,3072]{1,0:T(8,128)(2,1)}, bf16[128,4096]{1,0:T(8,128)(2,1)}, bf16[128,1024]{1,0:T(8,128)(2,1)}, bf16[128,4096]{1,0:T(8,128)(2,1)}, f32[15...) custom-call(s32[2]{0:T(128)} %pad_add_fusion.refs_0_, s32[32]{0:T(128)} %refs_1_.1, ...), custom_call_target="tpu_custom_call" | custom-call | tf_op jit(solution)/shard_map/prepare/pallas_call | solution.py:1235
  6.9 269.7 %gather_all.1 = (bf16[1536,2048]{1,0:T(8,128)(2,1)}, bf16[1536,2048]{1,0:T(8,128)(2,1)}, bf16[1536,768]{1,0:T(8,128)(2,1)}, bf16[1536,1024]{1,0:T(8,128)(2,1)}, ...) custom-call(bf16[128,3072]{1,0:T(8,128)(2,1)} %get-tuple-element.74., ...), custom_call_target="tpu_custom_call" | custom-call | tf_op jit(solution)/shard_map/gather_all/pallas_call | solution.py:714
  276.6 154.0 %scatter_all.1 = (bf16[2,192,2048]{2,1,0:T(8,128)(2,1)}, bf16[2,192,2048]{2,1,0:T(8,128)(2,1)}, bf16[128,3072]{1,0:T(8,128)(2,1)}, bf16[128,4096]{1,0:T(8,128)(2...) custom-call(s32[8]{0:T(128)} %get-tuple-element.73.refs_0_, ...), custom_call_target="tpu_custom_call" | custom-call | tf_op jit(solution)/shard_map/scatter_all/pallas_call | solution.py:1116
  430.7 0.0 copy-start
  430.7 16.5 %finish.1 = (f32[128,3072]{1,0:T(8,128)}, f32[128,1024]{1,0:T(8,128)}, f32[128,4096]{1,0:T(8,128)}, f32[128,4096]{1,0:T(8,128)}, f32[128,3072]{1,0:T(8,128)}, /*...) custom-call(s32[2]{0:T(128)} %pad_add_fusion.refs_0_, ...), custom_call_target="tpu_custom_call" | custom-call | tf_op jit(solution)/shard_map/finish/pallas_call | solution.py:1374
  447.2 0.0 copy-done
  447.2 1.1 copy.38
Async XLA Ops:
  430.7 16.6 %copy-start = (bf16[2,192,2048]{2,1,0:T(8,128)(2,1)S(1)}, bf16[2,192,2048]{2,1,0:T(8,128)(2,1)}, u32[]{:S(2)}) copy-start(bf16[2,192,2048]{2,1,0:T(8,128)(2,1)} %get-tuple-element.146) | copy-start | bytes 4718596

commit v5 on v4

--- a/solution.py
+++ b/solution.py
@@ -119,16 +119,16 @@
     w_in = refs[:count]
     acts_in = refs[count : count + 2]
     vec_ref, bias_ref, valid_ref, turn_ref = refs[count + 2 : count + 6]
-    outs = refs[count + 6 : count + 18]
-    (n1_out, n2_out, qg_out, pg_out, near_out, far_out, s_out, gd_own, g2_own, gd_got, g2_got, early_ref) = outs
-    rest = refs[count + 18 :]
+    outs = refs[count + 6 : count + 19]
+    (n1_out, n2_out, qg_out, pg_out, near_out, far_out, s_out, s_far, gd_own, g2_own, gd_got, g2_got, early_ref) = outs
+    rest = refs[count + 19 :]
     w_out = rest[:count]
     acts_out = rest[count : count + 2]
     (qkv_keep, prob_keep, attn_keep, hid_keep, pg_keep, one_buf, two_buf, back_buf, m_buf, m_got, m_half, s_got,
-     qkv_now, pre_now, stat_keep, norm_acc, bias_acc) = rest[count + 2 : count + 19]
+     s_half, qkv_now, pre_now, stat_keep, norm_acc, bias_acc) = rest[count + 2 : count + 20]
     (one_s, one_r, two_s, two_r, three_s, three_r, row_s, row_r, sib_s, sib_r, here, out_a, out_b,
-     out_d, msib_s, msib_r, ssib_s, ssib_r, half_s, half_r, far_s, far_r, near_sem, s_here, gp_s, gp_r,
-     g_here) = rest[count + 19 :]
+     out_d, msib_s, msib_r, ssib_s, ssib_r, half_s, half_r, far_s, far_r, near_sem, s_here, s1_s, s1_r,
+     s2_s, s2_r, gp_s, gp_r, g_here) = rest[count + 20 :]
     me = Place(groups)
     c, g, k = me.line, me.group, me.core
     me.greet()
@@ -464,6 +464,10 @@
     pieces = (cols[2] + cols[3]) // part_cols
     dense_pieces = cols[2] // part_cols
 
+    def own_spot(t, nb):
+        row, column = divmod(t * pieces + nb, D // part_cols)
+        return slice(row * 128, (row + 1) * 128), slice(column * part_cols, (column + 1) * part_cols)
+
     def out_group(i):
         flip_x, flip_y = 1 - i % 2, 1 - i // 2
         return (g // 2 + flip_y) % 2 * 2 + (g % 2 + flip_x) % 2
@@ -481,10 +485,23 @@
             out = dot(lhs, right[...]).astype(low)
             for n in range(right.shape[1] // part_cols):
                 nb = first + n
-                for t in range(LINE):
-                    m_buf[slot, nb // fits, t, (nb % fits) * 128 : (nb % fits + 1) * 128, :] = out[
-                        t * 128 : (t + 1) * 128, n * part_cols : (n + 1) * part_cols
-                    ]
+                part = out[:, n * part_cols : (n + 1) * part_cols]
+
+                @pl.when((i < groups - 1) | (not near))
+                def _(part=part, nb=nb):
+                    for t in range(LINE):
+                        m_buf[slot, nb // fits, t, (nb % fits) * 128 : (nb % fits + 1) * 128, :] = part[
+                            t * 128 : (t + 1) * 128
+                        ]
+
+                if near:
+
+                    @pl.when(i == groups - 1)
+                    def _(part=part, nb=nb):
+                        for t in range(LINE):
+                            rows, at = own_spot(t, nb)
+                            one_buf[rows, at] = part[t * 128 : (t + 1) * 128]
+
             first += right.shape[1] // part_cols
 
     def out_piece(i, nb, to):
@@ -512,10 +529,19 @@
 
     def out_keep(i, act):
         for nb in range(pieces):
-            copy = pltpu.make_async_copy(
-                out_piece(i, nb, g), out_place((gd_own, g2_own), i, nb, None), g_here.at[0 if near else i, nb]
-            )
-            getattr(copy, act)()
+            if near:
+                for t in range(LINE):
+                    rows, at = own_spot(t, nb)
+                    dst = out_place((gd_own, g2_own), i, nb, None)
+                    copy = pltpu.make_async_copy(
+                        one_buf.at[pl.ds(rows.start, 128), pl.ds(at.start, part_cols)], dst.at[t], g_here.at[t, nb]
+                    )
+                    getattr(copy, act)()
+            else:
+                copy = pltpu.make_async_copy(
+                    out_piece(i, nb, g), out_place((gd_own, g2_own), i, nb, None), g_here.at[i, nb]
+                )
+                getattr(copy, act)()
 
     def out_sends(i, act):
         local = "wait" if act == SENT else act
@@ -533,29 +559,44 @@
                 out_send(i, step, act)
             out_keep(i, local)
 
+    def line_at(i):
+        first = partner + (c - partner) * (i % 2)
+        return (first + 2 * (1 - i // 2)) % LINE
+
     def pair_s(i, act):
-        line = (c + i) % LINE
         rows = pl.ds(pl.multiple_of(me.other * slot_len, 32), slot_len)
-        copy = remote(two_buf.at[i % 2, rows], s_got.at[line], ssib_s.at[i], ssib_r.at[i], sibling)
+        copy = remote(two_buf.at[i % 2, rows], s_got.at[i], ssib_s.at[i], ssib_r.at[i], sibling)
         getattr(copy, act)()
 
     def put_s(i, act):
-        line = (c + i) % LINE
-        rows = pl.ds(pl.multiple_of(k * slot_len, 32), slot_len)
-        getattr(pltpu.make_async_copy(two_buf.at[i % 2, rows], s_out.at[line], s_here.at[i]), act)()
+        getattr(pltpu.make_async_copy(s_got.at[i], s_out.at[i - 2], s_here.at[i]), act)()
+
+    def s_one(act):
+        getattr(remote(s_got.at[0], s_half, s1_s, s1_r, me.at(partner, g, k)), act)()
+
+    def s_two(act):
+        getattr(remote(s_got.at[1], s_far, s2_s, s2_r, me.at(beyond, g, k)), act)()
 
     def finish_s(i):
-        line = (c + i) % LINE
         pair_s(i, "wait_recv")
+        if i == 1:
+            s_one("wait_recv")
 
         @pl.loop(0, slot_len // chunk)
         def add(j):
             at = pl.ds(pl.multiple_of(k * slot_len + j * chunk, chunk), chunk)
             to = pl.ds(pl.multiple_of(j * chunk, chunk), chunk)
-            total = two_buf[i % 2, at, :].astype(f32) + s_got[line, to, :].astype(f32)
-            two_buf[i % 2, at, :] = total.astype(low)
-
-        put_s(i, START)
+            total = two_buf[i % 2, at, :].astype(f32) + s_got[i, to, :].astype(f32)
+            if i == 1:
+                total = total + s_half[to, :].astype(f32)
+            s_got[i, to, :] = total.astype(low)
+
+        if i == 0:
+            s_one(START)
+        elif i == 1:
+            s_two(START)
+        else:
+            put_s(i, START)
 
     def put_rest(line, act):
         rows = pl.ds(pl.multiple_of(line * block_rows, 128), block_rows)
@@ -564,7 +605,7 @@
 
     @pl.loop(0, LINE)
     def backward(i):
-        line = (c + i) % LINE
+        line = line_at(i)
         base = pl.multiple_of(line * block_rows, 128)
         whole = pl.ds(base, block_rows)
         slot = i % 2
@@ -577,7 +618,7 @@
         def _():
             pair_m(LINE - 1, SENT)
 
-        @pl.when(i >= 2)
+        @pl.when((i == 2) if near else (i >= 2))
         def _():
             out_sends(i - 2, SENT)
 
@@ -587,6 +628,12 @@
         @pl.when(i == 0)
         def _():
             pair_add(LINE - 1)
+
+        for late in (0, 2):
+
+            @pl.when(i == late + 1)
+            def _(late=late):
+                finish_s(late)
 
         @pl.when((i == 1) | (i == 2))
         def _():
@@ -598,7 +645,7 @@
         attn_grad = dot(back_buf[...], wd[...]).astype(low)
         pre_now[...] = dot(back_buf[...], w2[...])
 
-        @pl.when(i == 0)
+        @pl.when(i == LINE - 1)
         def _():
             rows = pl.ds(pl.multiple_of(k * slot_len, 32), slot_len)
             total = jnp.sum(back_buf[rows, :].astype(f32).reshape(slot_len // 8, 8, D), 0)
@@ -641,7 +688,6 @@
         @pl.when(i >= 2)
         def _():
             pair_s(i - 2, SENT)
-            put_s(i - 2, "wait")
 
         @pl.loop(0, ways)
         def inputs(j):
@@ -655,9 +701,9 @@
 
         pair_s(i, START)
 
-        @pl.when(i >= 1)
+        @pl.when(i == 2)
         def _():
-            finish_s(i - 1)
+            finish_s(1)
 
     finish_s(LINE - 1)
     for r in range(5):
@@ -678,7 +724,11 @@
     for i in (LINE - 2, LINE - 1):
         pair_s(i, SENT)
         put_s(i, "wait")
+    for i in range(1 if near else 2, LINE):
         out_sends(i, SENT)
+    s_one(SENT)
+    s_two(SENT)
+    s_two("wait_recv")
     for step in range(1, groups):
         for nb in range(pieces):
             for i in range(1 if near else LINE):
@@ -717,7 +767,8 @@
         + [
             jax.ShapeDtypeStruct((LINE, block_rows, feat), low),
             jax.ShapeDtypeStruct((LINE, block_rows, feat), low),
-            jax.ShapeDtypeStruct((LINE, slot_len, D), low),
+            jax.ShapeDtypeStruct((2, slot_len, D), low),
+            jax.ShapeDtypeStruct((slot_len, D), low),
             jax.ShapeDtypeStruct((LINE, rows_own, cols[2]), low),
             jax.ShapeDtypeStruct((LINE, rows_own, cols[3]), low),
             jax.ShapeDtypeStruct((groups - 1, LINE, rows_own, cols[2]), low),
@@ -725,7 +776,7 @@
             jax.ShapeDtypeStruct((early_rows, 128), f32),
         ],
         in_specs=[ANY] * (count + 2) + [VMEM] * 4,
-        out_specs=[ANY] * 11 + [VMEM],
+        out_specs=[ANY] * 12 + [VMEM],
         scratch_shapes=[pltpu.VMEM((D, w), low) for w in cols]
         + [pltpu.VMEM((rows, D), low)] * 2
         + [
@@ -741,6 +792,7 @@
             pltpu.VMEM((LINE, LINE, block_rows, feat), low),
             pltpu.VMEM((LINE, 2, block_rows, feat), low),
             pltpu.VMEM((LINE, slot_len, D), low),
+            pltpu.VMEM((slot_len, D), low),
             pltpu.VMEM((block_rows, cols[0]), f32),
             pltpu.VMEM((block_rows, cols[1]), f32),
             pltpu.VMEM((rows, 2), f32),
@@ -770,6 +822,10 @@
             dma((LINE,)),
             dma((LINE,)),
             dma((LINE,)),
+            dma(()),
+            dma(()),
+            dma(()),
+            dma(()),
             dma((LINE, groups, pieces)),
             dma((LINE, groups, pieces)),
             dma((LINE, pieces)),
@@ -787,20 +843,20 @@
     pick = refs[0]
     lefts_in = refs[1:3]
     rights_in = refs[3:5]
-    near_ref, far_ref, s_ref = refs[5:8]
-    done_own, done_got = refs[8:10], refs[10:12]
-    early_ref = refs[12]
-    mixed_ref, ssum_ref = refs[13:15]
-    g_out = refs[15 : 15 + count]
-    early_out, col_out, row_out = refs[15 + count : 18 + count]
-    rest = refs[18 + count :]
+    near_ref, far_ref, s_ref, s_far_ref = refs[5:9]
+    done_own, done_got = refs[9:11], refs[11:13]
+    early_ref = refs[13]
+    mixed_ref, ssum_ref = refs[14:16]
+    g_out = refs[16 : 16 + count]
+    early_out, col_out, row_out = refs[16 + count : 19 + count]
+    rest = refs[19 + count :]
     left_buf, right_a, right_b = rest[:3]
     g_own = rest[3 : 3 + count]
     g_got = rest[3 + count : 3 + 2 * count]
     (m_in, m_all, m_send, s_own, s_half, s_far, early_group, col_now, col_group, row_keep, row_turn) = rest[
         3 + 2 * count : 14 + 2 * count
     ]
-    (here, half_s, half_r, far_s, far_r, fin_s, fin_r, mall_s, mall_r, mout_s, mout_r, gp_s, gp_r, gl_s, gl_r, eg_s,
+    (here, half_s, half_r, fin_s, fin_r, mall_s, mall_r, mout_s, mout_r, gp_s, gp_r, gl_s, gl_r, eg_s,
      eg_r, el_s, el_r, es_s, es_r, cg_s, cg_r, cl_s, cl_r, cs_s, cs_r, rl_s, rl_r, keep_sem) = rest[14 + 2 * count :]
     me = Place(groups)
     c, g, k = me.line, me.group, me.core
@@ -840,9 +896,7 @@
         return copy
 
     partner = c + 1 - 2 * (c % 2)
-    beyond = (c + 2) % LINE
-    for q, to in enumerate((partner, (partner + 2) % LINE)):
-        go(remote(s_ref.at[to], s_half.at[q], half_s.at[q], half_r.at[q], me.at(partner, g, k)))
+    go(remote(s_ref.at[0], s_half, half_s, half_r, me.at(partner, g, k)))
     got_m = [load(near_ref, m_in.at[0], here.at[10]), load(far_ref, m_in.at[1], here.at[11])]
     got_done = []
     for q in range(2):
@@ -853,7 +907,7 @@
     if double:
         got_one = load(lefts_in[0], left_buf.at[1], here.at[0])
         got_q = load(rights_in[0], right_b, here.at[1])
-    got_s = [load(s_ref.at[c], s_own.at[0], here.at[8]), load(s_ref.at[beyond], s_own.at[1], here.at[9])]
+    got_s = [load(s_ref.at[1], s_own, here.at[8]), load(s_far_ref, s_far, here.at[9])]
     for step in range(1, groups):
         go(remote(early_ref, early_group.at[g], eg_s.at[step], eg_r.at[step], me.at(c, to_group(step), k)))
     early_group[g] = early_ref[...]
@@ -1000,14 +1054,17 @@
         got_one = load(lefts_in[0], left_buf.at[0], here.at[0])
         got_q = load(rights_in[0], right_b, here.at[1])
 
-    for q in range(2):
-        got_s[q].wait()
-        arrived(s_half.at[q], half_s.at[q], half_r.at[q])
-        add_rows(
-            lambda at: s_own.at[q, at], [lambda at: s_own.at[q, at], lambda at: s_half.at[q, at]], slot_len, 16
-        )
-    go(remote(s_own.at[1], s_far, far_s, far_r, me.at(beyond, g, k)))
-
+    for copy in got_s:
+        copy.wait()
+    arrived(s_half, half_s, half_r)
+    add_rows(
+        lambda at: s_own.at[at],
+        [lambda at: s_own.at[at], lambda at: s_half.at[at], lambda at: s_far.at[at]],
+        slot_len,
+        16,
+    )
+    go(remote(s_own, ssum_ref.at[k], fin_s, fin_r, sibling))
+    keep.append(load(s_own, ssum_ref.at[k], keep_sem.at[0]))
     got_one.wait()
     got_q.wait()
     products(left_buf.at[1 if double else 0], ((0, right_b),))
@@ -1059,10 +1116,6 @@
     col_out[k, c] = acc
     for step in range(1, LINE):
         go(remote(col_out.at[k, c], col_out.at[k, c], cl_s.at[step], cl_r.at[step], me.at(me.line_to(step), g, k)))
-    arrived(s_far, far_s, far_r)
-    add_rows(lambda at: s_own.at[0, at], [lambda at: s_own.at[0, at], lambda at: s_far.at[at]], slot_len, 16)
-    go(remote(s_own.at[0], ssum_ref.at[k], fin_s, fin_r, sibling))
-    keep.append(load(s_own.at[0], ssum_ref.at[k], keep_sem.at[0]))
     for step in range(1, LINE):
         arrived(early_out.at[k, me.line_from(step)], el_s.at[step], el_r.at[step])
     go(remote(early_out.at[k], early_out.at[k], es_s, es_r, sibling))
@@ -1103,7 +1156,7 @@
 
 
 def scatter_all(groups, cols, seq_dev, rows_own, pick, lefts, rights, between):
-    near, far, s_pair, *done, early = between
+    near, far, s_pair, s_far, *done, early = between
     slot_len = s_pair.shape[1]
     rows = lefts[0].shape[0]
     count = len(cols)
@@ -1125,7 +1178,7 @@
             jax.ShapeDtypeStruct((2, LINE, col_rows, 128), f32),
             jax.ShapeDtypeStruct((2, LINE, 8, 128), f32),
         ],
-        in_specs=[SMEM] + [ANY] * 11 + [VMEM],
+        in_specs=[SMEM] + [ANY] * 12 + [VMEM],
         out_specs=[ANY] * (2 + count) + [VMEM] * 3,
         scratch_shapes=[
             pltpu.VMEM((2 if groups == 4 else 1, rows, D), low),
@@ -1138,8 +1191,8 @@
             pltpu.VMEM((2, seqs, slot_len, feat), low),
             pltpu.VMEM((groups * seqs, slot_len, feat), low),
             pltpu.VMEM((LINE, seq_dev, slot_len, feat), low),
-            pltpu.VMEM((2, slot_len, D), low),
-            pltpu.VMEM((2, slot_len, D), low),
+            pltpu.VMEM((slot_len, D), low),
+            pltpu.VMEM((slot_len, D), low),
             pltpu.VMEM((slot_len, D), low),
             pltpu.VMEM((groups,) + early.shape, f32),
             pltpu.VMEM((col_rows, 128), f32),
@@ -1147,8 +1200,6 @@
             pltpu.VMEM((LINE, 128, 128), f32),
             pltpu.VMEM((LINE, 8, 128), f32),
             dma((12,)),
-            dma((2,)),
-            dma((2,)),
             dma(()),
             dma(()),
             dma(()),
@@ -1181,7 +1232,7 @@
             collective_id=1, has_side_effects=True, vmem_limit_bytes=62 * 1024 * 1024
         ),
         name="scatter_all",
-    )(pick, *lefts, *rights, near.reshape(blocks), far.reshape(blocks), s_pair, *done, early)
+    )(pick, *lefts, *rights, near.reshape(blocks), far.reshape(blocks), s_pair, s_far, *done, early)
 
 
 def prepare_kernel(groups, cols, seq_dev, slot_len, *refs):

time: 449 us -> 456 us (1.016)
  Pallas kernels: 446 us -> 454 us
    pallas_call x1, Pallas kernels: 270 us -> 292 us  [gather_all(): pl.pallas_call(partial(gather_kernel, groups, cols, seq_dev, slot_len), o...]
    pallas_call x1, Pallas kernels: 154 us -> 140 us  [scatter_all(): pl.pallas_call(partial(scatter_kernel, groups, cols, seq_dev, slot_len, r...]
where the time goes in v5:
time: 456 us
  Pallas kernels  454 us (100%)
    pallas_call x1, Pallas kernels, gather_all(): pl.pallas_call(partial(gather_kernel, groups, cols, seq_dev, slot_len), o...  292 us
    pallas_call x1, Pallas kernels, scatter_all(): pl.pallas_call(partial(scatter_kernel, groups, cols, seq_dev, slot_len, r...  140 us
    pallas_call x1, Pallas kernels, finish(): pl.pallas_call(partial(finish_kernel, order, cols, rows_own), grid=(steps...  16.5 us

profile of v5, /device:TPU:0, one launch (start us, length us, event | category | flops | bytes accessed | tf_op | source)
XLA Modules:
  0.0 456.2 jit_solution(6074045743378637212)
XLA Ops:
  0.7 0.6 pad_add_fusion.refs_0_
  1.2 5.6 %prepare.1 = (bf16[128,3072]{1,0:T(8,128)(2,1)}, bf16[128,4096]{1,0:T(8,128)(2,1)}, bf16[128,1024]{1,0:T(8,128)(2,1)}, bf16[128,4096]{1,0:T(8,128)(2,1)}, f32[15...) custom-call(s32[2]{0:T(128)} %pad_add_fusion.refs_0_, s32[32]{0:T(128)} %refs_1_.1, ...), custom_call_target="tpu_custom_call" | custom-call | tf_op jit(solution)/shard_map/prepare/pallas_call | solution.py:1286
  6.8 291.9 %gather_all.1 = (bf16[1536,2048]{1,0:T(8,128)(2,1)}, bf16[1536,2048]{1,0:T(8,128)(2,1)}, bf16[1536,768]{1,0:T(8,128)(2,1)}, bf16[1536,1024]{1,0:T(8,128)(2,1)}, ...) custom-call(bf16[128,3072]{1,0:T(8,128)(2,1)} %get-tuple-element.75., ...), custom_call_target="tpu_custom_call" | custom-call | tf_op jit(solution)/shard_map/gather_all/pallas_call | solution.py:764
  298.8 139.7 %scatter_all.1 = (bf16[2,192,2048]{2,1,0:T(8,128)(2,1)}, bf16[2,192,2048]{2,1,0:T(8,128)(2,1)}, bf16[128,3072]{1,0:T(8,128)(2,1)}, bf16[128,4096]{1,0:T(8,128)(2...) custom-call(s32[8]{0:T(128)} %get-tuple-element.74.refs_0_, ...), custom_call_target="tpu_custom_call" | custom-call | tf_op jit(solution)/shard_map/scatter_all/pallas_call | solution.py:1169
  438.5 0.0 copy-start
  438.5 16.5 %finish.1 = (f32[128,3072]{1,0:T(8,128)}, f32[128,1024]{1,0:T(8,128)}, f32[128,4096]{1,0:T(8,128)}, f32[128,4096]{1,0:T(8,128)}, f32[128,3072]{1,0:T(8,128)}, /*...) custom-call(s32[2]{0:T(128)} %pad_add_fusion.refs_0_, ...), custom_call_target="tpu_custom_call" | custom-call | tf_op jit(solution)/shard_map/finish/pallas_call | solution.py:1425
  455.1 0.0 copy-done
  455.1 1.1 copy.38
Async XLA Ops:
  438.5 16.6 %copy-start = (bf16[2,192,2048]{2,1,0:T(8,128)(2,1)S(1)}, bf16[2,192,2048]{2,1,0:T(8,128)(2,1)}, u32[]{:S(2)}) copy-start(bf16[2,192,2048]{2,1,0:T(8,128)(2,1)} %get-tuple-element.148) | copy-start | bytes 4718596

commit v6 on v4

--- a/solution.py
+++ b/solution.py
@@ -455,6 +455,9 @@
         def _():
             pair_add(i - 1)
 
+    pair_add(LINE - 1)
+    pair_m(LINE - 2, SENT)
+    pair_m(LINE - 1, SENT)
     local_acts(1, "wait")
     arrive_sibling(1)
 
@@ -468,8 +471,12 @@
         flip_x, flip_y = 1 - i % 2, 1 - i // 2
         return (g // 2 + flip_y) % 2 * 2 + (g % 2 + flip_x) % 2
 
+    def flat_piece(i, t, nb):
+        row, column = divmod(t * pieces + nb, D // part_cols)
+        at = (pl.ds(row * 128, 128), pl.ds(column * part_cols, part_cols))
+        return one_buf.at[at] if i == 2 else two_buf.at[(1,) + at]
+
     def out_products(i):
-        slot = i % 2
         if near:
             to = out_group(i)
             tiles = [(l, to) for l in range(LINE)]
@@ -482,56 +489,51 @@
             for n in range(right.shape[1] // part_cols):
                 nb = first + n
                 for t in range(LINE):
-                    m_buf[slot, nb // fits, t, (nb % fits) * 128 : (nb % fits + 1) * 128, :] = out[
-                        t * 128 : (t + 1) * 128, n * part_cols : (n + 1) * part_cols
-                    ]
+                    part = out[t * 128 : (t + 1) * 128, n * part_cols : (n + 1) * part_cols]
+                    if near and i >= 2:
+                        flat_piece(i, t, nb)[...] = part
+                    else:
+                        m_buf[i % 2, nb // fits, t, (nb % fits) * 128 : (nb % fits + 1) * 128, :] = part
             first += right.shape[1] // part_cols
 
-    def out_piece(i, nb, to):
-        row = (nb % fits) * 128
-        if near:
-            return m_buf.at[i % 2, nb // fits, :, pl.ds(row, 128), :]
-        return m_buf.at[i % 2, nb // fits, to // per, pl.ds(pl.multiple_of(row + (to % per) * rows_own, 32), rows_own), :]
-
-    def out_place(refs, i, nb, step):
+    def out_place(refs, nb, step):
         ref, n = (refs[0], nb) if nb < dense_pieces else (refs[1], nb - dense_pieces)
         at = pl.ds(n * part_cols, part_cols)
         if step is not None:
             ref = ref.at[step - 1]
-        return ref.at[:, :, at] if near else ref.at[i, :, at]
-
-    def out_send(i, step, act):
-        to = out_group(i) if near else (g + step) % groups
+        return ref.at[:, :, at]
+
+    def out_copies(i, step):
+        to = g if step is None else (out_group(i) if near else (g + step) % groups)
         for nb in range(pieces):
-            sem = (0 if near else i, step, nb)
-            copy = remote(
-                out_piece(i, nb, to), out_place((gd_got, g2_got), i, nb, step), gp_s.at[sem], gp_r.at[sem],
-                me.at(c, to, k),
-            )
-            getattr(copy, act)()
-
-    def out_keep(i, act):
-        for nb in range(pieces):
-            copy = pltpu.make_async_copy(
-                out_piece(i, nb, g), out_place((gd_own, g2_own), i, nb, None), g_here.at[0 if near else i, nb]
-            )
-            getattr(copy, act)()
+            dst = out_place((gd_own, g2_own) if step is None else (gd_got, g2_got), nb, step)
+            row = (nb % fits) * 128
+            if near and i < 2:
+                yield m_buf.at[i % 2, nb // fits, :, pl.ds(row, 128), :], dst, (0, nb)
+            elif near:
+                for t in range(LINE):
+                    yield flat_piece(i, t, nb), dst.at[t], (t, nb)
+            else:
+                rows = pl.ds(pl.multiple_of(row + (to % per) * rows_own, 32), rows_own)
+                yield m_buf.at[i % 2, nb // fits, to // per, rows, :], dst.at[i], (i, nb)
 
     def out_sends(i, act):
-        local = "wait" if act == SENT else act
-        if near:
-
-            @pl.when(i < groups - 1)
-            def _():
-                out_send(i, groups - 1 - i, act)
-
-            @pl.when(i == groups - 1)
-            def _():
-                out_keep(i, local)
-        else:
-            for step in range(1, groups):
-                out_send(i, step, act)
-            out_keep(i, local)
+        for step in (groups - 1 - i,) if near else range(groups):
+            if step == 0:
+                for src, dst, (t, nb) in out_copies(i, None):
+                    copy = pltpu.make_async_copy(src, dst, g_here.at[t, nb])
+                    getattr(copy, "wait" if act == SENT else act)()
+            else:
+                to = out_group(i) if near else (g + step) % groups
+                for src, dst, (t, nb) in out_copies(i, step):
+                    copy = remote(src, dst, gp_s.at[t, step, nb], gp_r.at[t, step, nb], me.at(c, to, k))
+                    getattr(copy, act)()
+
+    for i in range(LINE):
+        if i >= 2 and not near:
+            out_sends(i - 2, SENT)
+        out_products(i)
+        out_sends(i, START)
 
     def pair_s(i, act):
         line = (c + i) % LINE
@@ -569,24 +571,11 @@
         whole = pl.ds(base, block_rows)
         slot = i % 2
 
-        @pl.when(i == 0)
-        def _():
-            pair_m(LINE - 2, SENT)
-
-        @pl.when(i == 1)
-        def _():
-            pair_m(LINE - 1, SENT)
-
-        @pl.when(i >= 2)
-        def _():
-            out_sends(i - 2, SENT)
-
-        out_products(i)
-        out_sends(i, START)
-
-        @pl.when(i == 0)
-        def _():
-            pair_add(LINE - 1)
+        if near:
+
+            @pl.when(i == 1)
+            def _():
+                out_sends(LINE - 1, SENT)
 
         @pl.when((i == 1) | (i == 2))
         def _():
@@ -678,13 +667,13 @@
     for i in (LINE - 2, LINE - 1):
         pair_s(i, SENT)
         put_s(i, "wait")
+    for i in range(LINE - 1) if near else (LINE - 2, LINE - 1):
         out_sends(i, SENT)
-    for step in range(1, groups):
-        for nb in range(pieces):
-            for i in range(1 if near else LINE):
-                dst = out_place((gd_got, g2_got), i, nb, step)
-                sem = (i, step, nb)
-                remote(dst, dst, gp_s.at[sem], gp_r.at[sem], sibling).wait_recv()
+    for i in range(LINE):
+        for step in (groups - 1 - i,) if near else range(1, groups):
+            if step:
+                for _, dst, (t, nb) in out_copies(i, step):
+                    remote(dst, dst, gp_s.at[t, step, nb], gp_r.at[t, step, nb], sibling).wait_recv()
     for m in range(count):
         stage_one(m, SENT)
         for step in range(LINE):

time: 449 us -> 438 us (0.976)
  Pallas kernels: 446 us -> 435 us
    pallas_call x1, Pallas kernels: 270 us -> 259 us  [gather_all(): pl.pallas_call(partial(gather_kernel, groups, cols, seq_dev, slot_len), o...]
where the time goes in v6:
time: 438 us
  Pallas kernels  435 us (99%)
    pallas_call x1, Pallas kernels, gather_all(): pl.pallas_call(partial(gather_kernel, groups, cols, seq_dev, slot_len), o...  259 us
    pallas_call x1, Pallas kernels, scatter_all(): pl.pallas_call(partial(scatter_kernel, groups, cols, seq_dev, slot_len, r...  154 us
    pallas_call x1, Pallas kernels, finish(): pl.pallas_call(partial(finish_kernel, order, cols, rows_own), grid=(steps...  16.5 us

profile of v6, /device:TPU:0, one launch (start us, length us, event | category | flops | bytes accessed | tf_op | source)
XLA Modules:
  0.0 437.8 jit_solution(10004904916535862281)
XLA Ops:
  0.7 0.7 pad_add_fusion.refs_0_
  1.3 5.6 %prepare.1 = (bf16[128,3072]{1,0:T(8,128)(2,1)}, bf16[128,4096]{1,0:T(8,128)(2,1)}, bf16[128,1024]{1,0:T(8,128)(2,1)}, bf16[128,4096]{1,0:T(8,128)(2,1)}, f32[15...) custom-call(s32[2]{0:T(128)} %pad_add_fusion.refs_0_, s32[32]{0:T(128)} %refs_1_.1, ...), custom_call_target="tpu_custom_call" | custom-call | tf_op jit(solution)/shard_map/prepare/pallas_call | solution.py:1224
  6.9 259.2 %gather_all.1 = (bf16[1536,2048]{1,0:T(8,128)(2,1)}, bf16[1536,2048]{1,0:T(8,128)(2,1)}, bf16[1536,768]{1,0:T(8,128)(2,1)}, bf16[1536,1024]{1,0:T(8,128)(2,1)}, ...) custom-call(bf16[128,3072]{1,0:T(8,128)(2,1)} %get-tuple-element.74., ...), custom_call_target="tpu_custom_call" | custom-call | tf_op jit(solution)/shard_map/gather_all/pallas_call | solution.py:703
  266.1 153.9 %scatter_all.1 = (bf16[2,192,2048]{2,1,0:T(8,128)(2,1)}, bf16[2,192,2048]{2,1,0:T(8,128)(2,1)}, bf16[128,3072]{1,0:T(8,128)(2,1)}, bf16[128,4096]{1,0:T(8,128)(2...) custom-call(s32[8]{0:T(128)} %get-tuple-element.73.refs_0_, ...), custom_call_target="tpu_custom_call" | custom-call | tf_op jit(solution)/shard_map/scatter_all/pallas_call | solution.py:1105
  420.0 0.0 copy-start
  420.0 16.5 %finish.1 = (f32[128,3072]{1,0:T(8,128)}, f32[128,1024]{1,0:T(8,128)}, f32[128,4096]{1,0:T(8,128)}, f32[128,4096]{1,0:T(8,128)}, f32[128,3072]{1,0:T(8,128)}, /*...) custom-call(s32[2]{0:T(128)} %pad_add_fusion.refs_0_, ...), custom_call_target="tpu_custom_call" | custom-call | tf_op jit(solution)/shard_map/finish/pallas_call | solution.py:1363
  436.6 0.0 copy-done
  436.6 1.1 copy.38
Async XLA Ops:
  420.0 16.6 %copy-start = (bf16[2,192,2048]{2,1,0:T(8,128)(2,1)S(1)}, bf16[2,192,2048]{2,1,0:T(8,128)(2,1)}, u32[]{:S(2)}) copy-start(bf16[2,192,2048]{2,1,0:T(8,128)(2,1)} %get-tuple-element.146) | copy-start | bytes 4718596

commit v7 on v6

--- a/solution.py
+++ b/solution.py
@@ -435,19 +435,23 @@
         def _():
             pair_m(i - 2, SENT)
 
-        live = valid_ref[whole, :]
-
         @pl.loop(0, ways)
         def output(j):
             at = pl.ds(pl.multiple_of(j * wide, 128), wide)
             total = contract(attn_keep[whole, :], wd[at, :], ((1,), (1,)))
-            total = total + contract(hid_keep[whole, :], w2[at, :], ((1,), (1,)))
+            pre_now[:, :wide] = total + contract(hid_keep[whole, :], w2[at, :], ((1,), (1,)))
             feature = (lax.broadcasted_iota(jnp.int32, (1, wide), 1) + j * wide) // (D // (2 * LINE))
             mask = jnp.where(feature == mine, 1.0, 0.0)
-            extra = x_all[whole, at].astype(f32) + (vec_ref[4:5, at] + vec_ref[5:6, at])
-            total = ((total + mask * extra) * live).astype(low)
-            m_buf[slot, 0, j] = total[:, : wide // 2]
-            m_buf[slot, 1, j] = total[:, wide // 2 :]
+            bias = vec_ref[4:5, at] + vec_ref[5:6, at]
+
+            @pl.loop(0, block_rows // chunk)
+            def rows(r):
+                to = pl.ds(pl.multiple_of(r * chunk, chunk), chunk)
+                here_rows = pl.ds(pl.multiple_of(base + r * chunk, chunk), chunk)
+                extra = x_all[here_rows, at].astype(f32) + bias
+                total = ((pre_now[to, :wide] + mask * extra) * valid_ref[here_rows, :]).astype(low)
+                m_buf[slot, 0, j, to, :] = total[:, : wide // 2]
+                m_buf[slot, 1, j, to, :] = total[:, wide // 2 :]
 
         pair_m(i, START)
 
@@ -582,8 +586,12 @@
             second_m(i * 2 - 2)
             second_m(i * 2 - 1)
 
-        live = valid_ref[whole, :]
-        back_buf[...] = (ct_all[whole, :].astype(f32) * live).astype(low)
+        @pl.loop(0, block_rows // chunk)
+        def mask_back(r):
+            to = pl.ds(pl.multiple_of(r * chunk, chunk), chunk)
+            here_rows = pl.ds(pl.multiple_of(base + r * chunk, chunk), chunk)
+            back_buf[to, :] = (ct_all[here_rows, :].astype(f32) * valid_ref[here_rows, :]).astype(low)
+
         attn_grad = dot(back_buf[...], wd[...]).astype(low)
         pre_now[...] = dot(back_buf[...], w2[...])
 
@@ -624,8 +632,6 @@
             bias_acc[:, : cols[0]] += jnp.sum(summed, 0)
 
         put_rest(line, "start")
-        mean = stat_keep[whole, 0:1]
-        scale = stat_keep[whole, 1:2]
 
         @pl.when(i >= 2)
         def _():
@@ -635,12 +641,23 @@
         @pl.loop(0, ways)
         def inputs(j):
             at = pl.ds(pl.multiple_of(j * wide, 128), wide)
-            first = contract(qkv_keep[whole, :], wq[at, :], ((1,), (1,)))
-            second = contract(pg_keep[whole, :], w1[at, :], ((1,), (1,)))
-            two_buf[slot, :, at] = (first * vec_ref[0:1, at] + second * vec_ref[2:3, at]).astype(low)
-            unit = (x_all[whole, at].astype(f32) - mean) * scale
-            for place_at, value in enumerate((first * unit, first, second * unit, second)):
-                norm_acc[place_at, :, at] += jnp.sum(value.reshape(block_rows // 8, 8, wide), 0)
+            pre_now[:, :wide] = contract(qkv_keep[whole, :], wq[at, :], ((1,), (1,)))
+            pre_now[:, wide:] = contract(pg_keep[whole, :], w1[at, :], ((1,), (1,)))
+            gain_one, gain_two = vec_ref[0:1, at], vec_ref[2:3, at]
+
+            def body(r, sums):
+                to = pl.ds(pl.multiple_of(r * chunk, chunk), chunk)
+                here_rows = pl.ds(pl.multiple_of(base + r * chunk, chunk), chunk)
+                first, second = pre_now[to, :wide], pre_now[to, wide:]
+                two_buf[slot, to, at] = (first * gain_one + second * gain_two).astype(low)
+                unit = (x_all[here_rows, at].astype(f32) - stat_keep[here_rows, 0:1]) * stat_keep[here_rows, 1:2]
+                values = (first * unit, first, second * unit, second)
+                return tuple(total + value[:8] + value[8:] for total, value in zip(sums, values))
+
+            zero = jnp.zeros((8, wide), f32)
+            sums = lax.fori_loop(0, block_rows // chunk, body, (zero,) * 4)
+            for place_at in range(4):
+                norm_acc[place_at, :, at] += sums[place_at]
 
         pair_s(i, START)
 
@@ -982,26 +999,6 @@
         copy.wait()
     sum_groups(3, firsts[3])
     sum_groups(2, firsts[2])
-    got_two.wait()
-    got_1.wait()
-    products(left_buf.at[0], ((1, right_a),))
-    if not double:
-        got_one = load(lefts_in[0], left_buf.at[0], here.at[0])
-        got_q = load(rights_in[0], right_b, here.at[1])
-
-    for q in range(2):
-        got_s[q].wait()
-        arrived(s_half.at[q], half_s.at[q], half_r.at[q])
-        add_rows(
-            lambda at: s_own.at[q, at], [lambda at: s_own.at[q, at], lambda at: s_half.at[q, at]], slot_len, 16
-        )
-    go(remote(s_own.at[1], s_far, far_s, far_r, me.at(beyond, g, k)))
-
-    got_one.wait()
-    got_q.wait()
-    products(left_buf.at[1 if double else 0], ((0, right_b),))
-    if two_phase:
-        between_phases(1)
     for step in range(1, groups):
         arrived(early_group.at[from_group(step)], eg_s.at[step], eg_r.at[step])
     acc = early_group[0]
@@ -1011,6 +1008,29 @@
     for step in range(1, LINE):
         go(remote(early_out.at[k, c], early_out.at[k, c], el_s.at[step], el_r.at[step], me.at(me.line_to(step), g, k)))
 
+    got_two.wait()
+    got_1.wait()
+    products(left_buf.at[0], ((1, right_a),))
+    if not double:
+        got_one = load(lefts_in[0], left_buf.at[0], here.at[0])
+        got_q = load(rights_in[0], right_b, here.at[1])
+
+    for q in range(2):
+        got_s[q].wait()
+        arrived(s_half.at[q], half_s.at[q], half_r.at[q])
+        add_rows(
+            lambda at: s_own.at[q, at], [lambda at: s_own.at[q, at], lambda at: s_half.at[q, at]], slot_len, 16
+        )
+    go(remote(s_own.at[1], s_far, far_s, far_r, me.at(beyond, g, k)))
+
+    got_one.wait()
+    got_q.wait()
+    products(left_buf.at[1 if double else 0], ((0, right_b),))
+    if two_phase:
+        between_phases(1)
+    if two_phase:
+        between_phases(0)
+    sum_groups(1, firsts[1])
     for step in range(1, groups):
         arrived(m_all.at[pl.ds(from_group(step) * seqs, seqs)], mall_s.at[step], mall_r.at[step])
     mixed_cols = pl.ds(pl.multiple_of((c * 2 + k) * feat, 128), feat)
@@ -1024,9 +1044,7 @@
         else:
             keep.append(load(m_send.at[line], where, keep_sem.at[1]))
             go(remote(m_send.at[line], where, mout_s.at[1, 0], mout_r.at[1, 0], sibling))
-    if two_phase:
-        between_phases(0)
-    sum_groups(1, firsts[1])
+
     sum_groups(0, firsts[0])
 
     for step in range(1, groups):

time: 438 us -> 493 us (1.13)
  Pallas kernels: 435 us -> 490 us
    pallas_call x1, Pallas kernels: 259 us -> 311 us  [gather_all(): pl.pallas_call(partial(gather_kernel, groups, cols, seq_dev, slot_len), o...]
where the time goes in v7:
time: 493 us; the launch traced here: 492 us
  Pallas kernels  490 us (99%)
    pallas_call x1, Pallas kernels, gather_all(): pl.pallas_call(partial(gather_kernel, groups, cols, seq_dev, slot_len), o...  311 us
    pallas_call x1, Pallas kernels, scatter_all(): pl.pallas_call(partial(scatter_kernel, groups, cols, seq_dev, slot_len, r...  156 us
    pallas_call x1, Pallas kernels, finish(): pl.pallas_call(partial(finish_kernel, order, cols, rows_own), grid=(steps...  16.5 us

profile of v7, /device:TPU:0, one launch (start us, length us, event | category | flops | bytes accessed | tf_op | source)
XLA Modules:
  0.0 492.3 jit_solution(4822725070797028749)
XLA Ops:
  0.7 0.7 pad_add_fusion.refs_0_
  1.3 5.6 %prepare.1 = (bf16[128,3072]{1,0:T(8,128)(2,1)}, bf16[128,4096]{1,0:T(8,128)(2,1)}, bf16[128,1024]{1,0:T(8,128)(2,1)}, bf16[128,4096]{1,0:T(8,128)(2,1)}, f32[15...) custom-call(s32[2]{0:T(128)} %pad_add_fusion.refs_0_, s32[32]{0:T(128)} %refs_1_.1, ...), custom_call_target="tpu_custom_call" | custom-call | tf_op jit(solution)/shard_map/prepare/pallas_call | solution.py:1242
  6.9 311.3 %gather_all.1 = (bf16[1536,2048]{1,0:T(8,128)(2,1)}, bf16[1536,2048]{1,0:T(8,128)(2,1)}, bf16[1536,768]{1,0:T(8,128)(2,1)}, bf16[1536,1024]{1,0:T(8,128)(2,1)}, ...) custom-call(bf16[128,3072]{1,0:T(8,128)(2,1)} %get-tuple-element.74., ...), custom_call_target="tpu_custom_call" | custom-call | tf_op jit(solution)/shard_map/gather_all/pallas_call | solution.py:720
  318.3 156.4 %scatter_all.1 = (bf16[2,192,2048]{2,1,0:T(8,128)(2,1)}, bf16[2,192,2048]{2,1,0:T(8,128)(2,1)}, bf16[128,3072]{1,0:T(8,128)(2,1)}, bf16[128,4096]{1,0:T(8,128)(2...) custom-call(s32[8]{0:T(128)} %get-tuple-element.73.refs_0_, ...), custom_call_target="tpu_custom_call" | custom-call | tf_op jit(solution)/shard_map/scatter_all/pallas_call | solution.py:1123
  474.6 0.0 copy-start
  474.6 16.5 %finish.1 = (f32[128,3072]{1,0:T(8,128)}, f32[128,1024]{1,0:T(8,128)}, f32[128,4096]{1,0:T(8,128)}, f32[128,4096]{1,0:T(8,128)}, f32[128,3072]{1,0:T(8,128)}, /*...) custom-call(s32[2]{0:T(128)} %pad_add_fusion.refs_0_, ...), custom_call_target="tpu_custom_call" | custom-call | tf_op jit(solution)/shard_map/finish/pallas_call | solution.py:1381
  491.2 0.0 copy-done
  491.2 1.1 copy.38
Async XLA Ops:
  474.6 16.6 %copy-start = (bf16[2,192,2048]{2,1,0:T(8,128)(2,1)S(1)}, bf16[2,192,2048]{2,1,0:T(8,128)(2,1)}, u32[]{:S(2)}) copy-start(bf16[2,192,2048]{2,1,0:T(8,128)(2,1)} %get-tuple-element.146) | copy-start | bytes 4718596

commit v8 on v6

--- a/solution.py
+++ b/solution.py
@@ -276,7 +276,7 @@
     x_all, ct_all = acts_out
     head = cols[0] // 3
     half = head // 2
-    chunk = 16
+    chunk = 64
     wide = 512
     ways = D // wide
     root = math.sqrt(head)
@@ -398,9 +398,9 @@
     def second_m(i):
         half_m(i, "wait_recv")
 
-        @pl.loop(0, block_rows // 64)
+        @pl.loop(0, block_rows // 192)
         def add(j):
-            at = pl.ds(pl.multiple_of(j * 64, 64), 64)
+            at = pl.ds(pl.multiple_of(j * 192, 64), 192)
             for q, to in enumerate((c, beyond)):
                 total = m_got[i, to, at, :].astype(f32) + m_half[i, q, at, :].astype(f32)
                 m_got[i, to, at, :] = total.astype(low)
@@ -413,9 +413,9 @@
 
         @pl.loop(0, LINE)
         def add_outer(p):
-            @pl.loop(0, block_rows // 64)
+            @pl.loop(0, block_rows // 192)
             def add(j):
-                at = pl.ds(pl.multiple_of(j * 64, 64), 64)
+                at = pl.ds(pl.multiple_of(j * 192, 64), 192)
                 total = m_buf[i % 2, k, p, at, :].astype(f32) + m_got[i, p, at, :].astype(f32)
                 m_got[i, p, at, :] = total.astype(low)
 
@@ -600,7 +600,7 @@
             grad = grad.astype(low)
             pg_keep[at, :] = grad
             grad = grad.astype(f32)
-            bias_acc[:, cols[0] :] += grad[:8] + grad[8:]
+            bias_acc[:, cols[0] :] += jnp.sum(grad.reshape(chunk // 8, 8, cols[1]), 0)
 
         for s in range(seq_dev):
             rows = pl.ds(pl.multiple_of(base + s * slot_len, 32), slot_len)
@@ -894,7 +894,7 @@
                     lambda at: g_own[m].at[line, to, at],
                     [lambda at: g_own[m].at[line, to, at], lambda at: g_got[m].at[1, line, at]],
                     rows_own,
-                    16,
+                    min(64, rows_own),
                 )
             phase_two(m, way, "start")
 
@@ -939,16 +939,16 @@
             line = me.line_to(step)
 
             def body(i, carry, line=line):
-                at = pl.ds(pl.multiple_of(i * 16, 16), 16)
+                at = pl.ds(pl.multiple_of(i * 32, 32), 32)
                 acc = g_own[m][line, mine, at, :].astype(f32)
                 for p in got:
                     acc = acc + g_got[m][p, line, at, :].astype(f32)
                 g_own[m][line, mine, at, :] = acc.astype(low)
                 square = acc * acc + eps_second
                 row_keep[line, at, m : m + 1] = jnp.sum(square, 1, keepdims=True)
-                return carry + square[:8] + square[8:]
-
-            total = lax.fori_loop(0, rows_own // 16, body, total)
+                return carry + jnp.sum(square.reshape(4, 8, cols[m]), 0)
+
+            total = lax.fori_loop(0, rows_own // 32, body, total)
             src = g_own[m].at[line, mine]
             if step:
                 go(remote(src, g_out[m].at[:, width], gl_s.at[m, step], gl_r.at[m, step], me.at(line, g, k)))
@@ -973,7 +973,7 @@
             lambda at: m_all.at[g * seqs + s, at],
             [lambda at: m_in.at[0, s, at], lambda at: m_in.at[1, s, at]],
             slot_len,
-            64,
+            192,
         )
     for step in range(1, groups):
         go(remote(m_all.at[ours], m_all.at[ours], mall_s.at[step], mall_r.at[step], me.at(c, to_group(step), k)))
@@ -993,7 +993,7 @@
         got_s[q].wait()
         arrived(s_half.at[q], half_s.at[q], half_r.at[q])
         add_rows(
-            lambda at: s_own.at[q, at], [lambda at: s_own.at[q, at], lambda at: s_half.at[q, at]], slot_len, 16
+            lambda at: s_own.at[q, at], [lambda at: s_own.at[q, at], lambda at: s_half.at[q, at]], slot_len, 64
         )
     go(remote(s_own.at[1], s_far, far_s, far_r, me.at(beyond, g, k)))
 

time: 438 us -> 424 us (0.968)
  Pallas kernels: 435 us -> 421 us
    pallas_call x1, Pallas kernels: 259 us -> 245 us  [gather_all(): pl.pallas_call(partial(gather_kernel, groups, cols, seq_dev, slot_len), o...]
where the time goes in v8:
time: 424 us
  Pallas kernels  421 us (99%)
    pallas_call x1, Pallas kernels, gather_all(): pl.pallas_call(partial(gather_kernel, groups, cols, seq_dev, slot_len), o...  245 us
    pallas_call x1, Pallas kernels, scatter_all(): pl.pallas_call(partial(scatter_kernel, groups, cols, seq_dev, slot_len, r...  154 us
    pallas_call x1, Pallas kernels, finish(): pl.pallas_call(partial(finish_kernel, order, cols, rows_own), grid=(steps...  16.5 us

profile of v8, /device:TPU:0, one launch (start us, length us, event | category | flops | bytes accessed | tf_op | source)
XLA Modules:
  0.0 424.0 jit_solution(13665825082254808029)
XLA Ops:
  0.7 0.7 pad_add_fusion.refs_0_
  1.3 5.6 %prepare.1 = (bf16[128,3072]{1,0:T(8,128)(2,1)}, bf16[128,4096]{1,0:T(8,128)(2,1)}, bf16[128,1024]{1,0:T(8,128)(2,1)}, bf16[128,4096]{1,0:T(8,128)(2,1)}, f32[15...) custom-call(s32[2]{0:T(128)} %pad_add_fusion.refs_0_, s32[32]{0:T(128)} %refs_1_.1, ...), custom_call_target="tpu_custom_call" | custom-call | tf_op jit(solution)/shard_map/prepare/pallas_call | solution.py:1224
  6.9 245.4 %gather_all.1 = (bf16[1536,2048]{1,0:T(8,128)(2,1)}, bf16[1536,2048]{1,0:T(8,128)(2,1)}, bf16[1536,768]{1,0:T(8,128)(2,1)}, bf16[1536,1024]{1,0:T(8,128)(2,1)}, ...) custom-call(bf16[128,3072]{1,0:T(8,128)(2,1)} %get-tuple-element.74., ...), custom_call_target="tpu_custom_call" | custom-call | tf_op jit(solution)/shard_map/gather_all/pallas_call | solution.py:703
  252.3 153.9 %scatter_all.1 = (bf16[2,192,2048]{2,1,0:T(8,128)(2,1)}, bf16[2,192,2048]{2,1,0:T(8,128)(2,1)}, bf16[128,3072]{1,0:T(8,128)(2,1)}, bf16[128,4096]{1,0:T(8,128)(2...) custom-call(s32[8]{0:T(128)} %get-tuple-element.73.refs_0_, ...), custom_call_target="tpu_custom_call" | custom-call | tf_op jit(solution)/shard_map/scatter_all/pallas_call | solution.py:1105
  406.3 0.0 copy-start
  406.3 16.5 %finish.1 = (f32[128,3072]{1,0:T(8,128)}, f32[128,1024]{1,0:T(8,128)}, f32[128,4096]{1,0:T(8,128)}, f32[128,4096]{1,0:T(8,128)}, f32[128,3072]{1,0:T(8,128)}, /*...) custom-call(s32[2]{0:T(128)} %pad_add_fusion.refs_0_, ...), custom_call_target="tpu_custom_call" | custom-call | tf_op jit(solution)/shard_map/finish/pallas_call | solution.py:1363
  422.9 0.0 copy-done
  422.9 1.1 copy.38
Async XLA Ops:
  406.3 16.6 %copy-start = (bf16[2,192,2048]{2,1,0:T(8,128)(2,1)S(1)}, bf16[2,192,2048]{2,1,0:T(8,128)(2,1)}, u32[]{:S(2)}) copy-start(bf16[2,192,2048]{2,1,0:T(8,128)(2,1)} %get-tuple-element.146) | copy-start | bytes 4718596
